TPU v7x, 32 devices: a whole 2x2x4 slice. The times are simulated.
32 devices in a mesh: dp: 16 (over z, y, core), seq: 2 (over x).
Axes of the slice: x: 2, y: 2, z: 4, core: 2. Of those that a mesh axis runs over, the one named last changes fastest.
Arguments:
- tokens: bfloat16 [32, 1024, 2048], P('dp', 'seq'), may hold values from -6 to 6
- doc_start: int32 [32, 1024], P('dp', 'seq'), may hold values from 0 to 1, as said below
- in_weight: bfloat16 [2048, 8512], P(('dp', 'seq')), may hold values from -0.125 to 0.125
- norm_gain: bfloat16 [2048], P(('dp', 'seq')), may hold values from 0.5 to 1.5
- out_weight: bfloat16 [4096, 2048], P(('dp', 'seq')), may hold values from -0.09375 to 0.09375
- gate_gain: bfloat16 [4096], P(('dp', 'seq')), may hold values from 0.5 to 1.5
- conv_weight: bfloat16 [4, 4352], P(None, ('dp', 'seq')), may hold values from -3 to 3
- conv_bias: bfloat16 [4352], P(('dp', 'seq')), may hold values from -2 to 2
- dt_bias: float32 [64], replicated, may hold values from -12 to -1, as said below
- a_log: float32 [64], replicated, may hold values from 0 to 1.3863, as said below
- skip_gain: float32 [64], replicated, may hold values from 0.25 to 1
- out_grad: bfloat16 [32, 1024, 2048], P('dp', 'seq'), may hold values from -6 to 6
Outputs:
- output: bfloat16 [32, 1024, 2048], P('dp', 'seq')
- input_grad: bfloat16 [32, 1024, 2048], P('dp', 'seq')
- in_weight_grad: float32 [2048, 8512], P(('dp', 'seq'))
- norm_gain_grad: float32 [2048], P(('dp', 'seq'))
- out_weight_grad: float32 [4096, 2048], P(('dp', 'seq'))
- gate_gain_grad: float32 [4096], P(('dp', 'seq'))
- conv_weight_grad: float32 [4, 4352], P(None, ('dp', 'seq'))
- conv_bias_grad: float32 [4352], P(('dp', 'seq'))
- dt_bias_grad: float32 [64], replicated
- a_log_grad: float32 [64], replicated
- skip_gain_grad: float32 [64], replicated
Inputs may be any that keep to these rules, and one draw needn't show every extreme that they name: `doc_start`: 1 marks the first position of a document; position 0 of every sequence is marked. `a_log`: per head. `dt_bias`: per head.
All inputs are finite; a program needn't handle non-finite values.
Results may differ from a plain program's by a relative error of at most 0.0069.
Values may be sent and summed in bfloat16 or wider, within the bound.
A program may use at most 576 MiB of HBM per device.

v0:
```python
from functools import partial
from functools import reduce

import jax
import jax.numpy as jnp
from jax import lax
from jax.sharding import PartitionSpec as P

H = 64
HD = 64
N = 128
CONV = 4
STRETCH = 256
DI = 4096
XBC = 4352
PROJ = 8512


EPS = 1e-05
HIGHEST = lax.Precision.HIGHEST
CONTRACT_LAST = (((1,), (1,)), ((), ()))
CONTRACT_FIRST = (((0,), (0,)), ((), ()))


def passed_along(block, axis, distance):
    devices = range(lax.axis_size(axis))
    route = [(i - distance, i) for i in devices if i - distance in devices]
    return lax.ppermute(block, axis, route)


def entering(shard, axis, join, neutral):
    place = lax.axis_index(axis)
    gathered = jax.tree.map(
        lambda a, kind: lax.all_gather(a.astype(kind), axis), shard, (jnp.bfloat16, jnp.bfloat16)
    )
    state = jax.tree.map(lambda a, e: jnp.zeros_like(a) + jnp.asarray(e, a.dtype), shard, neutral)

    def entering_one(step, state):
        return join(
            state,
            jax.tree.map(
                lambda a, own: lax.dynamic_index_in_dim(a, step, 0, False).astype(own.dtype),
                gathered,
                shard,
            ),
        )

    return lax.fori_loop(0, place, entering_one, state)


def prefix(shard, axis, join, neutral):
    count = lax.axis_size(axis)
    place = lax.axis_index(axis)
    ahead = count - 1 - place
    gathered = jax.tree.map(
        lambda a, kind: lax.all_gather(a.astype(kind), axis),
        shard,
        jax.tree.map(lambda a: jnp.bfloat16 if a.dtype == jnp.float32 else a.dtype, shard),
    )
    state = jax.tree.map(lambda a, e: jnp.zeros_like(a) + jnp.asarray(e, a.dtype), shard, neutral)

    def prefix_one(step, state):
        source = count - 1 - step
        return join(
            state,
            jax.tree.map(
                lambda a, own: lax.dynamic_index_in_dim(a, source, 0, False).astype(own.dtype),
                gathered,
                shard,
            ),
        )

    return lax.fori_loop(0, ahead, prefix_one, state)


def keep_round(values):
    rounded = lax.optimization_barrier(values.astype(jnp.bfloat16)).astype(jnp.float32)
    return values + lax.stop_gradient(rounded - values)


def stretch_step(carry_state, inputs):
    inner_x, b_proj, c_proj, decay, step_size, starts = inputs
    counts = jnp.cumsum(starts)
    decay_sum = jnp.cumsum(decay, axis=0)
    positions = jnp.arange(starts.shape[0])
    same_doc = (counts[:, None] == counts[None, :]) & (positions[None, :] <= positions[:, None])
    valid_pair = same_doc[:, :, None]
    decay_gap = decay_sum[:, None, :] - decay_sum[None, :, :]
    weights = jnp.where(valid_pair, jnp.exp(jnp.where(valid_pair, decay_gap, 0.0)), 0.0)
    affinity = jnp.dot(c_proj, b_proj.T, precision=HIGHEST)
    scaled = inner_x * step_size[:, :, None]
    mixing = affinity[:, :, None] * weights
    within = jnp.einsum("tsh,shp->thp", mixing, scaled, precision=HIGHEST)
    inflow = jnp.where((counts == 0)[:, None], jnp.exp(decay_sum), 0.0)
    carried = jnp.einsum("tn,hpn->thp", c_proj, carry_state, precision=HIGHEST) * inflow[:, :, None]
    final_sum = decay_sum[-1]
    outflow = jnp.where(
        (counts == counts[-1])[:, None], jnp.exp(final_sum[None, :] - decay_sum), 0.0
    )
    deposit = jnp.einsum("shp,sn->hpn", scaled * outflow[:, :, None], b_proj, precision=HIGHEST)
    retain = jnp.where(counts[-1] == 0, jnp.exp(final_sum), 0.0)
    new_state = retain[:, None, None] * carry_state + deposit
    return (new_state, within + carried)


def scan_stretches(inner_x, b_proj, c_proj, decay, step_size, starts, carry_state):
    blocks = inner_x.shape[0] // STRETCH
    pieces = (
        inner_x.reshape(blocks, STRETCH, H, HD),
        b_proj.reshape(blocks, STRETCH, N),
        c_proj.reshape(blocks, STRETCH, N),
        decay.reshape(blocks, STRETCH, H),
        step_size.reshape(blocks, STRETCH, H),
        starts.reshape(blocks, STRETCH),
    )
    final_state, outputs = lax.scan(jax.checkpoint(stretch_step), carry_state, pieces)
    return (final_state, outputs.reshape(-1, H, HD))


def conv_mix(front_rows, raw_rows, starts, conv_weight, conv_bias):
    length = raw_rows.shape[0]
    counts = jnp.cumsum(starts)
    extended = jnp.concatenate([front_rows, raw_rows], axis=0)
    count_ext = jnp.concatenate([jnp.zeros((CONV - 1,), jnp.int32), counts])
    summed = jnp.broadcast_to(conv_bias[None, :], raw_rows.shape)
    for offset in range(CONV):
        usable = count_ext[offset : offset + length] == counts
        summed = summed + jnp.where(
            usable[:, None], extended[offset : offset + length] * conv_weight[offset][None, :], 0.0
        )
    return summed


def section_in(starts, projected, front_rows, conv_weight, conv_bias, dt_bias, a_log):
    gate_part = projected[:, :DI]
    conv_in = projected[:, DI : DI + XBC]
    dt_raw = projected[:, DI + XBC :]
    conv_out = conv_mix(front_rows, conv_in, starts, conv_weight, conv_bias)
    activated = keep_round(jax.nn.silu(conv_out))
    inner_x = activated[:, :DI].reshape(-1, H, HD)
    b_proj = activated[:, DI : DI + N]
    c_proj = activated[:, DI + N :]
    step_size = jax.nn.softplus(dt_raw + dt_bias)
    decay = -step_size * jnp.exp(a_log)
    local_state, local_out = scan_stretches(
        inner_x, b_proj, c_proj, decay, step_size, starts, jnp.zeros((H, HD, N), jnp.float32)
    )
    decay_sum = jnp.cumsum(decay, axis=0)
    counts = jnp.cumsum(starts)
    inflow = jnp.where((counts == 0)[:, None], jnp.exp(decay_sum), 0.0)
    carry_decay = jnp.where(counts[-1] == 0, jnp.exp(decay_sum[-1]), 0.0)
    return (gate_part, inner_x, c_proj, local_out, local_state, carry_decay, inflow)


def section_out(gate_part, inner_x, c_proj, local_out, inflow, incoming, skip_gain, gate_gain):
    carried = jnp.einsum("tn,hpn->thp", c_proj, incoming, precision=HIGHEST) * inflow[:, :, None]
    ssm_out = local_out + carried + skip_gain[None, :, None] * inner_x
    gated = ssm_out.reshape(-1, DI) * jax.nn.silu(gate_part)
    return gated * lax.rsqrt(jnp.mean(gated * gated, axis=-1, keepdims=True) + EPS) * gate_gain


def link(earlier, later):
    return (earlier[0] * later[0], later[0][..., None, None] * earlier[1] + later[1])


def weight_term(left, right, extra):
    product = lax.dot_general(left, right, CONTRACT_FIRST, preferred_element_type=jnp.float32)
    return jnp.concatenate([product, extra[:, None]], axis=1)


def add_all(pieces):
    return reduce(jnp.add, pieces)


def shards(
    tokens,
    doc_start,
    in_weight,
    norm_gain,
    out_weight,
    gate_gain,
    conv_weight,
    conv_bias,
    dt_bias,
    a_log,
    skip_gain,
    out_grad,
):
    local_seqs, length, width = tokens.shape
    total_rows = local_seqs * length
    values = tokens.reshape(total_rows, width).astype(jnp.float32)
    scale = lax.rsqrt(jnp.mean(values * values, axis=-1, keepdims=True) + EPS)
    normed = values * scale
    in_full, gain_full, out_full, gate_full, conv_full, bias_full = (
        lax.all_gather(in_weight, ("dp", "seq"), axis=0, tiled=True),
        lax.all_gather(norm_gain, ("dp", "seq"), axis=0, tiled=True),
        lax.all_gather(out_weight, ("dp", "seq"), axis=0, tiled=True),
        lax.all_gather(gate_gain, ("dp", "seq"), axis=0, tiled=True),
        lax.all_gather(conv_weight, ("dp", "seq"), axis=1, tiled=True),
        lax.all_gather(conv_bias, ("dp", "seq"), axis=0, tiled=True),
    )
    norm_full = gain_full.astype(jnp.float32)
    hidden_low = (normed * norm_full[None, :]).astype(jnp.bfloat16)
    projected = jnp.dot(hidden_low, in_full, preferred_element_type=jnp.float32)
    gate_gains = gate_full.astype(jnp.float32)
    conv_taps = conv_full.astype(jnp.float32)
    conv_shift = bias_full.astype(jnp.float32)
    projected_seqs = projected.reshape(local_seqs, length, PROJ)
    counts = jnp.cumsum(doc_start, axis=1)
    tail_mask = (counts[:, length - CONV + 1 :] == counts[:, length - 1 :])[:, :, None]
    tail_send = jnp.where(tail_mask, projected_seqs[:, length - CONV + 1 :, DI : DI + XBC], 0.0)
    front_rows = passed_along(tail_send.astype(jnp.bfloat16), "seq", 1).astype(tail_send.dtype)
    sections = [partial(section_in, doc_start[item]) for item in range(local_seqs)]
    kept = [
        sections[item](
            projected_seqs[item], front_rows[item], conv_taps, conv_shift, dt_bias, a_log
        )
        for item in range(local_seqs)
    ]
    local_state = jnp.stack([piece[4] for piece in kept])
    carry_decay = jnp.stack([piece[5] for piece in kept])
    identity = (
        jnp.ones((local_seqs, H), jnp.float32),
        jnp.zeros((local_seqs, H, HD, N), jnp.float32),
    )
    unused, incoming = entering((carry_decay, local_state), "seq", link, identity)
    outer_args = [
        (piece[0], piece[1], piece[2], piece[3], piece[6], incoming[item], skip_gain, gate_gains)
        for item, piece in enumerate(kept)
    ]
    mixed = jnp.concatenate([section_out(*arguments) for arguments in outer_args], axis=0)
    mixed_low = mixed.astype(jnp.bfloat16)
    output = (values + jnp.dot(mixed_low, out_full, preferred_element_type=jnp.float32)).astype(
        jnp.bfloat16
    )
    cotangent = out_grad.reshape(total_rows, width)
    mixed_grad = lax.dot_general(
        cotangent, out_full, CONTRACT_LAST, preferred_element_type=jnp.float32
    )
    grad_seqs = mixed_grad.reshape(local_seqs, length, DI)
    pulled = []
    for item in range(local_seqs):
        primal_out, pull_out = jax.vjp(section_out, *outer_args[item])
        pulled.append(pull_out(grad_seqs[item]))
    incoming_grad = jnp.stack([grads[5] for grads in pulled])
    skip_grad = add_all([grads[6] for grads in pulled])
    gate_gain_grad = add_all([grads[7] for grads in pulled])
    out_block = lax.psum_scatter(
        weight_term(mixed_low, cotangent, gate_gain_grad),
        ("dp", "seq"),
        scatter_dimension=0,
        tiled=True,
    )
    out_weight_grad = out_block[:, :width]
    gate_share = out_block[:, width]
    unused_back, outgoing = prefix((carry_decay, incoming_grad), "seq", link, identity)
    decay_grad = jnp.sum(outgoing * incoming, axis=(2, 3))
    backward = []
    for item in range(local_seqs):
        primal_in, pull_in = jax.vjp(
            sections[item],
            projected_seqs[item],
            front_rows[item],
            conv_taps,
            conv_shift,
            dt_bias,
            a_log,
        )
        grads = pulled[item]
        backward.append(
            pull_in(
                (grads[0], grads[1], grads[2], grads[3], outgoing[item], decay_grad[item], grads[4])
            )
        )
    proj_grad = jnp.stack([grads[0] for grads in backward])
    front_grad = jnp.stack([grads[1] for grads in backward])
    conv_grad = add_all([grads[2] for grads in backward])
    shift_grad = add_all([grads[3] for grads in backward])
    dt_grad = add_all([grads[4] for grads in backward])
    alog_grad = add_all([grads[5] for grads in backward])
    tail_back = passed_along(front_grad.astype(jnp.bfloat16), "seq", -1).astype(front_grad.dtype)
    proj_grad = proj_grad.at[:, length - CONV + 1 :, DI : DI + XBC].add(
        jnp.where(tail_mask, tail_back, 0.0)
    )
    proj_low = proj_grad.reshape(total_rows, PROJ).astype(jnp.bfloat16)
    hidden_grad = lax.dot_general(
        proj_low, in_full, CONTRACT_LAST, preferred_element_type=jnp.float32
    )
    norm_grad = jnp.sum(hidden_grad * normed, axis=0)
    in_block = lax.psum_scatter(
        weight_term(hidden_low, proj_low, norm_grad), ("dp", "seq"), scatter_dimension=0, tiled=True
    )
    in_weight_grad = in_block[:, :PROJ]
    norm_share = in_block[:, PROJ]
    normed_grad = hidden_grad * norm_full[None, :]
    input_grad = scale * (
        normed_grad - normed * jnp.mean(normed_grad * normed, axis=-1, keepdims=True)
    ) + cotangent.astype(jnp.float32)
    conv_share, shift_share = (
        lax.psum_scatter(conv_grad, ("dp", "seq"), scatter_dimension=1, tiled=True),
        lax.psum_scatter(shift_grad, ("dp", "seq"), scatter_dimension=0, tiled=True),
    )
    dt_total, alog_total, skip_total = lax.psum((dt_grad, alog_grad, skip_grad), ("dp", "seq"))
    return (
        output.reshape(local_seqs, length, width),
        input_grad.astype(jnp.bfloat16).reshape(local_seqs, length, width),
        in_weight_grad,
        norm_share,
        out_weight_grad,
        gate_share,
        conv_share,
        shift_share,
        dt_total,
        alog_total,
        skip_total,
    )


def solution(mesh):
    return jax.shard_map(
        shards,
        mesh=mesh,
        in_specs=(
            P("dp", "seq", None),
            P("dp", "seq"),
            P(("dp", "seq"), None),
            P(("dp", "seq")),
            P(("dp", "seq"), None),
            P(("dp", "seq")),
            P(None, ("dp", "seq")),
            P(("dp", "seq")),
            P(),
            P(),
            P(),
            P("dp", "seq", None),
        ),
        out_specs=(
            P("dp", "seq", None),
            P("dp", "seq", None),
            P(("dp", "seq"), None),
            P(("dp", "seq")),
            P(("dp", "seq"), None),
            P(("dp", "seq")),
            P(None, ("dp", "seq")),
            P(("dp", "seq")),
            P(),
            P(),
            P(),
        ),
        check_vma=False,
    )
```

profile of v0, /device:TPU:0, one launch (start us, length us, event | category | flops | bytes accessed | tf_op | source)
XLA Modules:
  0.0 4414.6 jit_solution(5303378008953925291)
XLA Ops:
  10.5 43.0 all-reduce.39
  60.3 68.1 %all-gather = bf16[32,136,4]{1,2,0:T(4,128)(2,1)S(1)} all-gather(bf16[1,136,4]{1,2,0:T(4,128)(2,1)} %bitcast.1096), channel_id=1, replica_groups=mesh['dp'=16,'seq'=2] {'dp','seq'}, dimensions={0}, use_global_device_ids=true | all-gather | bytes 35904 | tf_op jit(solution)/shard_map/all_gather | solution.py:199
  134.3 64.4 %all-gather.1 = bf16[32,1,128]{2,1,0:T(2,128)(2,1)S(1)} all-gather(bf16[1,1,128]{2,1,0:T(2,128)(2,1)} %bitcast.1098), channel_id=1, replica_groups=mesh['dp'=16,'seq'=2] {'dp','seq'}, dimensions={0}, use_global_device_ids=true | all-gather | bytes 8448 | tf_op jit(solution)/shard_map/all_gather | solution.py:198
  208.1 24.6 fusion.362
  232.7 101.8 %all-gather.7.cloned.1.call-done = bf16[2048,8512]{1,0:T(8,128)(2,1)} async-done(((bf16[64,8512]{1,0:T(8,128)(2,1)}), bf16[2048,8512]{1,0:T(8,128)(2,1)}) %all-gather.7.cloned.1.call-update) | async-done | bytes 34865168 | tf_op jit(solution)/shard_map/all_gather | solution.py:195
  334.4 44.9 %fusion.361 = f32[1024,8512]{1,0:T(8,128)} fusion(bf16[1024,2048]{1,0:T(8,128)(2,1)} %fusion.242, bf16[2048,8512]{1,0:T(8,128)(2,1)} %all-gather.7.cloned.1.call-done), kind=kOutput, calls=%fused_computation.609 | convolution fusion | flops 35701915648 | bytes 73924608 | tf_op jit(solution)/shard_map/dot_general | solution.py:204
  379.3 12.4 fusion.354
  436.5 20.9 fusion.281
  524.8 260.4 %while.134 = (s32[]{:T(128)}, f32[64,64,128]{2,1,0:T(8,128)S(1)}, f32[2,256,64,64]{1,0,3,2:T(2,128)}, s32[2,256]{1,0:T(2,128)S(1)}, f32[2,256,64]{1,2,0:T(8,128)...) while((s32[]{:T(128)}, f32[64,64,128]{2,1,0:T(8,128)S(1)}, ...), condition=%wide.region_22.23_spmd.clone, body=%wide.region_17.22_spmd.clone.sunk | while | flops 6569624576 | bytes 48974684 | solution.py:116
  528.8 21.4 fusion.554
  564.4 84.4 %dynamic_update_slice.151 = f32[2,256,64,64]{1,0,3,2:T(2,128)} dynamic-update-slice(f32[2,256,64,64]{1,0,3,2:T(2,128)} %get-tuple-element.2676, f32[1,256,64,64]{1,0,3,2:T(1,128)} %copy.1008, s32[]{:T(128)} %get-tuple-element.2674, s32[]{:T(128)} %constant.386.clone.1..sunk.5, s32[]{:T(128)} %constant.386.clone.1..sunk.5, s32[]{:T(128)} %constant.386.clone.1..sunk.5) | dynamic-update-slice | bytes 8388612 | tf_op jit(solution)/shard_map/while/body/jit(dynamic_update_index_in_dim)/dynamic_update_slice | solution.py:116
  658.7 21.4 fusion.554
  694.4 84.4 %dynamic_update_slice.151 = f32[2,256,64,64]{1,0,3,2:T(2,128)} dynamic-update-slice(f32[2,256,64,64]{1,0,3,2:T(2,128)} %get-tuple-element.2676, f32[1,256,64,64]{1,0,3,2:T(1,128)} %copy.1008, s32[]{:T(128)} %get-tuple-element.2674, s32[]{:T(128)} %constant.386.clone.1..sunk.5, s32[]{:T(128)} %constant.386.clone.1..sunk.5, s32[]{:T(128)} %constant.386.clone.1..sunk.5) | dynamic-update-slice | bytes 8388612 | tf_op jit(solution)/shard_map/while/body/jit(dynamic_update_index_in_dim)/dynamic_update_slice | solution.py:116
  795.2 10.5 reshape_reshape.6
  821.1 261.5 %while.133 = (s32[]{:T(128)}, f32[64,64,128]{2,1,0:T(8,128)S(1)}, f32[2,256,64,64]{1,0,3,2:T(2,128)}, s32[2,256]{1,0:T(2,128)S(1)}, f32[2,256,64]{1,2,0:T(8,128)...) while((s32[]{:T(128)}, f32[64,64,128]{2,1,0:T(8,128)S(1)}, ...), condition=%wide.region_10.11_spmd.clone, body=%wide.region_5.10_spmd.clone.sunk | while | flops 6569624576 | bytes 46877476 | solution.py:116
  825.8 21.4 fusion.543
  861.4 84.3 %dynamic_update_slice.150 = f32[2,256,64,64]{1,0,3,2:T(2,128)} dynamic-update-slice(f32[2,256,64,64]{1,0,3,2:T(2,128)} %get-tuple-element.2640, f32[1,256,64,64]{1,0,3,2:T(1,128)} %copy.1004, s32[]{:T(128)} %get-tuple-element.2638, s32[]{:T(128)} %constant.386.clone.1..sunk.4, s32[]{:T(128)} %constant.386.clone.1..sunk.4, s32[]{:T(128)} %constant.386.clone.1..sunk.4) | dynamic-update-slice | bytes 8388612 | tf_op jit(solution)/shard_map/while/body/jit(dynamic_update_index_in_dim)/dynamic_update_slice | solution.py:116
  956.5 21.4 fusion.543
  992.1 84.3 %dynamic_update_slice.150 = f32[2,256,64,64]{1,0,3,2:T(2,128)} dynamic-update-slice(f32[2,256,64,64]{1,0,3,2:T(2,128)} %get-tuple-element.2640, f32[1,256,64,64]{1,0,3,2:T(1,128)} %copy.1004, s32[]{:T(128)} %get-tuple-element.2638, s32[]{:T(128)} %constant.386.clone.1..sunk.4, s32[]{:T(128)} %constant.386.clone.1..sunk.4, s32[]{:T(128)} %constant.386.clone.1..sunk.4) | dynamic-update-slice | bytes 8388612 | tf_op jit(solution)/shard_map/while/body/jit(dynamic_update_index_in_dim)/dynamic_update_slice | solution.py:116
  1086.3 11.8 reshape.1561
  1098.2 11.7 reshape.1548
  1112.3 24.3 while.136
  1153.4 25.8 multiply_add_fusion.11
  1197.0 18.0 multiply_reduce_fusion.25
  1215.1 14.3 multiply_reduce_fusion.19
  1229.4 43.9 multiply_reduce_fusion.17
  1313.6 26.0 while.135
  1339.7 14.2 reshape.1653
  1353.9 14.2 reshape.1651
  1368.1 14.2 copy.788
  1382.3 14.2 copy.768
  1397.1 24.4 fusion.259
  1440.4 228.7 %while.132 = (s32[]{:T(128)}, f32[64,64,128]{2,1,0:T(8,128)S(1)}, f32[2,256,64,64]{1,3,2,0:T(8,128)}, f32[2,256,128]{2,1,0:T(8,128)}, f32[2,256,128]{2,1,0:T(8,1...) while((s32[]{:T(128)}, f32[64,64,128]{2,1,0:T(8,128)S(1)}, ...), condition=%wide.region_80.82_spmd, body=%wide.region_65.81_spmd.sunk | while | flops 14882882560 | bytes 180704672 | solution.py:116
  1461.5 18.5 multiply_reduce_fusion.39
  1489.4 28.0 fusion.525
  1575.3 18.5 multiply_reduce_fusion.39
  1602.5 28.2 fusion.525
  1676.3 233.7 %while.131 = (s32[]{:T(128)}, f32[64,64,128]{2,1,0:T(8,128)S(1)}, f32[2,256,64,64]{1,3,2,0:T(8,128)}, f32[2,256,128]{2,1,0:T(8,128)}, f32[2,256,128]{2,1,0:T(8,1...) while((s32[]{:T(128)}, f32[64,64,128]{2,1,0:T(8,128)S(1)}, ...), condition=%wide.region_52.54_spmd, body=%wide.region_37.53_spmd.sunk | while | flops 14882882560 | bytes 180704672 | solution.py:116
  1698.2 18.5 multiply_reduce_fusion.36
  1725.4 28.2 fusion.497
  1811.8 18.5 multiply_reduce_fusion.36
  1839.0 27.9 fusion.497
  1910.1 16.3 copy.818
  1926.3 14.8 reshape.1654
  1941.1 14.4 fusion.357
  1964.6 16.2 copy.815
  1980.8 14.7 reshape.1652
  1995.5 14.4 fusion.358
  2019.1 16.7 fusion.300
  2035.8 15.7 fusion.303
  2051.7 11.9 multiply_reduce_fusion.14
  2063.7 32.6 multiply_reduce_fusion.15
  2097.3 23.1 pad_maximum_fusion.2
  2153.9 24.9 broadcast_multiply_fusion
  2178.8 12.6 pad_add_fusion.1
  2195.5 12.7 pad_add_fusion
  2240.4 50.4 %fusion.248 = (f32[2048]{0:T(1024)S(1)}, f32[1024]{0:T(1024)}, f32[1024,2048]{1,0:T(8,128)}) fusion(bf16[2,512,2048]{2,1,0:T(8,128)(2,1)} %param.31, f32[1024]{0:T(1024)S(1)} %bitcast.1088, f32[2048]{0:T(1024)S(1)} %copy-done.94, bf16[1024,8512]{1,0:T(8,128)(2,1)} %bitcast.1055, bf16[2048,8512]{1,0:T(8,128)(2,1)} %all-gather.7.cloned.1.call-done), kind=kOutput, calls=%fused_computation.411 | convolution fusion | flops 35716595712 | bytes 64905216 | tf_op jit(solution)/shard_map/dot_general | solution.py:286
  2290.8 48.0 %convolution_bitcast_fusion = f32[2048,8512]{0,1:T(8,128)} fusion(bf16[2,512,8512]{2,1,0:T(8,128)(2,1)} %scatter-add.4, bf16[2,512,2048]{2,1,0:T(8,128)(2,1)} %param.31, f32[2048]{0:T(1024)S(1)} %copy-done.94, f32[2,512]{1,0:T(2,128)S(1)} %copy-done.121), kind=kOutput, calls=%fused_computation.350 | convolution fusion | flops 35710304256 | bytes 91369472 | tf_op jit(solution)/shard_map/dot_general | solution.py:167
  2338.8 46.7 %pad_maximum_fusion = f32[2048,8513]{0,1:T(8,128)} fusion(f32[2048,1]{0,1:T(1,128)S(1)} %bitcast.1092, f32[2048,8512]{0,1:T(8,128)} %convolution_bitcast_fusion), kind=kLoop, calls=%fused_computation.346 | loop fusion | flops 17434624 | bytes 139476992 | tf_op jit(solution)/shard_map/concatenate | solution.py:168
  2385.6 68.3 %copy.819 = f32[2048,8513]{1,0:T(8,128)} copy(f32[2048,8513]{0,1:T(8,128)} %pad_maximum_fusion) | data formatting | bytes 139476992
  2455.1 24.3 fusion.252
  2479.5 44.9 %all-reduce.38 = (f32[4352]{0:T(1024)S(1)}, f32[64]{0:T(128)}, f32[64]{0:T(128)}, f32[64]{0:T(128)}) all-reduce(f32[4352]{0:T(1024)S(1)} %add.408, f32[64]{0:T(128)S(1)} %add.409, f32[64]{0:T(128)S(1)} %add_multiply_fusion, f32[64]{0:T(128)S(1)} %add.411), channel_id=5, replica_groups=mesh['dp'=16,'seq'=2] {'dp','seq'}, use_global_device_ids=true, to_apply=%region_103.105.clone | all-reduce | flops 4544 | bytes 36352
  2535.5 396.9 %reduce-scatter.6.cloned.1.call-done = f32[128,2049]{0,1:T(8,128)} async-done(((f32[4096,2049]{0,1:T(8,128)}), f32[128,2049]{0,1:T(8,128)}) %reduce-scatter.6.cloned.1.call-update) | async-done | bytes 1049104 | tf_op jit(solution)/shard_map/reduce_scatter | solution.py:248
  2936.2 1469.8 %reduce-scatter.8.cloned.1.call-done = f32[64,8513]{1,0:T(8,128)} async-done(((f32[2048,8513]{1,0:T(8,128)}), f32[64,8513]{1,0:T(8,128)}) %reduce-scatter.8.cloned.1.call-update) | async-done | bytes 2179344
  (934 shorter events, 785.2 us)
Async XLA Ops:
  7.2 200.9 %all-gather.11.cloned.1.call-start = ((), (), s32[]{:S(2)}) async-start(), calls=%async_computation.4 | async-start | bytes 17301504 | tf_op jit(solution)/shard_map/all_gather | solution.py:197
  7.9 326.5 %all-gather.7.cloned.1.call-start = ((), (), s32[]{:S(2)}) async-start(), calls=%async_computation.2 | async-start | bytes 36225024 | tf_op jit(solution)/shard_map/all_gather | solution.py:195
  8.7 1131.8 %all-gather.9.cloned.1.call-start = ((), (), s32[]{:S(2)}) async-start(), calls=%async_computation.3 | async-start | bytes 6291456 | tf_op jit(solution)/shard_map/all_gather | solution.py:34
  53.5 179.2 %copy-start.93 = (f32[2048]{0:T(1024)}, f32[2048]{0:T(1024)S(1)}, u32[]{:S(2)}) copy-start(f32[2048]{0:T(1024)S(1)} %convert_element_type.141) | copy-start | bytes 24580
  57.2 175.5 %copy-start.98 = (f32[1,4,2,128]{3,1,2,0:T(4,128)}, f32[1,4,2,128]{3,1,2,0:T(4,128)S(1)}, u32[]{:S(2)}) copy-start(f32[1,4,2,128]{3,1,2,0:T(4,128)S(1)} %copy.912) | copy-start | bytes 12292
  129.8 266.7 %copy-start.125 = (f32[64]{0:T(128)}, f32[64]{0:T(128)S(1)}, u32[]{:S(2)}) copy-start(f32[64]{0:T(128)S(1)} %exp.226) | copy-start | bytes 772
  131.6 270.0 %copy-start.115 = (pred[512]{0:T(512)(128)(4,1)}, pred[512]{0:T(512)(128)(4,1)S(1)}, u32[]{:S(2)}) copy-start(pred[512]{0:T(512)(128)(4,1)S(1)} %get-tuple-element.1960) | copy-start | bytes 1540
  132.4 269.4 %copy-start.117 = (pred[512]{0:T(512)(128)(4,1)}, pred[512]{0:T(512)(128)(4,1)S(1)}, u32[]{:S(2)}) copy-start(pred[512]{0:T(512)(128)(4,1)S(1)} %get-tuple-element.1964) | copy-start | bytes 1540
  201.6 190.1 %copy-start.119 = (pred[2,3]{1,0:T(4,128)(4,1)}, pred[2,3]{1,0:T(4,128)(4,1)S(1)}, u32[]{:S(2)}) copy-start(pred[2,3]{1,0:T(4,128)(4,1)S(1)} %slice_compare_fusion) | copy-start | bytes 22
  392.8 43.5 collective-permute-start
  397.9 20.6 copy-start.42
  397.9 20.6 copy-start.44
  399.8 18.8 copy-start.38
  436.4 21.0 copy-start.63
  436.4 32.0 copy-start.65
  524.9 25.2 copy-start.28
  528.8 21.4 copy-start.32
  558.1 91.4 %copy-start.33 = (f32[256,64]{0,1:T(8,128)S(1)}, f32[256,64]{0,1:T(8,128)}, u32[]{:S(2)}) copy-start(f32[256,64]{0,1:T(8,128)} %copy-done.32) | copy-start | bytes 196612 | tf_op jit(solution)/shard_map/while
  564.4 90.4 %copy-start.29 = (f32[2,256,128]{2,1,0:T(8,128)S(1)}, f32[2,256,128]{2,1,0:T(8,128)}, u32[]{:S(2)}) copy-start(f32[2,256,128]{2,1,0:T(8,128)} %copy-done.28) | copy-start | bytes 786436 | tf_op jit(solution)/shard_map/while
  654.9 25.2 copy-start.28
  658.7 21.4 copy-start.32
  688.0 91.4 %copy-start.33 = (f32[256,64]{0,1:T(8,128)S(1)}, f32[256,64]{0,1:T(8,128)}, u32[]{:S(2)}) copy-start(f32[256,64]{0,1:T(8,128)} %copy-done.32) | copy-start | bytes 196612 | tf_op jit(solution)/shard_map/while
  694.4 90.4 %copy-start.29 = (f32[2,256,128]{2,1,0:T(8,128)S(1)}, f32[2,256,128]{2,1,0:T(8,128)}, u32[]{:S(2)}) copy-start(f32[2,256,128]{2,1,0:T(8,128)} %copy-done.28) | copy-start | bytes 786436 | tf_op jit(solution)/shard_map/while
  825.8 21.4 copy-start.34
  855.1 91.3 %copy-start.35 = (f32[256,64]{0,1:T(8,128)S(1)}, f32[256,64]{0,1:T(8,128)}, u32[]{:S(2)}) copy-start(f32[256,64]{0,1:T(8,128)} %copy-done.34) | copy-start | bytes 196612 | tf_op jit(solution)/shard_map/while
  956.5 21.4 copy-start.34
  985.8 91.3 %copy-start.35 = (f32[256,64]{0,1:T(8,128)S(1)}, f32[256,64]{0,1:T(8,128)}, u32[]{:S(2)}) copy-start(f32[256,64]{0,1:T(8,128)} %copy-done.34) | copy-start | bytes 196612 | tf_op jit(solution)/shard_map/while
  1086.3 335.2 %all-gather.13.cloned.1.call-start = ((), (), s32[]{:S(2)}) async-start(), calls=%async_computation.5 | async-start | bytes 6291456 | tf_op jit(solution)/shard_map/all_gather | solution.py:56
  1112.3 30.7 copy-start.101
  1311.1 1213.9 %all-reduce.42.cloned.1.call-start = ((), (), s32[]{:S(2)}) async-start(), calls=%async_computation.8 | async-start | bytes 139264
  1397.1 26.9 copy-start.102
  1457.8 22.3 copy-start.36
  1461.4 18.6 copy-start.54
  1527.9 18.9 copy-start.14
  1571.5 22.3 copy-start.36
  1575.2 18.6 copy-start.54
  1641.2 18.7 copy-start.14
  1694.4 22.3 copy-start.37
  1764.1 18.7 copy-start.15
  1808.0 22.3 copy-start.37
  1811.7 18.6 copy-start.55
  1877.3 19.0 copy-start.15
  2019.0 32.5 slice-start.3
  2019.1 32.5 slice-start.4
  2019.1 32.5 copy-start.21
  2019.1 32.5 copy-start.66
  2019.1 32.5 copy-start.110
  2019.1 32.5 copy-start.112
  2019.1 32.5 copy-start.114
  2063.6 32.7 copy-start.18
  2063.7 33.6 copy-start.97
  2097.2 835.2 %reduce-scatter.6.cloned.1.call-start = ((), (), s32[]{:S(2)}) async-start(), calls=%async_computation.6 | async-start | bytes 34738176 | tf_op jit(solution)/shard_map/reduce_scatter | solution.py:248
  2120.5 2285.6 %reduce-scatter.8.cloned.1.call-start = ((), (), s32[]{:S(2)}) async-start(), calls=%async_computation.7 | async-start | bytes 72450048
  2212.4 25.8 collective-permute-start.1
  2240.4 50.4 %copy-start.121 = (f32[2,512]{1,0:T(2,128)S(1)}, f32[2,512]{1,0:T(2,128)}, u32[]{:S(2)}) copy-start(f32[2,512]{1,0:T(2,128)} %get-tuple-element.2036) | copy-start | bytes 12292
  2455.0 24.4 copy-start.130
  2455.0 24.4 copy-start.131
  2455.0 24.4 copy-start.91
  2455.1 24.4 copy-start.92
  2455.1 24.4 copy-start.127
  2455.1 24.4 copy-start.128
  2455.1 24.4 copy-start.132
  2455.1 71.3 %copy-start.122 = (f32[1024]{0:T(1024)S(1)}, f32[1024]{0:T(1024)}, u32[]{:S(2)}) copy-start(f32[1024]{0:T(1024)} %get-tuple-element.1774) | copy-start | bytes 12292
  2455.1 71.3 %copy-start.100 = (f32[1,4,2,128]{3,1,2,0:T(4,128)S(1)}, f32[1,4,2,128]{3,1,2,0:T(4,128)}, u32[]{:S(2)}) copy-start(f32[1,4,2,128]{3,1,2,0:T(4,128)} %copy-done.98) | copy-start | bytes 12292
  (116 other events, 1135.9 us)
Sparse Core Ops, SparseCore 0:
  11.0 119.6 all-gather.10
  133.5 200.8 all-gather.6
  1086.4 54.0 all-gather.8
  1311.3 62.0 all-gather.12
  2097.4 117.8 all-reduce.41
  2217.4 714.9 reduce-scatter.5
  2935.3 1470.6 reduce-scatter.7
where the time goes:
time: 4450 us; the launch traced here: 4410 us
  waiting for transfers between devices  1970 us (44%)
  local copies, waits for them, and re-layouts  916 us (21%)
  matrix products  783 us (18%)
  other arithmetic  474 us (11%)
  blocking collectives  225 us (5%)
    unnamed x9, waiting for transfers between devices  1470 us
    reduce_scatter x1, waiting for transfers between devices, shards(): lax.psum_scatter(weight_term(mixed_low, cotangent, gate_gain_grad), ('dp'...  397 us
    dynamic_update_slice x12, local copies, waits for them, and re-layouts, scan_stretches(): lax.scan(jax.checkpoint(stretch_step), carry_state, pieces)  363 us
    dot_general x12, matrix products, stretch_step(): within = jnp.einsum('tsh,shp->thp', mixing, scaled, precision=HIGHEST)  272 us
    dot_general x16, matrix products, stretch_step(): jnp.einsum('tn,hpn->thp', c_proj, carry_state, precision=HIGHEST)  107 us
    all_gather x1, waiting for transfers between devices, shards(): lax.all_gather(in_weight, ('dp', 'seq'), axis=0, tiled=True)  102 us
    unnamed x232, local copies, waits for them, and re-layouts  97.2 us
    dot_general x16, matrix products, stretch_step(): jnp.einsum('shp,sn->hpn', scaled * outflow[:, :, None], b_proj, precision...  89.3 us
  transfers between devices with their start and end apart: 9, of which 4 were waited for; matrix products, arithmetic and copies ran while one was open for 14% of the time, Pallas kernels for 0%

commit v1 on v0

v1 whole, which is shorter than its diff:
```python
from functools import partial

import jax
import jax.numpy as jnp
from jax import lax
from jax.experimental import pallas as pl
from jax.experimental.pallas import tpu as pltpu
from jax.sharding import PartitionSpec as P

H = 64
HD = 64
N = 128
CONV = 4
DI = 4096
XBC = 4352
PROJ = 8512
CD = XBC + H
Q = 128
LB = 256
EPS = 1e-05
HIGHEST = lax.Precision.HIGHEST
F32 = jnp.float32
BF = jnp.bfloat16
NEG = -1e30
VMEM_LIMIT = 60 * 1024 * 1024
BOTH = ("dp", "seq")


def dot(a, b):
    return lax.dot_general(a, b, (((1,), (0,)), ((), ())), preferred_element_type=F32)


def dot_nt(a, b):
    return lax.dot_general(a, b, (((1,), (1,)), ((), ())), preferred_element_type=F32)


def dot_tn(a, b):
    return lax.dot_general(a, b, (((0,), (0,)), ((), ())), preferred_element_type=F32)


def dot_exact(a, b):
    return lax.dot_general(
        a, b, (((1,), (0,)), ((), ())), preferred_element_type=F32, precision=HIGHEST
    )


def two_parts(v):
    high = v.astype(BF)
    return high, (v - high.astype(F32)).astype(BF)


def doubled(v):
    high = v.astype(BF).astype(F32)
    return jnp.concatenate([high, v - high], axis=1).astype(BF)


def head_sum(v, spread):
    high, low = two_parts(v)
    return dot_nt(high, spread) + dot_nt(low, spread)


def sigmoid(v):
    return 1.0 / (1.0 + jnp.exp(-v))


def softplus(z):
    e = jnp.exp(-jnp.abs(z))
    small = e * (1.0 - e * (0.5 - e * (1.0 / 3.0 - e * 0.25)))
    return jnp.maximum(z, 0.0) + jnp.where(e < 0.01, small, jnp.log(1.0 + e))


def lanes(i, width=LB):
    return pl.ds(pl.multiple_of(i * width, width), width)


def grid_iota(shape, dim):
    return lax.broadcasted_iota(jnp.int32, shape, dim)


def pair_masks():
    lane = grid_iota((Q, 128), 1)
    left = jnp.where(lane < HD, 1.0, 0.0).astype(BF)
    right = jnp.where(lane < HD, 0.0, 1.0).astype(BF)
    return left, right


def conv_block(ext, cw_ref, taps, at):
    t0 = ext[8:136, at]
    t1 = ext[7:135, at]
    t2 = ext[6:134, at]
    t3 = ext[5:133, at]
    total = cw_ref[4:5, at] + cw_ref[3:4, at] * t0
    total = total + taps[0] * (cw_ref[2:3, at] * t1)
    total = total + taps[1] * (cw_ref[1:2, at] * t2)
    total = total + taps[2] * (cw_ref[0:1, at] * t3)
    return total, (t0, t1, t2, t3)


def forward_kernel(
    pc_ref, front_ref, info_ref, infot_ref, cw_ref, hp_ref, spread_ref,
    y_ref, act_ref, st_ref, row_ref, fin_ref,
    ext, state, pre,
):
    chunk = pl.program_id(1)

    @pl.when(chunk == 0)
    def _():
        ext[0:8, :] = front_ref[:, :XBC]
        state[...] = jnp.zeros_like(state)
        pre[...] = jnp.zeros_like(pre)

    @pl.when(chunk > 0)
    def _():
        ext[0:8, :] = ext[128:136, :]

    ext[8:136, :] = pc_ref[:, :XBC]
    info = info_ref[...]
    taps = [jnp.broadcast_to(info[:, k : k + 1], (Q, LB)) for k in (1, 2, 3)]

    @pl.loop(0, XBC // LB)
    def _(i):
        at = lanes(i)
        out, _ = conv_block(ext, cw_ref, taps, at)
        act_ref[:, at] = (out * sigmoid(out)).astype(BF)

    z = pc_ref[:, XBC:CD] + hp_ref[0:1, :]
    dt = softplus(z)
    decay = -dt * hp_ref[1:2, :]
    rows, cols = grid_iota((Q, Q), 0), grid_iota((Q, Q), 1)
    lower = jnp.where(cols <= rows, 1.0, 0.0)
    cs = dot_exact(lower, decay)
    shifted = cs - jnp.log(jnp.maximum(dt, 1e-37))
    inflow = jnp.exp(cs) * info[:, 4:5]
    outflow = jnp.exp(cs[Q - 1 : Q, :] - shifted) * info[:, 5:6]
    before = pre[0:1, :]
    row_ref[:, 0:64] = cs
    row_ref[:, 64:128] = shifted
    row_ref[:, 128:192] = jnp.exp(before + cs) * info[:, 6:7]
    row_ref[:, 192:256] = z
    pre[0:1, :] = before + cs[Q - 1 : Q, :]
    turned = jnp.transpose(jnp.concatenate([cs, shifted], axis=1))
    same = (info[:, 0:1] == infot_ref[0:1, :]) & (cols <= rows)
    bias = jnp.where(same, 0.0, NEG)
    b_proj = act_ref[:, DI : DI + N]
    c_proj = act_ref[:, DI + N : XBC]
    affinity = dot_nt(c_proj, b_proj)
    in_parts = doubled(inflow)
    out_parts = doubled(outflow)

    @pl.loop(0, DI // LB)
    def _(i):
        at = lanes(i)
        spread = spread_ref[:, at]
        in_wide = dot(in_parts, spread)
        out_wide = dot(out_parts, spread)
        held = state[:, at]
        low = held.astype(BF)
        st_ref[:, at] = low
        y_ref[:, at] = dot(c_proj, low) * in_wide
        given = (act_ref[:, at].astype(F32) * out_wide).astype(BF)
        state[:, at] = held * in_wide[Q - 1 : Q, :] + dot_tn(b_proj, given)

    left, right = pair_masks()
    for p in range(H // 2):
        weights = []
        for h in (2 * p, 2 * p + 1):
            gap = (cs[:, h : h + 1] - turned[64 + h : 65 + h, :]) + bias
            weights.append((affinity * jnp.exp(gap)).astype(BF))
        x = act_ref[:, p * 128 : (p + 1) * 128]
        blocks = jnp.concatenate([x * left, x * right], axis=0)
        y_ref[:, p * 128 : (p + 1) * 128] += dot(jnp.concatenate(weights, axis=1), blocks)

    @pl.when(chunk == pl.num_programs(1) - 1)
    def _():
        fin_ref[...] = state[...].astype(BF)


def gate_kernel(
    y_ref, act_ref, row_ref, sin_ref, gate_ref, mg_ref, gain_ref, hp_ref, spread_ref,
    mixed_ref, dy_ref, dgate_ref, dot_ref, dsin_ref, skip_ref,
    full, gated,
):
    chunk = pl.program_id(1)

    @pl.when(chunk == 0)
    def _():
        dsin_ref[...] = jnp.zeros_like(dsin_ref)

    @pl.when((chunk == 0) & (pl.program_id(0) == 0))
    def _():
        skip_ref[...] = jnp.zeros_like(skip_ref)

    c_proj = act_ref[:, DI + N : XBC]
    parts = doubled(row_ref[:, 128:192])
    skip_parts = doubled(jnp.broadcast_to(hp_ref[2:3, :], (16, H)))

    def first(i, sums):
        at = lanes(i)
        spread = spread_ref[:, at]
        flow = dot(parts, spread)
        y = y_ref[:, at] + dot(c_proj, sin_ref[:, at]) * flow
        full[:, at] = y
        out = y + dot(skip_parts, spread)[0:1, :] * act_ref[:, at].astype(F32)
        g = gate_ref[:, at]
        v = out * (g * sigmoid(g))
        gated[:, at] = v
        e = mg_ref[:, at] * gain_ref[0:1, at]
        return sums[0] + v * v, sums[1] + e * v

    zero = jnp.zeros((Q, LB), F32)
    squares, cross = lax.fori_loop(0, DI // LB, first, (zero, zero))
    rs = lax.rsqrt(jnp.sum(squares, axis=1, keepdims=True) * (1.0 / DI) + EPS)
    mean_eu = jnp.sum(cross, axis=1, keepdims=True) * rs * (1.0 / DI)
    rs = jnp.broadcast_to(rs, (Q, LB))
    mean_eu = jnp.broadcast_to(mean_eu, (Q, LB))

    def second(i, total):
        at = lanes(i)
        spread = spread_ref[:, at]
        flow = dot(parts, spread)
        y = full[:, at]
        x = act_ref[:, at].astype(F32)
        out = y + dot(skip_parts, spread)[0:1, :] * x
        g = gate_ref[:, at]
        sig = sigmoid(g)
        sl = g * sig
        u = gated[:, at] * rs
        gain = gain_ref[0:1, at]
        mixed_ref[:, at] = (u * gain).astype(BF)
        grad = (mg_ref[:, at] * gain - u * mean_eu) * rs
        dgate_ref[:, at] = (grad * out * (sig + sl * (1.0 - sig))).astype(BF)
        dy = (grad * sl).astype(BF)
        dy_ref[:, at] = dy
        dyf = dy.astype(F32)
        dsin_ref[:, at] += dot_tn(c_proj, (dyf * flow).astype(BF))
        skip_ref[0:1, at] += jnp.sum(dyf * x, axis=0, keepdims=True)
        return total + head_sum(dyf * y, spread[:H])

    dot_ref[...] = lax.fori_loop(0, DI // LB, second, jnp.zeros((Q, H), F32))


def backward_kernel(
    pc_ref, halo_ref, info_ref, infot_ref, cw_ref, hp_ref, spread_ref,
    dy_ref, st_ref, sin_ref, dsin_ref, row_ref, prev_ref, pdot_ref,
    dproj_ref, front_ref, cwg_ref, hg_ref,
    ext, act, slope, dact, d1, d2, d3, dstate, state,
):
    step = pl.program_id(1)
    chunk = pl.num_programs(1) - 1 - step

    @pl.when((step == 0) & (pl.program_id(0) == 0))
    def _():
        cwg_ref[...] = jnp.zeros_like(cwg_ref)
        hg_ref[...] = jnp.zeros_like(hg_ref)

    @pl.when(step == 0)
    def _():
        dstate[...] = dsin_ref[...].astype(F32)
        for d in (d1, d2, d3):
            d[0:8, :] = jnp.zeros((8, XBC), F32)
            d[136:144, :] = jnp.zeros((8, XBC), F32)

    @pl.when(step > 0)
    def _():
        for d in (d1, d2, d3):
            d[136:144, :] = d[8:16, :]

    ext[0:8, :] = halo_ref[:, :XBC]
    ext[8:136, :] = pc_ref[:, :XBC]
    info = info_ref[...]
    taps = [jnp.broadcast_to(info[:, k : k + 1], (Q, LB)) for k in (1, 2, 3)]

    @pl.loop(0, XBC // LB)
    def _(i):
        at = lanes(i)
        out, _ = conv_block(ext, cw_ref, taps, at)
        sig = sigmoid(out)
        sl = out * sig
        act[:, at] = sl.astype(BF)
        slope[:, at] = sig + sl * (1.0 - sig)

    cs = row_ref[:, 0:64]
    shifted = row_ref[:, 64:128]
    z = row_ref[:, 192:256]
    inflow = jnp.exp(cs) * info[:, 4:5]
    outflow = jnp.exp(cs[Q - 1 : Q, :] - shifted) * info[:, 5:6]
    entry = jnp.where(chunk == 0, 1.0, prev_ref[7:8, 128:192])
    entry_parts = doubled(jnp.broadcast_to(entry, (16, H)))
    skip_parts = doubled(jnp.broadcast_to(hp_ref[2:3, :], (16, H)))
    in_parts = doubled(inflow)
    out_parts = doubled(outflow)
    rows, cols = grid_iota((Q, Q), 0), grid_iota((Q, Q), 1)
    turned = jnp.transpose(row_ref[:, 0:128])
    same = (info[:, 0:1] == infot_ref[0:1, :]) & (rows <= cols)
    bias = jnp.where(same, 0.0, NEG)
    b_proj = act[:, DI : DI + N]
    c_proj = act[:, DI + N : XBC]
    affinity = dot_nt(b_proj, c_proj)

    def shared(i, sums):
        db, dc, rdep, kept = sums
        at = lanes(i)
        spread = spread_ref[:, at]
        heads = spread[:H]
        s = st_ref[:, at].astype(F32) + dot(entry_parts, spread)[0:1, :] * sin_ref[:, at].astype(F32)
        s_low = s.astype(BF)
        in_wide = dot(in_parts, spread)
        out_wide = dot(out_parts, spread)
        ds = dstate[:, at]
        ds_low = ds.astype(BF)
        dep = out_wide * dot(b_proj, ds_low)
        dact[:, at] = dep
        x = act[:, at].astype(F32)
        rdep = rdep + head_sum(x * dep, heads)
        db = db + dot_nt((x * out_wide).astype(BF), ds_low)
        dye = (dy_ref[:, at].astype(F32) * in_wide).astype(BF)
        dc = dc + dot_nt(dye, s_low)
        held = jnp.sum(ds * s, axis=0, keepdims=True)
        kept = kept + head_sum(jnp.broadcast_to(held, (16, LB)), heads)
        dstate[:, at] = in_wide[Q - 1 : Q, :] * ds + dot_tn(c_proj, dye)
        return db, dc, rdep, kept

    zero = jnp.zeros((Q, N), F32)
    db, dc, rdep, kept = lax.fori_loop(
        0, DI // LB, shared, (zero, zero, jnp.zeros((Q, H), F32), jnp.zeros((16, H), F32))
    )
    left, right = pair_masks()
    daff = jnp.zeros((Q, Q), F32)
    for p in range(H // 2):
        at = slice(p * 128, (p + 1) * 128)
        dy = dy_ref[:, at]
        blocks = jnp.concatenate([dy * left, dy * right], axis=0)
        x = act[:, at]
        both = dot_nt(x, blocks)
        weights = []
        for j in (0, 1):
            h = 2 * p + j
            gap = (turned[h : h + 1, :] - shifted[:, h : h + 1]) + bias
            decays = jnp.exp(gap)
            weights.append((affinity * decays).astype(BF))
            daff = daff + both[:, j * Q : (j + 1) * Q] * decays
        dact[:, at] += dot(jnp.concatenate(weights, axis=1), blocks)

    def finish(i, total):
        at = lanes(i)
        spread = spread_ref[:, at]
        x = act[:, at].astype(F32)
        dx = dact[:, at]
        dact[:, at] = dx + dot(skip_parts, spread)[0:1, :] * dy_ref[:, at].astype(F32)
        return total + head_sum(x * dx, spread[:H])

    rfull = lax.fori_loop(0, DI // LB, finish, jnp.zeros((Q, H), F32))
    daff_low = daff.astype(BF)
    dact[:, DI : DI + N] = db + dot(daff_low, c_proj)
    dact[:, DI + N : XBC] = dc + dot_tn(daff_low, b_proj)

    upper = jnp.where(cols >= rows, 1.0, 0.0)
    dec = dot_exact(upper, pdot_ref[...] - rfull)
    dec = dec + jnp.sum(rdep, axis=0, keepdims=True) + inflow[Q - 1 : Q, :] * kept[0:1, :]
    rate = hp_ref[1:2, :]
    dt = softplus(z)
    sig = sigmoid(z)
    dz = rfull * (sig / jnp.maximum(dt, 1e-37)) - rate * dec * sig
    dproj_ref[:, XBC:CD] = dz.astype(BF)
    hg_ref[0:1, :] += jnp.sum(dz, axis=0, keepdims=True)
    hg_ref[1:2, :] += jnp.sum(-dec * dt * rate, axis=0, keepdims=True)

    @pl.loop(0, XBC // LB)
    def _(i):
        at = lanes(i)
        g = dact[:, at] * slope[:, at]
        g1, g2, g3 = taps[0] * g, taps[1] * g, taps[2] * g
        d1[8:136, at] = g1
        d2[8:136, at] = g2
        d3[8:136, at] = g3
        w0, w1, w2, w3 = (cw_ref[k : k + 1, at] for k in range(4))
        total = w3 * g + w2 * d1[9:137, at] + w1 * d2[10:138, at] + w0 * d3[11:139, at]
        dproj_ref[:, at] = total.astype(BF)
        for k, (grad, shift) in enumerate(((g3, 3), (g2, 2), (g1, 1), (g, 0))):
            cwg_ref[k : k + 1, at] += jnp.sum(
                grad * ext[8 - shift : 136 - shift, at], axis=0, keepdims=True
            )
        cwg_ref[4:5, at] += jnp.sum(g, axis=0, keepdims=True)

    @pl.when(chunk == 0)
    def _():
        @pl.loop(0, XBC // LB)
        def _(i):
            at = lanes(i)
            w0, w1, w2 = (cw_ref[k : k + 1, at] for k in range(3))
            front_ref[:, at] = w2 * d1[1:9, at] + w1 * d2[2:10, at] + w0 * d3[3:11, at]


def shift_along(block, distance):
    devices = range(lax.axis_size("seq"))
    return lax.ppermute(block, "seq", [(i - distance, i) for i in devices if i - distance in devices])


def chained(local, keep, distance):
    seqs = keep.shape[0]
    wide = jnp.repeat(keep, HD, axis=1)[:, None, :]
    entering = shift_along(local, distance)
    for _ in range(lax.axis_size("seq") - 2):
        total = wide * entering.reshape(seqs, N, DI).astype(F32) + local.reshape(seqs, N, DI).astype(F32)
        entering = shift_along(total.reshape(seqs * N, DI).astype(BF), distance)
    return entering


def scatter_sum(part, rows, swap):
    n_dp, n_seq = lax.axis_size("dp"), lax.axis_size("seq")
    dp_bits, seq_bits = n_dp.bit_length() - 1, n_seq.bit_length() - 1
    cols = part.shape[1]
    blocks = part.reshape((2,) * (dp_bits + seq_bits) + (rows, cols))
    left = [("dp", b) for b in reversed(range(dp_bits))] + [("seq", b) for b in reversed(range(seq_bits))]
    seq_order = [("seq", b) for b in range(seq_bits)]
    if swap:
        order = [("dp", 0), ("dp", 1)] + seq_order + [("dp", b) for b in range(2, dp_bits)]
    else:
        order = [("dp", 0)] + seq_order + [("dp", b) for b in range(1, dp_bits)]
    for number, (axis, bit) in enumerate(order):
        at = left.index((axis, bit))
        left.pop(at)
        mine = (lax.axis_index(axis) >> bit) & 1
        kept = lax.dynamic_index_in_dim(blocks, mine, at, False)
        sent = lax.dynamic_index_in_dim(blocks, 1 - mine, at, False)
        got = lax.ppermute(sent, axis, [(i, i ^ (1 << bit)) for i in range(lax.axis_size(axis))])
        blocks = kept.astype(F32) + got.astype(F32)
        if number < len(order) - 1:
            blocks = blocks.astype(BF)
    return blocks


def scatter_halves(part, rows):
    half = part.shape[1] // 256 * 128
    return jnp.concatenate(
        [scatter_sum(part[:, :half], rows, False), scatter_sum(part[:, half:], rows, True)], axis=1
    )


def row_block(width, at=lambda s, c, n: s * n + c, height=Q):
    return lambda n: pl.BlockSpec((height, width), lambda s, c: (at(s, c, n), 0))


def params():
    return pltpu.CompilerParams(
        dimension_semantics=("arbitrary", "arbitrary"), vmem_limit_bytes=VMEM_LIMIT
    )


def shards(
    tokens, doc_start, in_weight, norm_gain, out_weight, gate_gain,
    conv_weight, conv_bias, dt_bias, a_log, skip_gain, out_grad,
):
    seqs, length, width = tokens.shape
    total = seqs * length
    chunks = length // Q
    in_rows, out_rows = in_weight.shape[0], out_weight.shape[0]

    conv_own = in_weight[:, DI:]
    gate_own = in_weight[:, :DI]
    gains = lax.all_gather(
        jnp.concatenate([norm_gain, gate_gain, conv_weight.reshape(-1), conv_bias]), BOTH
    )
    w_conv = lax.all_gather(conv_own, BOTH, axis=0, tiled=True)
    w_gate = lax.all_gather(gate_own, BOTH, axis=0, tiled=True)
    w_out = lax.all_gather(out_weight, BOTH, axis=0, tiled=True)
    own = conv_bias.shape[0]
    cut = in_rows + out_rows
    norm_full = gains[:, :in_rows].reshape(-1).astype(F32)
    gate_full = gains[:, in_rows:cut].reshape(1, DI).astype(F32)
    taps_full = gains[:, cut : cut + CONV * own].reshape(-1, CONV, own).transpose(1, 0, 2).reshape(CONV, XBC)
    bias_full = gains[:, cut + CONV * own :].reshape(1, XBC)
    cw = jnp.concatenate([taps_full, bias_full, jnp.zeros((3, XBC), BF)]).astype(F32)

    counts = jnp.cumsum(doc_start, axis=1)
    last = counts[:, length - 1 :]
    tail_mask = (counts[:, length - 8 :] == last)[:, :, None]
    tail = jnp.where(tail_mask, tokens[:, length - 8 :], jnp.zeros((), BF))
    front = shift_along(tail, 1)
    values = jnp.concatenate([tokens.reshape(total, width), front.reshape(seqs * 8, width)]).astype(F32)
    scale = lax.rsqrt(jnp.mean(values * values, axis=-1, keepdims=True) + EPS)
    hidden = (values * scale * norm_full[None, :]).astype(BF)
    projected = jnp.dot(hidden, w_conv, preferred_element_type=F32)
    hidden = hidden[:total]
    gate_part = jnp.dot(hidden, w_gate, preferred_element_type=F32)
    cotangent = out_grad.reshape(total, width)
    mixed_grad = lax.dot_general(
        cotangent, w_out, (((1,), (1,)), ((), ())), preferred_element_type=F32
    )

    by_chunk = counts.reshape(seqs, chunks, Q)
    entered = jnp.concatenate([jnp.zeros((seqs, 1), counts.dtype), by_chunk[:, :-1, -1]], axis=1)[:, :, None]
    flags = [counts.reshape(total)]
    for k in (1, 2, 3):
        earlier = jnp.pad(counts, ((0, 0), (k, 0)))[:, :length]
        flags.append((earlier == counts).reshape(total))
    flags.append((by_chunk == entered).reshape(total))
    flags.append((by_chunk == by_chunk[:, :, -1:]).reshape(total))
    flags.append((counts == 0).reshape(total))
    info = jnp.pad(jnp.stack([f.astype(F32) for f in flags], axis=1), ((0, 0), (0, 128 - len(flags))))
    infot = jnp.broadcast_to(counts.reshape(1, total).astype(F32), (8, total))
    hp = jnp.pad(jnp.stack([dt_bias, jnp.exp(a_log), skip_gain]), ((0, 5), (0, 0)))
    spread = (jnp.arange(DI)[None, :] // HD == jnp.arange(2 * H)[:, None] % H).astype(BF)

    grid = (seqs, chunks)
    at_row = lambda s, c: (s * chunks + c, 0)
    fixed = lambda s, c: (0, 0)
    per_seq = lambda s, c: (s, 0)
    common_specs = [
        pl.BlockSpec((Q, 128), at_row),
        pl.BlockSpec((8, Q), lambda s, c: (0, s * chunks + c)),
        pl.BlockSpec((8, XBC), fixed),
        pl.BlockSpec((8, H), fixed),
        pl.BlockSpec((2 * H, DI), fixed),
    ]
    y, act, states, rowp, final = pl.pallas_call(
        forward_kernel,
        grid=grid,
        in_specs=[
            pl.BlockSpec((Q, CD), at_row),
            pl.BlockSpec((8, CD), lambda s, c: (total // 8 + s, 0)),
        ]
        + common_specs,
        out_specs=[
            pl.BlockSpec((Q, DI), at_row),
            pl.BlockSpec((Q, XBC), at_row),
            pl.BlockSpec((N, DI), at_row),
            pl.BlockSpec((Q, 256), at_row),
            pl.BlockSpec((N, DI), per_seq),
        ],
        out_shape=[
            jax.ShapeDtypeStruct((total, DI), F32),
            jax.ShapeDtypeStruct((total, XBC), BF),
            jax.ShapeDtypeStruct((seqs * chunks * N, DI), BF),
            jax.ShapeDtypeStruct((total, 256), F32),
            jax.ShapeDtypeStruct((seqs * N, DI), BF),
        ],
        scratch_shapes=[
            pltpu.VMEM((136, XBC), F32),
            pltpu.VMEM((N, DI), F32),
            pltpu.VMEM((8, H), F32),
        ],
        compiler_params=params(),
        name="scan_forward",
    )(projected, projected, info, infot, cw, hp, spread)

    keep = rowp.reshape(seqs, length, 256)[:, length - 1, 128:192]
    entering = chained(final, keep, 1)

    mixed, dy, dgate, pdot, dsin, skip_sums = pl.pallas_call(
        gate_kernel,
        grid=grid,
        in_specs=[
            pl.BlockSpec((Q, DI), at_row),
            pl.BlockSpec((Q, XBC), at_row),
            pl.BlockSpec((Q, 256), at_row),
            pl.BlockSpec((N, DI), per_seq),
            pl.BlockSpec((Q, DI), at_row),
            pl.BlockSpec((Q, DI), at_row),
            pl.BlockSpec((1, DI), fixed),
            pl.BlockSpec((8, H), fixed),
            pl.BlockSpec((2 * H, DI), fixed),
        ],
        out_specs=[
            pl.BlockSpec((Q, DI), at_row),
            pl.BlockSpec((Q, DI), at_row),
            pl.BlockSpec((Q, DI), at_row),
            pl.BlockSpec((Q, H), at_row),
            pl.BlockSpec((N, DI), per_seq),
            pl.BlockSpec((8, DI), fixed),
        ],
        out_shape=[
            jax.ShapeDtypeStruct((total, DI), BF),
            jax.ShapeDtypeStruct((total, DI), BF),
            jax.ShapeDtypeStruct((total, DI), BF),
            jax.ShapeDtypeStruct((total, H), F32),
            jax.ShapeDtypeStruct((seqs * N, DI), F32),
            jax.ShapeDtypeStruct((8, DI), F32),
        ],
        scratch_shapes=[pltpu.VMEM((Q, DI), F32), pltpu.VMEM((Q, DI), F32)],
        compiler_params=params(),
        name="gate_both",
    )(y, act, rowp, entering, gate_part, mixed_grad, gate_full, hp, spread)

    leaving = chained(dsin.astype(BF), keep, -1)

    values = values[:total]
    output = (values + jnp.dot(mixed, w_out, preferred_element_type=F32)).astype(BF)
    dw_out = dot_tn(mixed, cotangent).astype(BF)
    out_weight_grad = scatter_halves(dw_out, out_rows)
    dw_gate = dot_tn(hidden, dgate).astype(BF)
    gate_cols_grad = scatter_halves(dw_gate, in_rows)

    back = lambda s, c: (s * chunks + chunks - 1 - c, 0)
    before = lambda s, c: jnp.where(
        c == chunks - 1, total // 8 + s, (s * chunks + chunks - 1 - c) * (Q // 8) - 1
    )
    before_row = lambda s, c: jnp.maximum((s * chunks + chunks - 1 - c) * (Q // 8) - 1, 0)
    dproj, front_grad, conv_sums, head_sums = pl.pallas_call(
        backward_kernel,
        grid=grid,
        in_specs=[
            pl.BlockSpec((Q, CD), back),
            pl.BlockSpec((8, CD), lambda s, c: (before(s, c), 0)),
            pl.BlockSpec((Q, 128), back),
            pl.BlockSpec((8, Q), lambda s, c: (0, s * chunks + chunks - 1 - c)),
        ]
        + common_specs[2:]
        + [
            pl.BlockSpec((Q, DI), back),
            pl.BlockSpec((N, DI), back),
            pl.BlockSpec((N, DI), per_seq),
            pl.BlockSpec((N, DI), per_seq),
            pl.BlockSpec((Q, 256), back),
            pl.BlockSpec((8, 256), lambda s, c: (before_row(s, c), 0)),
            pl.BlockSpec((Q, H), back),
        ],
        out_specs=[
            pl.BlockSpec((Q, CD), back),
            pl.BlockSpec((8, XBC), per_seq),
            pl.BlockSpec((8, XBC), fixed),
            pl.BlockSpec((8, H), fixed),
        ],
        out_shape=[
            jax.ShapeDtypeStruct((total, CD), BF),
            jax.ShapeDtypeStruct((seqs * 8, XBC), F32),
            jax.ShapeDtypeStruct((8, XBC), F32),
            jax.ShapeDtypeStruct((8, H), F32),
        ],
        scratch_shapes=[
            pltpu.VMEM((136, XBC), F32),
            pltpu.VMEM((Q, XBC), BF),
            pltpu.VMEM((Q, XBC), F32),
            pltpu.VMEM((Q, XBC), F32),
            pltpu.VMEM((144, XBC), F32),
            pltpu.VMEM((144, XBC), F32),
            pltpu.VMEM((144, XBC), F32),
            pltpu.VMEM((N, DI), F32),
            pltpu.VMEM((8, H), F32),
        ],
        compiler_params=params(),
        name="scan_backward",
    )(projected, projected, info, infot, cw, hp, spread, dy, states, entering, leaving, rowp, rowp, pdot)

    tail_back = shift_along(front_grad.astype(BF), -1).reshape(seqs, 8, XBC)
    tail_back = jnp.where(tail_mask, tail_back.astype(F32), 0.0)
    dproj = dproj.reshape(seqs, length, CD)
    ends = dproj[:, length - 8 :, :XBC].astype(F32) + tail_back
    dproj = lax.dynamic_update_slice(dproj, ends.astype(BF), (0, length - 8, 0)).reshape(total, CD)

    dw_conv = dot_tn(hidden, dproj).astype(BF)
    conv_cols_grad = scatter_halves(dw_conv, in_rows)
    hidden_grad = lax.dot_general(
        dgate, w_gate, (((1,), (1,)), ((), ())), preferred_element_type=F32
    ) + lax.dot_general(dproj, w_conv, (((1,), (1,)), ((), ())), preferred_element_type=F32)
    scale = scale[:total]
    normed = values * scale
    weighted = hidden_grad * norm_full[None, :]
    input_grad = cotangent.astype(F32) + scale * (
        weighted - normed * jnp.mean(weighted * normed, axis=-1, keepdims=True)
    )

    in_weight_grad = jnp.concatenate([gate_cols_grad, conv_cols_grad], axis=1)
    norm_share = jnp.sum(in_weight_grad * in_weight.astype(F32), axis=1) / norm_gain.astype(F32)
    gate_share = jnp.sum(out_weight_grad * out_weight.astype(F32), axis=1) / gate_gain.astype(F32)

    skip_grad = jnp.sum(skip_sums[0].reshape(H, HD), axis=1)
    small = jnp.concatenate([conv_sums[:5].reshape(-1), head_sums[:2].reshape(-1), skip_grad])
    small = lax.psum(small, BOTH)
    place = lax.axis_index("dp") * lax.axis_size("seq") + lax.axis_index("seq")
    shares = lax.dynamic_slice(small[: 5 * XBC].reshape(5, XBC), (0, place * own), (5, own))
    heads = small[5 * XBC :].reshape(3, H)
    return (
        output.reshape(seqs, length, width),
        input_grad.astype(BF).reshape(seqs, length, width),
        in_weight_grad,
        norm_share,
        out_weight_grad,
        gate_share,
        shares[:4],
        shares[4],
        heads[0],
        heads[1],
        heads[2],
    )


def solution(mesh):
    return jax.shard_map(
        shards,
        mesh=mesh,
        in_specs=(
            P("dp", "seq", None),
            P("dp", "seq"),
            P(("dp", "seq"), None),
            P(("dp", "seq")),
            P(("dp", "seq"), None),
            P(("dp", "seq")),
            P(None, ("dp", "seq")),
            P(("dp", "seq")),
            P(),
            P(),
            P(),
            P("dp", "seq", None),
        ),
        out_specs=(
            P("dp", "seq", None),
            P("dp", "seq", None),
            P(("dp", "seq"), None),
            P(("dp", "seq")),
            P(("dp", "seq"), None),
            P(("dp", "seq")),
            P(None, ("dp", "seq")),
            P(("dp", "seq")),
            P(),
            P(),
            P(),
        ),
        check_vma=False,
    )
```

time: 4450 us -> 1330 us (0.30)
  waiting for transfers between devices: 1970 us -> 457 us
  local copies, waits for them, and re-layouts: 916 us -> 129 us
  matrix products: 783 us -> 229 us
  other arithmetic: 474 us -> 80.1 us
  Pallas kernels: 0 us -> 328 us
  blocking collectives: 225 us -> 41.4 us
    unnamed x9 -> x4, waiting for transfers between devices: 1470 us -> 0.73 us
    dot_general x72 -> x9, matrix products: 783 us -> 229 us  [the longest x3 76.5 us: dot_tn(): lax.dot_general(a, b, (((0,), (0,)), ((), ())), preferred_element_type=F32)]
    reduce_scatter x1 -> x0, waiting for transfers between devices: 397 us -> none  [shards(): lax.psum_scatter(weight_term(mixed_low, cotangent, gate_gain_grad), ('dp'...]
    dynamic_update_slice x12 -> x0, local copies, waits for them, and re-layouts: 363 us -> none  [scan_stretches(): lax.scan(jax.checkpoint(stretch_step), carry_state, pieces)]
    pallas_call x0 -> x3, Pallas kernels: none -> 328 us  [the longest x1 156 us: shards(): pl.pallas_call(backward_kernel, grid=grid, in_specs=[pl.BlockSpec((Q, CD)...]
    ppermute x2 -> x34, waiting for transfers between devices: 0.01 us -> 214 us  [the longest x30 192 us: scatter_sum(): lax.ppermute(sent, axis, [(i, i ^ 1 << bit) for i in range(lax.axis_size(...]
    reduce_sum x19 -> x3, other arithmetic: 149 us -> 2.93 us  [the longest x1 1.72 us: shards(): jnp.sum(in_weight_grad * in_weight.astype(F32), axis=1)]
    all_gather x3 -> x0, blocking collectives: 137 us -> none  [the longest x1 68.1 us: shards(): lax.all_gather(conv_weight, ('dp', 'seq'), axis=1, tiled=True)]
  transfers between devices with their start and end apart: 9 -> 38, of which waited for: 4 -> 21; matrix products, arithmetic and copies ran while one was open for 14% -> 29% of each run, Pallas kernels for 0% -> 18%
where the time goes in v1:
time: 1330 us; the launch traced here: 1320 us
  waiting for transfers between devices  457 us (34%)
  Pallas kernels  328 us (25%)
  matrix products  229 us (17%)
  local copies, waits for them, and re-layouts  129 us (10%)
  other arithmetic  80.1 us (6%)
  blocking collectives  41.4 us (3%)
  starting transfers between devices  40.4 us (3%)
  between operations  15.2 us (1%)
    ppermute x30, waiting for transfers between devices, scatter_sum(): lax.ppermute(sent, axis, [(i, i ^ 1 << bit) for i in range(lax.axis_size(...  192 us
    pallas_call x1, Pallas kernels, shards(): pl.pallas_call(backward_kernel, grid=grid, in_specs=[pl.BlockSpec((Q, CD)...  156 us
    all_gather x1, waiting for transfers between devices, shards(): w_conv = lax.all_gather(conv_own, BOTH, axis=0, tiled=True)  100 us
    psum x1, waiting for transfers between devices, shards(): small = lax.psum(small, BOTH)  92.1 us
    pallas_call x1, Pallas kernels, shards(): pl.pallas_call(gate_kernel, grid=grid, in_specs=[pl.BlockSpec((Q, DI), at...  88.6 us
    pallas_call x1, Pallas kernels, shards(): pl.pallas_call(forward_kernel, grid=grid, in_specs=[pl.BlockSpec((Q, CD),...  83.2 us
    dot_general x3, matrix products, dot_tn(): lax.dot_general(a, b, (((0,), (0,)), ((), ())), preferred_element_type=F32)  76.5 us
    all_gather x1, waiting for transfers between devices, shards(): w_gate = lax.all_gather(gate_own, BOTH, axis=0, tiled=True)  47.7 us
  transfers between devices with their start and end apart: 38, of which 21 were waited for; matrix products, arithmetic and copies ran while one was open for 29% of the time, Pallas kernels for 18%

profile of v1, /device:TPU:0, one launch (start us, length us, event | category | flops | bytes accessed | tf_op | source)
XLA Modules:
  0.0 1320.6 jit_solution(11123069558348523833)
XLA Ops:
  14.9 4.8 collective-permute-start
  21.6 41.4 %all-reduce.6 = bf16[27904]{0:T(1024)(128)(2,1)S(1)} all-reduce(bf16[27904]{0:T(1024)(128)(2,1)S(1)} %dynamic-update-slice), channel_id=2, replica_groups=mesh['dp'=16,'seq'=2] {'dp','seq'}, use_global_device_ids=true, to_apply=%add.6 | all-reduce | flops 27904 | bytes 111616
  69.0 2.7 multiply_reduce_fusion
  72.3 4.7 maximum_convert_fusion
  77.0 5.0 multiply_convert_fusion
  82.0 47.7 %all-gather.7.cloned.1.call-done = bf16[2048,4096]{1,0:T(8,128)(2,1)} async-done(((bf16[64,4096]{1,0:T(8,128)(2,1)}), bf16[2048,4096]{1,0:T(8,128)(2,1)}) %all-gather.7.cloned.1.call-update) | async-done | bytes 16777232 | tf_op jit(solution)/shard_map/all_gather | solution.py:465
  129.8 23.5 %fusion.14.gate_ref = f32[1024,4096]{1,0:T(8,128)} fusion(bf16[2048,4096]{1,0:T(8,128)(2,1)} %all-gather.7.cloned.1.call-done, bf16[1040,2048]{1,0:T(8,128)(2,1)} %multiply_convert_fusion), kind=kOutput, calls=%fused_computation.47 | convolution fusion | flops 17179869184 | bytes 37748736 | tf_op jit(solution)/shard_map/dot_general | solution.py:485
  153.2 100.2 %all-gather.5.cloned.1.call-done = bf16[2048,4416]{1,0:T(8,128)(2,1)} async-done(((bf16[64,4416]{1,0:T(8,128)(2,1)}), bf16[2048,4416]{1,0:T(8,128)(2,1)}) %all-gather.5.cloned.1.call-update) | async-done | bytes 18087952 | tf_op jit(solution)/shard_map/all_gather | solution.py:464
  253.5 27.1 %fusion.40.pc_ref.front_ref.halo_ref = f32[1040,4416]{1,0:T(8,128)} fusion(bf16[1040,2048]{1,0:T(8,128)(2,1)} %multiply_convert_fusion, bf16[2048,4416]{1,0:T(8,128)(2,1)} %all-gather.5.cloned.1.call-done), kind=kOutput, calls=%fused_computation.167 | convolution fusion | flops 18811453440 | bytes 40718336 | tf_op jit(solution)/shard_map/dot_general | solution.py:483
  281.2 83.2 %scan_forward.1 = (f32[1024,4096]{1,0:T(8,128)}, bf16[1024,4352]{1,0:T(8,128)(2,1)}, bf16[1024,4096]{1,0:T(8,128)(2,1)}, f32[1024,256]{1,0:T(8,128)}, bf16[256,4096]{1,0:T(8,128)(2,1)}) custom-call(f32[1040,4416]{1,0:T(8,128)} %fusion.40.pc_ref.front_ref.halo_ref, f32[1040,4416]{1,0:T(8,128)} %fusion.40.pc_ref.front_ref.halo_ref, f32[1024,128]{1,0:T(8,128)} %pad.24.info_ref, ...), custom_call_target="tpu_custom_call" | custom-call | tf_op jit(solution)/shard_map/scan_forward/pallas_call | solution.py:516
  364.4 3.3 collective-permute-start.1
  369.6 23.6 %fusion.41.mg_ref = f32[1024,4096]{1,0:T(8,128)} fusion(bf16[1024,2048]{1,0:T(8,128)(2,1)} %bitcast.249, bf16[4096,2048]{1,0:T(8,128)(2,1)} %all-gather.9.cloned.1.call-done), kind=kOutput, calls=%fused_computation.168 | convolution fusion | flops 17179869184 | bytes 37748736 | tf_op jit(solution)/shard_map/dot_general | solution.py:487
  393.2 19.9 %collective-permute-done.1.sin_ref = bf16[256,4096]{1,0:T(8,128)(2,1)S(1)} collective-permute-done((bf16[256,4096]{1,0:T(8,128)(2,1)}, bf16[256,4096]{1,0:T(8,128)(2,1)S(1)}, u32[]{:S(2)}, u32[]{:S(2)}) %collective-permute-start.1) | collective-permute-done | bytes 2097184 | tf_op jit(solution)/shard_map/ppermute | solution.py:396
  414.5 88.6 %gate_both.1 = (bf16[1024,4096]{1,0:T(8,128)(2,1)}, bf16[1024,4096]{1,0:T(8,128)(2,1)}, bf16[1024,4096]{1,0:T(8,128)(2,1)}, f32[1024,64]{1,0:T(8,128)}, f32[256,4096]{1,0:T(8,128)}, /*index=5*/f32[8,4096]{1,0:T(8,128)}) custom-call(f32[1024,4096]{1,0:T(8,128)} %get-tuple-element.26.y_ref, bf16[1024,4352]{1,0:T(8,128)(2,1)} %get-tuple-element.27.act_ref, ...), custom_call_target="tpu_custom_call" | custom-call | tf_op jit(solution)/shard_map/gate_both/pallas_call | solution.py:550
  503.0 25.1 %convolution_convert_fusion.1 = bf16[4096,2048]{1,0:T(8,128)(2,1)} fusion(bf16[1024,4096]{1,0:T(8,128)(2,1)} %get-tuple-element.30, bf16[1024,2048]{1,0:T(8,128)(2,1)} %bitcast.250), kind=kOutput, calls=%fused_computation.1 | convolution fusion | flops 17188257792 | bytes 29360128 | tf_op jit(solution)/shard_map/dot_general | solution.py:38
  528.1 6.8 fusion.37
  534.9 6.1 constant_dynamic-slice_fusion.2
  541.0 5.0 copy.112
  546.0 2.6 copy.111
  553.7 25.4 %convolution_convert_fusion.2 = bf16[2048,4096]{1,0:T(8,128)(2,1)} fusion(bf16[1024,4096]{1,0:T(8,128)(2,1)} %get-tuple-element.31, bf16[1040,2048]{1,0:T(8,128)(2,1)} %multiply_convert_fusion), kind=kOutput, calls=%fused_computation.2 | convolution fusion | flops 17188257792 | bytes 29360128 | tf_op jit(solution)/shard_map/dot_general | solution.py:38
  579.1 6.6 fusion.38
  585.7 6.0 constant_dynamic-slice_fusion.6
  591.7 4.9 copy.114
  597.1 2.3 copy.113
  602.8 156.4 %scan_backward.1 = (bf16[1024,4416]{1,0:T(8,128)(2,1)}, f32[16,4352]{1,0:T(8,128)}, f32[8,4352]{1,0:T(8,128)}, f32[8,64]{1,0:T(8,128)}) custom-call(f32[1040,4416]{1,0:T(8,128)} %fusion.40.pc_ref.front_ref.halo_ref, f32[1040,4416]{1,0:T(8,128)} %fusion.40.pc_ref.front_ref.halo_ref, f32[1024,128]{1,0:T(8,128)} %pad.24.info_ref, ...), custom_call_target="tpu_custom_call" | custom-call | tf_op jit(solution)/shard_map/scan_backward/pallas_call | solution.py:599
  761.5 24.3 %add_convert_fusion.1 = bf16[1024,2048]{1,0:T(8,128)(2,1)} fusion(f32[1040,2048]{1,0:T(8,128)} %maximum_convert_fusion, bf16[1024,4096]{1,0:T(8,128)(2,1)} %get-tuple-element.30, bf16[4096,2048]{1,0:T(8,128)(2,1)} %all-gather.9.cloned.1.call-done), kind=kOutput, calls=%fused_computation.20 | convolution fusion | flops 17184063488 | bytes 37748736 | tf_op jit(solution)/shard_map/dot_general | solution.py:588
  787.2 92.1 %all-reduce.9.cloned.1.call-done = f32[21952]{0:T(1024)} async-done(((f32[21952]{0:T(1024)}), f32[21952]{0:T(1024)}) %all-reduce.9.cloned.1.call-update) | async-done | bytes 87824 | tf_op jit(solution)/shard_map/psum | solution.py:669
  884.6 26.1 %convolution_convert_fusion = bf16[2048,4416]{0,1:T(8,128)(2,1)} fusion(bf16[1024,4416]{1,0:T(8,128)(2,1)} %bitcast.273, bf16[1040,2048]{1,0:T(8,128)(2,1)} %multiply_convert_fusion), kind=kOutput, calls=%fused_computation | convolution fusion | flops 18531090432 | bytes 31457280 | tf_op jit(solution)/shard_map/dot_general | solution.py:38
  910.6 8.8 slice.163
  919.4 11.7 copy.79
  931.2 4.8 dynamic-slice_bitcast_fusion.1
  936.0 26.7 %fusion.42 = f32[1024,2048]{1,0:T(8,128)} fusion(bf16[1024,4416]{1,0:T(8,128)(2,1)} %bitcast.274, bf16[2048,4416]{1,0:T(8,128)(2,1)} %all-gather.5.cloned.1.call-done), kind=kOutput, calls=%fused_computation.169 | convolution fusion | flops 18522046464 | bytes 35520512 | tf_op jit(solution)/shard_map/dot_general | solution.py:655
  962.7 27.1 %multiply_reduce_fusion.1 = (f32[1024]{0:T(1024)S(1)}, f32[1024,2048]{1,0:T(8,128)}) fusion(f32[1040,2048]{1,0:T(8,128)} %maximum_convert_fusion, f32[1024]{0:T(1024)S(1)} %copy-done.27, f32[2048]{0:T(1024)S(1)} %copy-done.26, f32[1024,2048]{1,0:T(8,128)} %fusion.42, bf16[1024,4096]{1,0:T(8,128)(2,1)} %get-tuple-element.31, ...), kind=kOutput, calls=%fused_computation.18 | convolution fusion | flops 17190354944 | bytes 50348032 | tf_op jit(solution)/shard_map/dot_general | solution.py:653
  989.9 9.1 slice.164
  999.0 12.0 copy.80
  1011.0 5.1 dynamic-slice_bitcast_fusion
  1016.5 4.3 fusion.3
  1023.8 4.3 fusion.2
  1031.1 4.1 fusion.5
  1039.7 6.2 fusion.4
  1047.9 23.2 %collective-permute-done.25 = bf16[2,2,2,128,1024]{4,3,0,1,2:T(8,128)(2,1)} collective-permute-done((bf16[2,2,2,128,1024]{4,3,0,1,2:T(8,128)(2,1)}, bf16[2,2,2,128,1024]{4,3,0,1,2:T(8,128)(2,1)}, u32[]{:S(2)}, u32[]{:S(2)}) %collective-permute-start.25) | collective-permute-done | bytes 2097184 | tf_op jit(solution)/shard_map/ppermute | solution.py:426
  1072.6 6.1 add_convert_fusion
  1078.8 2.6 fusion.9
  1084.3 2.8 fusion.8
  1089.5 25.7 %collective-permute-done.5 = bf16[2,2,2,64,2048]{4,3,0,1,2:T(8,128)(2,1)} collective-permute-done((bf16[2,2,2,64,2048]{4,3,0,1,2:T(8,128)(2,1)}, bf16[2,2,2,64,2048]{4,3,0,1,2:T(8,128)(2,1)}, u32[]{:S(2)}, u32[]{:S(2)}) %collective-permute-start.5) | collective-permute-done | bytes 2097184 | tf_op jit(solution)/shard_map/ppermute | solution.py:426
  1116.7 2.5 fusion.11
  1120.3 3.0 collective-permute-done.10
  1128.1 6.5 fusion.1
  1137.5 3.8 fusion
  1141.5 4.4 collective-permute-done.26
  1149.0 3.9 collective-permute-start.27
  1154.5 13.8 %collective-permute-done.6 = bf16[2,2,64,2048]{3,2,0,1:T(8,128)(2,1)} collective-permute-done((bf16[2,2,64,2048]{3,2,0,1:T(8,128)(2,1)}, bf16[2,2,64,2048]{3,2,0,1:T(8,128)(2,1)}, u32[]{:S(2)}, u32[]{:S(2)}) %collective-permute-start.6) | collective-permute-done | bytes 1048608 | tf_op jit(solution)/shard_map/ppermute | solution.py:426
  1168.4 3.8 collective-permute-start.32
  1175.6 2.1 collective-permute-start.12
  1177.9 9.9 collective-permute-done.32
  1189.1 15.6 %collective-permute-done.7 = bf16[2,64,2048]{2,1,0:T(8,128)(2,1)S(1)} collective-permute-done((bf16[2,64,2048]{2,1,0:T(8,128)(2,1)S(1)}, bf16[2,64,2048]{2,1,0:T(8,128)(2,1)S(1)}, u32[]{:S(2)}, u32[]{:S(2)}) %collective-permute-start.7) | collective-permute-done | bytes 524320 | tf_op jit(solution)/shard_map/ppermute | solution.py:426
  1205.8 7.4 collective-permute-done.12
  1214.1 16.8 %collective-permute-done.8 = bf16[64,2048]{1,0:T(8,128)(2,1)S(1)} collective-permute-done((bf16[64,2048]{1,0:T(8,128)(2,1)S(1)}, bf16[64,2048]{1,0:T(8,128)(2,1)S(1)}, u32[]{:S(2)}, u32[]{:S(2)}) %collective-permute-start.8) | collective-permute-done | bytes 262176 | tf_op jit(solution)/shard_map/ppermute | solution.py:426
  1232.2 8.0 collective-permute-done.13
  1244.7 22.1 %collective-permute-done.16 = bf16[2,2,64,2176]{3,2,1,0:T(8,128)(2,1)S(1)} collective-permute-done((bf16[2,2,64,2176]{3,2,1,0:T(8,128)(2,1)S(1)}, bf16[2,2,64,2176]{3,2,1,0:T(8,128)(2,1)S(1)}, u32[]{:S(2)}, u32[]{:S(2)}) %collective-permute-start.16) | collective-permute-done | bytes 1114144 | tf_op jit(solution)/shard_map/ppermute | solution.py:426
  1267.2 3.4 collective-permute-done.21
  1271.0 14.8 %collective-permute-done.17 = bf16[2,64,2176]{2,1,0:T(8,128)(2,1)S(1)} collective-permute-done((bf16[2,64,2176]{2,1,0:T(8,128)(2,1)S(1)}, bf16[2,64,2176]{2,1,0:T(8,128)(2,1)S(1)}, u32[]{:S(2)}, u32[]{:S(2)}) %collective-permute-start.17) | collective-permute-done | bytes 557088 | tf_op jit(solution)/shard_map/ppermute | solution.py:426
  1286.4 12.3 collective-permute-done.22
  1299.1 12.2 collective-permute-done.23
  (264 shorter events, 89.4 us)
Async XLA Ops:
  7.2 58.5 %copy-start.34 = (f32[64]{0:T(128)S(1)}, f32[64]{0:T(128)}, u32[]{:S(2)}) copy-start(f32[64]{0:T(128)} %param.21) | copy-start | bytes 772
  7.2 61.2 %copy-start.30 = (f32[64]{0:T(128)S(1)}, f32[64]{0:T(128)}, u32[]{:S(2)}) copy-start(f32[64]{0:T(128)} %param.22) | copy-start | bytes 772
  7.2 61.2 %copy-start.31 = (f32[64]{0:T(128)S(1)}, f32[64]{0:T(128)}, u32[]{:S(2)}) copy-start(f32[64]{0:T(128)} %param.20) | copy-start | bytes 772
  7.2 122.5 %all-gather.7.cloned.1.call-start = ((), (), s32[]{:S(2)}) async-start(), calls=%async_computation.1 | async-start | bytes 17301504 | tf_op jit(solution)/shard_map/all_gather | solution.py:465
  9.1 244.3 %all-gather.5.cloned.1.call-start = ((), (), s32[]{:S(2)}) async-start(), calls=%async_computation | async-start | bytes 18923520 | tf_op jit(solution)/shard_map/all_gather | solution.py:464
  11.1 358.4 %all-gather.9.cloned.1.call-start = ((), (), s32[]{:S(2)}) async-start(), calls=%async_computation.2 | async-start | bytes 17301504 | tf_op jit(solution)/shard_map/all_gather | solution.py:466
  11.9 867.4 %all-reduce.9.cloned.1.call-start = ((), (), s32[]{:S(2)}) async-start(), calls=%async_computation.3 | async-start | bytes 180224 | tf_op jit(solution)/shard_map/psum | solution.py:669
  14.0 49.5 %copy-start.28 = (pred[2,8]{1,0:T(4,128)(4,1)}, pred[2,8]{1,0:T(4,128)(4,1)S(1)}, u32[]{:S(2)}) copy-start(pred[2,8]{1,0:T(4,128)(4,1)S(1)} %slice_compare_fusion) | copy-start | bytes 52
  14.9 54.1 %collective-permute-start = (bf16[2,8,2048]{2,1,0:T(8,128)(2,1)S(1)}, bf16[2,8,2048]{2,1,0:T(8,128)(2,1)S(1)}, u32[]{:S(2)}, u32[]{:S(2)}) collective-permute-start(bf16[2,8,2048]{2,1,0:T(8,128)(2,1)S(1)} %slice_select_fusion), channel_id=1, source_target_pairs={{0,1},{2,3},{4,5},{6,7},{8,9},{10,11},{12,13},{14,15},{16,17},{18,... | collective-permute-start | bytes 196616 | tf_op jit(solution)/shard_map/ppermute | solution.py:396
  64.4 12.6 copy-start.25
  364.4 48.8 %collective-permute-start.1 = (bf16[256,4096]{1,0:T(8,128)(2,1)}, bf16[256,4096]{1,0:T(8,128)(2,1)S(1)}, u32[]{:S(2)}, u32[]{:S(2)}) collective-permute-start(bf16[256,4096]{1,0:T(8,128)(2,1)} %get-tuple-element.29), channel_id=1, source_target_pairs={{0,1},{2,3},{4,5},{6,7},{8,9},{10,11},{12,13},{14,15},{16,17},{18,... | collective-permute-start | bytes 6291464 | tf_op jit(solution)/shard_map/ppermute | solution.py:396
  546.0 470.0 %collective-permute-start.24 = (bf16[2,2,2,2,128,1024]{5,4,0,1,2,3:T(8,128)(2,1)}, bf16[2,2,2,2,128,1024]{5,4,0,1,2,3:T(8,128)(2,1)}, u32[]{:S(2)}, u32[]{:S(2)}) collective-permute-start(bf16[2,2,2,2,128,1024]{5,4,0,1,2,3:T(8,128)(2,1)} %bitcast.222), channel_id=1, source_target_pairs={{0,2},{2,0},{4,6},{6,4},{8,10},{10,8},{12,14},{14,12},{16,18},{18,... | collective-permute-start | bytes 12582920 | tf_op jit(solution)/shard_map/ppermute | solution.py:426
  548.6 473.7 %collective-permute-start.29 = (bf16[2,2,2,2,128,1024]{5,4,0,1,3,2:T(8,128)(2,1)}, bf16[2,2,2,2,128,1024]{5,4,0,1,3,2:T(8,128)(2,1)}, u32[]{:S(2)}, u32[]{:S(2)}) collective-permute-start(bf16[2,2,2,2,128,1024]{5,4,0,1,3,2:T(8,128)(2,1)} %bitcast.221), channel_id=1, source_target_pairs={{0,2},{2,0},{4,6},{6,4},{8,10},{10,8},{12,14},{14,12},{16,18},{18,... | collective-permute-start | bytes 12582920 | tf_op jit(solution)/shard_map/ppermute | solution.py:426
  551.3 50.2 %collective-permute-start.2 = (bf16[256,4096]{1,0:T(8,128)(2,1)}, bf16[256,4096]{1,0:T(8,128)(2,1)S(1)}, u32[]{:S(2)}, u32[]{:S(2)}) collective-permute-start(bf16[256,4096]{1,0:T(8,128)(2,1)} %convert_element_type.550), channel_id=1, source_target_pairs={{1,0},{3,2},{5,4},{7,6},{9,8},{11,10},{13,12},{15,14},{17,16},{19,... | collective-permute-start | bytes 6291464 | tf_op jit(solution)/shard_map/ppermute | solution.py:396
  596.6 433.1 %collective-permute-start.4 = (bf16[2,2,2,2,64,2048]{5,4,0,1,2,3:T(8,128)(2,1)}, bf16[2,2,2,2,64,2048]{5,4,0,1,2,3:T(8,128)(2,1)}, u32[]{:S(2)}, u32[]{:S(2)}) collective-permute-start(bf16[2,2,2,2,64,2048]{5,4,0,1,2,3:T(8,128)(2,1)} %bitcast.224), channel_id=1, source_target_pairs={{0,2},{2,0},{4,6},{6,4},{8,10},{10,8},{12,14},{14,12},{16,18},{18,... | collective-permute-start | bytes 12582920 | tf_op jit(solution)/shard_map/ppermute | solution.py:426
  599.4 437.2 %collective-permute-start.9 = (bf16[2,2,2,2,64,2048]{5,4,0,1,3,2:T(8,128)(2,1)}, bf16[2,2,2,2,64,2048]{5,4,0,1,3,2:T(8,128)(2,1)}, u32[]{:S(2)}, u32[]{:S(2)}) collective-permute-start(bf16[2,2,2,2,64,2048]{5,4,0,1,3,2:T(8,128)(2,1)} %bitcast.223), channel_id=1, source_target_pairs={{0,2},{2,0},{4,6},{6,4},{8,10},{10,8},{12,14},{14,12},{16,18},{18,... | collective-permute-start | bytes 12582920 | tf_op jit(solution)/shard_map/ppermute | solution.py:426
  761.5 24.4 %copy-start.24 = (f32[16,4352]{1,0:T(8,128)S(1)}, f32[16,4352]{1,0:T(8,128)}, u32[]{:S(2)}) copy-start(f32[16,4352]{1,0:T(8,128)} %get-tuple-element.37) | copy-start | bytes 835588
  761.5 121.4 %copy-start.29 = (pred[2,8]{1,0:T(4,128)(4,1)S(1)}, pred[2,8]{1,0:T(4,128)(4,1)}, u32[]{:S(2)}) copy-start(pred[2,8]{1,0:T(4,128)(4,1)} %copy-done.28) | copy-start | bytes 52
  785.9 97.0 %collective-permute-start.3 = (bf16[16,4352]{1,0:T(8,128)(2,1)S(1)}, bf16[16,4352]{1,0:T(8,128)(2,1)S(1)}, u32[]{:S(2)}, u32[]{:S(2)}) collective-permute-start(bf16[16,4352]{1,0:T(8,128)(2,1)S(1)} %convert_element_type.552), channel_id=1, source_target_pairs={{1,0},{3,2},{5,4},{7,6},{9,8},{11,10},{13,12},{15,14},{17,16},{19,... | collective-permute-start | bytes 417800 | tf_op jit(solution)/shard_map/ppermute | solution.py:396
  935.9 26.8 %copy-start.26 = (f32[2048]{0:T(1024)S(1)}, f32[2048]{0:T(1024)}, u32[]{:S(2)}) copy-start(f32[2048]{0:T(1024)} %copy-done.25) | copy-start | bytes 24580
  935.9 26.8 %copy-start.27 = (f32[1024]{0:T(1024)S(1)}, f32[1024]{0:T(1024)}, u32[]{:S(2)}) copy-start(f32[1024]{0:T(1024)} %slice.159) | copy-start | bytes 12292
  935.9 191.2 %collective-permute-start.14 = (bf16[2,2,2,2,64,2176]{5,4,3,2,1,0:T(8,128)(2,1)}, bf16[2,2,2,2,64,2176]{5,4,3,2,1,0:T(8,128)(2,1)}, u32[]{:S(2)}, u32[]{:S(2)}) collective-permute-start(bf16[2,2,2,2,64,2176]{5,4,3,2,1,0:T(8,128)(2,1)} %dynamic-slice_bitcast_fusion.1), channel_id=1, source_target_pairs={{0,2},{2,0},{4,6},{6,4},{8,10},{10,8},{12,14},{14,12},{16,18},{18,... | collective-permute-start | bytes 13369352 | tf_op jit(solution)/shard_map/ppermute | solution.py:426
  1016.0 120.3 %collective-permute-start.19 = (bf16[2,2,2,2,64,2240]{5,4,3,2,1,0:T(8,128)(2,1)}, bf16[2,2,2,2,64,2240]{5,4,3,2,1,0:T(8,128)(2,1)}, u32[]{:S(2)}, u32[]{:S(2)}) collective-permute-start(bf16[2,2,2,2,64,2240]{5,4,3,2,1,0:T(8,128)(2,1)} %dynamic-slice_bitcast_fusion), channel_id=1, source_target_pairs={{0,2},{2,0},{4,6},{6,4},{8,10},{10,8},{12,14},{14,12},{16,18},{18,... | collective-permute-start | bytes 13762568 | tf_op jit(solution)/shard_map/ppermute | solution.py:426
  1022.3 48.8 %collective-permute-start.25 = (bf16[2,2,2,128,1024]{4,3,0,1,2:T(8,128)(2,1)}, bf16[2,2,2,128,1024]{4,3,0,1,2:T(8,128)(2,1)}, u32[]{:S(2)}, u32[]{:S(2)}) collective-permute-start(bf16[2,2,2,128,1024]{4,3,0,1,2:T(8,128)(2,1)} %dynamic-slice_bitcast_fusion.5), channel_id=1, source_target_pairs={{0,1},{1,0},{2,3},{3,2},{4,5},{5,4},{6,7},{7,6},{8,9},{9,8},{10,11... | collective-permute-start | bytes 6291464 | tf_op jit(solution)/shard_map/ppermute | solution.py:426
  1029.7 54.1 %collective-permute-start.30 = (bf16[2,2,2,128,1024]{4,3,0,1,2:T(8,128)(2,1)}, bf16[2,2,2,128,1024]{4,3,0,1,2:T(8,128)(2,1)}, u32[]{:S(2)}, u32[]{:S(2)}) collective-permute-start(bf16[2,2,2,128,1024]{4,3,0,1,2:T(8,128)(2,1)} %dynamic-slice_bitcast_fusion.4), channel_id=1, source_target_pairs={{0,4},{2,6},{4,0},{6,2},{8,12},{10,14},{12,8},{14,10},{16,20},{18,... | collective-permute-start | bytes 6291464 | tf_op jit(solution)/shard_map/ppermute | solution.py:426
  1038.3 76.9 %collective-permute-start.5 = (bf16[2,2,2,64,2048]{4,3,0,1,2:T(8,128)(2,1)}, bf16[2,2,2,64,2048]{4,3,0,1,2:T(8,128)(2,1)}, u32[]{:S(2)}, u32[]{:S(2)}) collective-permute-start(bf16[2,2,2,64,2048]{4,3,0,1,2:T(8,128)(2,1)} %dynamic-slice_bitcast_fusion.7), channel_id=1, source_target_pairs={{0,1},{1,0},{2,3},{3,2},{4,5},{5,4},{6,7},{7,6},{8,9},{9,8},{10,11... | collective-permute-start | bytes 6291464 | tf_op jit(solution)/shard_map/ppermute | solution.py:426
  1039.7 32.9 %slice-start.6 = ((s8[8519680]{0:T(1024)(128)(4,1)}), s8[4194304]{0:T(1024)(128)(4,1)S(1)}, s32[]{:S(2)}) async-start(s8[8519680]{0:T(1024)(128)(4,1)} %bitcast.241), calls=%async_computation.10 | async-start | bytes 8388608
  1039.7 32.9 %slice-start.7 = ((s8[8519680]{0:T(1024)(128)(4,1)}), s8[4194304]{0:T(1024)(128)(4,1)S(1)}, s32[]{:S(2)}) async-start(s8[8519680]{0:T(1024)(128)(4,1)} %bitcast.241), calls=%async_computation.11 | async-start | bytes 8388608
  1039.7 32.9 %slice-start.8 = ((s8[8519680]{0:T(1024)(128)(4,1)}), s8[131072]{0:T(1024)(128)(4,1)S(1)}, s32[]{:S(2)}) async-start(s8[8519680]{0:T(1024)(128)(4,1)} %bitcast.241), calls=%async_computation.12 | async-start | bytes 262144
  1045.9 26.7 %copy-start.21 = (bf16[2,512,2048]{2,1,0:T(8,128)(2,1)S(1)}, bf16[2,512,2048]{2,1,0:T(8,128)(2,1)}, u32[]{:S(2)}) copy-start(bf16[2,512,2048]{2,1,0:T(8,128)(2,1)} %param.23) | copy-start | bytes 12582916
  1071.1 52.2 %collective-permute-start.10 = (bf16[2,2,2,64,2048]{4,3,0,1,2:T(8,128)(2,1)S(1)}, bf16[2,2,2,64,2048]{4,3,0,1,2:T(8,128)(2,1)S(1)}, u32[]{:S(2)}, u32[]{:S(2)}) collective-permute-start(bf16[2,2,2,64,2048]{4,3,0,1,2:T(8,128)(2,1)S(1)} %dynamic-slice_bitcast_fusion.6), channel_id=1, source_target_pairs={{0,4},{2,6},{4,0},{6,2},{8,12},{10,14},{12,8},{14,10},{16,20},{18,... | collective-permute-start | bytes 6291464 | tf_op jit(solution)/shard_map/ppermute | solution.py:426
  1083.7 32.9 %copy-start.6 = (bf16[2,2,2,2,64,2048]{5,4,0,1,2,3:T(8,128)(2,1)S(1)}, bf16[2,2,2,2,64,2048]{5,4,0,1,2,3:T(8,128)(2,1)}, u32[]{:S(2)}) copy-start(bf16[2,2,2,2,64,2048]{5,4,0,1,2,3:T(8,128)(2,1)} %copy-done.5) | copy-start | bytes 12582916
  1083.8 62.1 %collective-permute-start.26 = (bf16[2,2,128,1024]{3,2,0,1:T(8,128)(2,1)}, bf16[2,2,128,1024]{3,2,0,1:T(8,128)(2,1)}, u32[]{:S(2)}, u32[]{:S(2)}) collective-permute-start(bf16[2,2,128,1024]{3,2,0,1:T(8,128)(2,1)} %dynamic-slice_bitcast_fusion.11), channel_id=1, source_target_pairs={{0,4},{2,6},{4,0},{6,2},{8,12},{10,14},{12,8},{14,10},{16,20},{18,... | collective-permute-start | bytes 3145736 | tf_op jit(solution)/shard_map/ppermute | solution.py:426
  1089.5 35.2 %copy-start.7 = (bf16[2,2,2,2,64,2048]{5,4,0,1,3,2:T(8,128)(2,1)S(1)}, bf16[2,2,2,2,64,2048]{5,4,0,1,3,2:T(8,128)(2,1)}, u32[]{:S(2)}) copy-start(bf16[2,2,2,2,64,2048]{5,4,0,1,3,2:T(8,128)(2,1)} %fusion.4) | copy-start | bytes 12582916
  1115.2 33.8 %collective-permute-start.31 = (bf16[2,2,128,1024]{3,2,0,1:T(8,128)(2,1)}, bf16[2,2,128,1024]{3,2,0,1:T(8,128)(2,1)}, u32[]{:S(2)}, u32[]{:S(2)}) collective-permute-start(bf16[2,2,128,1024]{3,2,0,1:T(8,128)(2,1)} %dynamic-slice_bitcast_fusion.10), channel_id=1, source_target_pairs={{0,1},{1,0},{2,3},{3,2},{4,5},{5,4},{6,7},{7,6},{8,9},{9,8},{10,11... | collective-permute-start | bytes 3145736 | tf_op jit(solution)/shard_map/ppermute | solution.py:426
  1116.7 11.4 slice-start.3
  1116.7 11.4 slice-start.4
  1123.3 45.0 %collective-permute-start.6 = (bf16[2,2,64,2048]{3,2,0,1:T(8,128)(2,1)}, bf16[2,2,64,2048]{3,2,0,1:T(8,128)(2,1)}, u32[]{:S(2)}, u32[]{:S(2)}) collective-permute-start(bf16[2,2,64,2048]{3,2,0,1:T(8,128)(2,1)} %dynamic-slice_bitcast_fusion.13), channel_id=1, source_target_pairs={{0,4},{2,6},{4,0},{6,2},{8,12},{10,14},{12,8},{14,10},{16,20},{18,... | collective-permute-start | bytes 3145736 | tf_op jit(solution)/shard_map/ppermute | solution.py:426
  1125.5 12.0 slice-start
  1127.2 46.7 %collective-permute-start.11 = (bf16[2,2,64,2048]{3,2,0,1:T(8,128)(2,1)}, bf16[2,2,64,2048]{3,2,0,1:T(8,128)(2,1)}, u32[]{:S(2)}, u32[]{:S(2)}) collective-permute-start(bf16[2,2,64,2048]{3,2,0,1:T(8,128)(2,1)} %dynamic-slice_bitcast_fusion.12), channel_id=1, source_target_pairs={{0,1},{1,0},{2,3},{3,2},{4,5},{5,4},{6,7},{7,6},{8,9},{9,8},{10,11... | collective-permute-start | bytes 3145736 | tf_op jit(solution)/shard_map/ppermute | solution.py:426
  1136.3 103.9 %collective-permute-start.15 = (bf16[2,2,2,64,2176]{4,3,2,1,0:T(8,128)(2,1)S(1)}, bf16[2,2,2,64,2176]{4,3,2,1,0:T(8,128)(2,1)S(1)}, u32[]{:S(2)}, u32[]{:S(2)}) collective-permute-start(bf16[2,2,2,64,2176]{4,3,2,1,0:T(8,128)(2,1)S(1)} %dynamic-slice_bitcast_fusion.3), channel_id=1, source_target_pairs={{0,1},{1,0},{2,3},{3,2},{4,5},{5,4},{6,7},{7,6},{8,9},{9,8},{10,11... | collective-permute-start | bytes 6684680 | tf_op jit(solution)/shard_map/ppermute | solution.py:426
  1141.3 11.5 copy-start.14
  1141.5 30.6 %copy-start.16 = (bf16[2,2,2,64,2048]{4,3,0,1,2:T(8,128)(2,1)S(1)}, bf16[2,2,2,64,2048]{4,3,0,1,2:T(8,128)(2,1)}, u32[]{:S(2)}) copy-start(bf16[2,2,2,64,2048]{4,3,0,1,2:T(8,128)(2,1)} %copy-done.15) | copy-start | bytes 6291460
  1145.9 96.8 %collective-permute-start.20 = (bf16[2,2,2,64,2240]{4,3,2,1,0:T(8,128)(2,1)S(1)}, bf16[2,2,2,64,2240]{4,3,2,1,0:T(8,128)(2,1)S(1)}, u32[]{:S(2)}, u32[]{:S(2)}) collective-permute-start(bf16[2,2,2,64,2240]{4,3,2,1,0:T(8,128)(2,1)S(1)} %dynamic-slice_bitcast_fusion.2), channel_id=1, source_target_pairs={{0,4},{2,6},{4,0},{6,2},{8,12},{10,14},{12,8},{14,10},{16,20},{18,... | collective-permute-start | bytes 6881288 | tf_op jit(solution)/shard_map/ppermute | solution.py:426
  1148.9 25.0 %copy-start.18 = (bf16[2,2,2,64,2048]{4,3,0,1,2:T(8,128)(2,1)S(1)}, bf16[2,2,2,64,2048]{4,3,0,1,2:T(8,128)(2,1)}, u32[]{:S(2)}) copy-start(bf16[2,2,2,64,2048]{4,3,0,1,2:T(8,128)(2,1)} %copy-done.17) | copy-start | bytes 6291460
  1149.0 26.6 %collective-permute-start.27 = (bf16[2,128,1024]{2,1,0:T(8,128)(2,1)S(1)}, bf16[2,128,1024]{2,1,0:T(8,128)(2,1)S(1)}, u32[]{:S(2)}, u32[]{:S(2)}) collective-permute-start(bf16[2,128,1024]{2,1,0:T(8,128)(2,1)S(1)} %dynamic-slice_bitcast_fusion.17), channel_id=1, source_target_pairs={{0,8},{2,10},{4,12},{6,14},{8,0},{10,2},{12,4},{14,6},{16,24},{18,... | collective-permute-start | bytes 1572872 | tf_op jit(solution)/shard_map/ppermute | solution.py:426
  1168.4 19.4 %collective-permute-start.32 = (bf16[2,128,1024]{2,1,0:T(8,128)(2,1)S(1)}, bf16[2,128,1024]{2,1,0:T(8,128)(2,1)S(1)}, u32[]{:S(2)}, u32[]{:S(2)}) collective-permute-start(bf16[2,128,1024]{2,1,0:T(8,128)(2,1)S(1)} %dynamic-slice_bitcast_fusion.16), channel_id=1, source_target_pairs={{0,8},{2,10},{4,12},{6,14},{8,0},{10,2},{12,4},{14,6},{16,24},{18,... | collective-permute-start | bytes 1572872 | tf_op jit(solution)/shard_map/ppermute | solution.py:426
  1173.8 30.8 %collective-permute-start.7 = (bf16[2,64,2048]{2,1,0:T(8,128)(2,1)S(1)}, bf16[2,64,2048]{2,1,0:T(8,128)(2,1)S(1)}, u32[]{:S(2)}, u32[]{:S(2)}) collective-permute-start(bf16[2,64,2048]{2,1,0:T(8,128)(2,1)S(1)} %dynamic-slice_bitcast_fusion.19), channel_id=1, source_target_pairs={{0,8},{2,10},{4,12},{6,14},{8,0},{10,2},{12,4},{14,6},{16,24},{18,... | collective-permute-start | bytes 1572872 | tf_op jit(solution)/shard_map/ppermute | solution.py:426
  1175.6 37.6 %collective-permute-start.12 = (bf16[2,64,2048]{2,1,0:T(8,128)(2,1)S(1)}, bf16[2,64,2048]{2,1,0:T(8,128)(2,1)S(1)}, u32[]{:S(2)}, u32[]{:S(2)}) collective-permute-start(bf16[2,64,2048]{2,1,0:T(8,128)(2,1)S(1)} %dynamic-slice_bitcast_fusion.18), channel_id=1, source_target_pairs={{0,8},{2,10},{4,12},{6,14},{8,0},{10,2},{12,4},{14,6},{16,24},{18,... | collective-permute-start | bytes 1572872 | tf_op jit(solution)/shard_map/ppermute | solution.py:426
  1177.7 62.6 %slice-start.9 = ((s8[4456448]{0:T(1024)(128)(4,1)}), s8[4194304]{0:T(1024)(128)(4,1)S(1)}, s32[]{:S(2)}) async-start(s8[4456448]{0:T(1024)(128)(4,1)} %bitcast.247), calls=%async_computation.13 | async-start | bytes 8388608
  1187.8 43.1 %collective-permute-start.28 = (bf16[128,1024]{1,0:T(8,128)(2,1)S(1)}, bf16[128,1024]{1,0:T(8,128)(2,1)S(1)}, u32[]{:S(2)}, u32[]{:S(2)}) collective-permute-start(bf16[128,1024]{1,0:T(8,128)(2,1)S(1)} %dynamic-slice_bitcast_fusion.23), channel_id=1, source_target_pairs={{0,16},{2,18},{4,20},{6,22},{8,24},{10,26},{12,28},{14,30},{16,0},... | collective-permute-start | bytes 786440 | tf_op jit(solution)/shard_map/ppermute | solution.py:426
  1189.0 42.1 %copy-start.23 = (bf16[128,2048]{1,0:T(8,128)(2,1)S(1)}, bf16[128,2048]{1,0:T(8,128)(2,1)}, u32[]{:S(2)}) copy-start(bf16[128,2048]{1,0:T(8,128)(2,1)} %param.16) | copy-start | bytes 1572868
  1204.7 26.4 %collective-permute-start.33 = (bf16[128,1024]{1,0:T(8,128)(2,1)S(1)}, bf16[128,1024]{1,0:T(8,128)(2,1)S(1)}, u32[]{:S(2)}, u32[]{:S(2)}) collective-permute-start(bf16[128,1024]{1,0:T(8,128)(2,1)S(1)} %dynamic-slice_bitcast_fusion.22), channel_id=1, source_target_pairs={{0,16},{2,18},{4,20},{6,22},{8,24},{10,26},{12,28},{14,30},{16,0},... | collective-permute-start | bytes 786440 | tf_op jit(solution)/shard_map/ppermute | solution.py:426
  1205.8 34.4 %slice-start.10 = ((s8[4456448]{0:T(1024)(128)(4,1)}), s8[262144]{0:T(1024)(128)(4,1)S(1)}, s32[]{:S(2)}) async-start(s8[4456448]{0:T(1024)(128)(4,1)} %bitcast.247), calls=%async_computation.14 | async-start | bytes 524288
  1213.3 17.6 %collective-permute-start.8 = (bf16[64,2048]{1,0:T(8,128)(2,1)S(1)}, bf16[64,2048]{1,0:T(8,128)(2,1)S(1)}, u32[]{:S(2)}, u32[]{:S(2)}) collective-permute-start(bf16[64,2048]{1,0:T(8,128)(2,1)S(1)} %dynamic-slice_bitcast_fusion.25), channel_id=1, source_target_pairs={{0,16},{2,18},{4,20},{6,22},{8,24},{10,26},{12,28},{14,30},{16,0},... | collective-permute-start | bytes 786440 | tf_op jit(solution)/shard_map/ppermute | solution.py:426
  1230.9 9.3 collective-permute-start.13
  1241.0 25.8 %collective-permute-start.16 = (bf16[2,2,64,2176]{3,2,1,0:T(8,128)(2,1)S(1)}, bf16[2,2,64,2176]{3,2,1,0:T(8,128)(2,1)S(1)}, u32[]{:S(2)}, u32[]{:S(2)}) collective-permute-start(bf16[2,2,64,2176]{3,2,1,0:T(8,128)(2,1)S(1)} %dynamic-slice_bitcast_fusion.9), channel_id=1, source_target_pairs={{0,4},{2,6},{4,0},{6,2},{8,12},{10,14},{12,8},{14,10},{16,20},{18,... | collective-permute-start | bytes 3342344 | tf_op jit(solution)/shard_map/ppermute | solution.py:426
  1243.6 26.9 %collective-permute-start.21 = (bf16[2,2,64,2240]{3,2,1,0:T(8,128)(2,1)S(1)}, bf16[2,2,64,2240]{3,2,1,0:T(8,128)(2,1)S(1)}, u32[]{:S(2)}, u32[]{:S(2)}) collective-permute-start(bf16[2,2,64,2240]{3,2,1,0:T(8,128)(2,1)S(1)} %dynamic-slice_bitcast_fusion.8), channel_id=1, source_target_pairs={{0,1},{1,0},{2,3},{3,2},{4,5},{5,4},{6,7},{7,6},{8,9},{9,8},{10,11... | collective-permute-start | bytes 3440648 | tf_op jit(solution)/shard_map/ppermute | solution.py:426
  1267.1 18.6 %collective-permute-start.17 = (bf16[2,64,2176]{2,1,0:T(8,128)(2,1)S(1)}, bf16[2,64,2176]{2,1,0:T(8,128)(2,1)S(1)}, u32[]{:S(2)}, u32[]{:S(2)}) collective-permute-start(bf16[2,64,2176]{2,1,0:T(8,128)(2,1)S(1)} %dynamic-slice_bitcast_fusion.15), channel_id=1, source_target_pairs={{0,8},{2,10},{4,12},{6,14},{8,0},{10,2},{12,4},{14,6},{16,24},{18,... | collective-permute-start | bytes 1671176 | tf_op jit(solution)/shard_map/ppermute | solution.py:426
  1270.9 40.5 %copy-start.19 = (bf16[64,8512]{1,0:T(8,128)(2,1)S(1)}, bf16[64,8512]{1,0:T(8,128)(2,1)}, u32[]{:S(2)}) copy-start(bf16[64,8512]{1,0:T(8,128)(2,1)} %param.14) | copy-start | bytes 3268612
  1270.9 27.8 %collective-permute-start.22 = (bf16[2,64,2240]{2,1,0:T(8,128)(2,1)S(1)}, bf16[2,64,2240]{2,1,0:T(8,128)(2,1)S(1)}, u32[]{:S(2)}, u32[]{:S(2)}) collective-permute-start(bf16[2,64,2240]{2,1,0:T(8,128)(2,1)S(1)} %dynamic-slice_bitcast_fusion.14), channel_id=1, source_target_pairs={{0,8},{2,10},{4,12},{6,14},{8,0},{10,2},{12,4},{14,6},{16,24},{18,... | collective-permute-start | bytes 1720328 | tf_op jit(solution)/shard_map/ppermute | solution.py:426
  1285.9 13.1 collective-permute-start.18
  1298.9 14.2 %copy-start.33 = (bf16[64]{0:T(256)(128)(2,1)S(1)}, bf16[64]{0:T(256)(128)(2,1)}, u32[]{:S(2)}) copy-start(bf16[64]{0:T(256)(128)(2,1)} %param.15) | copy-start | bytes 388
  1298.9 12.3 collective-permute-start.23
  (20 other events, 90.8 us)
Sparse Core Ops, SparseCore 0:
  11.6 118.0 all-gather.6
  133.2 120.2 all-gather.4
  256.5 113.0 all-gather.8
  761.6 117.6 all-reduce.8

commit v2 on v1

--- a/solution.py
+++ b/solution.py
@@ -14,7 +14,8 @@
 DI = 4096
 XBC = 4352
 PROJ = 8512
-CD = XBC + H
+CD = 4608
+PIECE = 256
 Q = 128
 LB = 256
 EPS = 1e-05
@@ -123,7 +124,7 @@
         out, _ = conv_block(ext, cw_ref, taps, at)
         act_ref[:, at] = (out * sigmoid(out)).astype(BF)
 
-    z = pc_ref[:, XBC:CD] + hp_ref[0:1, :]
+    z = pc_ref[:, XBC : XBC + H] + hp_ref[0:1, :]
     dt = softplus(z)
     decay = -dt * hp_ref[1:2, :]
     rows, cols = grid_iota((Q, Q), 0), grid_iota((Q, Q), 1)
@@ -361,7 +362,8 @@
     dt = softplus(z)
     sig = sigmoid(z)
     dz = rfull * (sig / jnp.maximum(dt, 1e-37)) - rate * dec * sig
-    dproj_ref[:, XBC:CD] = dz.astype(BF)
+    dproj_ref[:, XBC : XBC + H] = dz.astype(BF)
+    dproj_ref[:, XBC + H : CD] = jnp.zeros((Q, CD - XBC - H), BF)
     hg_ref[0:1, :] += jnp.sum(dz, axis=0, keepdims=True)
     hg_ref[1:2, :] += jnp.sum(-dec * dt * rate, axis=0, keepdims=True)
 
@@ -404,6 +406,299 @@
         total = wide * entering.reshape(seqs, N, DI).astype(F32) + local.reshape(seqs, N, DI).astype(F32)
         entering = shift_along(total.reshape(seqs * N, DI).astype(BF), distance)
     return entering
+
+
+def place_bits():
+    dp_bits = lax.axis_size("dp").bit_length() - 1
+    seq_bits = lax.axis_size("seq").bit_length() - 1
+    return [("dp", b) for b in reversed(range(dp_bits))] + [("seq", b) for b in reversed(range(seq_bits))]
+
+
+def bit_of(dim):
+    axis, bit = place_bits()[dim]
+    return (lax.axis_index(axis) // (1 << bit)) % 2
+
+
+def partner(dim):
+    axis, bit = place_bits()[dim]
+    return {axis: lax.axis_index(axis) + (1 - 2 * bit_of(dim)) * (1 << bit)}
+
+
+def halving_orders():
+    names = place_bits()
+    seq_dims = [names.index(("seq", b)) for b in range(lax.axis_size("seq").bit_length() - 1)]
+    dp_dims = [names.index(("dp", b)) for b in range(lax.axis_size("dp").bit_length() - 1)]
+    return (
+        [dp_dims[0]] + seq_dims + dp_dims[1:],
+        dp_dims[:2] + seq_dims + dp_dims[2:],
+    )
+
+
+def greet():
+    barrier = pltpu.get_barrier_semaphore()
+    dims = len(place_bits())
+    for dim in range(dims):
+        pl.semaphore_signal(barrier, inc=1, device_id=partner(dim), device_id_type=pl.DeviceIdType.MESH)
+    pl.semaphore_wait(barrier, dims)
+
+
+def remote(src, dst, send, recv, dim):
+    return pltpu.make_async_remote_copy(
+        src_ref=src, dst_ref=dst, send_sem=send, recv_sem=recv,
+        device_id=partner(dim), device_id_type=pl.DeviceIdType.MESH,
+    )
+
+
+def gather_kernel(pieces, own_a, own_b, full_a, full_b, local, send, recv):
+    dims = len(place_bits())
+    orders = [list(reversed(order)) for order in halving_orders()]
+    own, full = (own_a, own_b), (full_a, full_b)
+    mine = tuple(bit_of(dim) for dim in range(dims))
+    greet()
+    locals_ = [pltpu.make_async_copy(own[j], full[j].at[mine], local.at[j]) for j in range(2)]
+    for copy in locals_:
+        copy.start()
+
+    def step(number, stage):
+        which, start, size, order = pieces[number]
+        dim = orders[order][stage]
+        done = orders[order][:stage]
+        at = tuple(slice(None) if d in done else mine[d] for d in range(dims))
+        at = at + (slice(None), pl.ds(start, size))
+        src = own[which].at[:, pl.ds(start, size)] if stage == 0 else full[which].at[at]
+        return remote(src, full[which].at[at], send.at[number, stage], recv.at[number, stage], dim)
+
+    count = len(pieces)
+    groups = (count + 1) // 2
+    for wave in range(groups + dims):
+        for stage in reversed(range(dims + 1)):
+            group = wave - stage
+            if not 0 <= group < groups:
+                continue
+            if stage == 1 and group == 0:
+                for copy in locals_:
+                    copy.wait()
+            for number in (2 * group, 2 * group + 1):
+                if number >= count:
+                    continue
+                if stage > 0:
+                    step(number, stage - 1).wait()
+                if stage < dims:
+                    step(number, stage).start()
+
+
+def gather_first(own_a, own_b):
+    dims = len(place_bits())
+    cols = own_a.shape[1]
+    width = cols // 8 // 128 * 128
+    cuts = [k * width for k in range(8)] + [cols]
+    pieces = [(1, 0, own_b.shape[1], 0)]
+    pieces += [(0, cuts[k], cuts[k + 1] - cuts[k], (k + 1) % 2) for k in range(8)]
+    any_space = pl.BlockSpec(memory_space=pl.ANY)
+    lead = (2,) * dims
+    full_a, full_b = pl.pallas_call(
+        partial(gather_kernel, pieces),
+        in_specs=[any_space, any_space],
+        out_specs=[any_space, any_space],
+        out_shape=[
+            jax.ShapeDtypeStruct(lead + own_a.shape, own_a.dtype),
+            jax.ShapeDtypeStruct(lead + own_b.shape, own_b.dtype),
+        ],
+        scratch_shapes=[
+            pltpu.SemaphoreType.DMA((2,)),
+            pltpu.SemaphoreType.DMA((len(pieces), dims)),
+            pltpu.SemaphoreType.DMA((len(pieces), dims)),
+        ],
+        compiler_params=pltpu.CompilerParams(collective_id=0, has_side_effects=True),
+        name="gather_first",
+    )(own_a, own_b)
+    return full_a.reshape((-1,) + own_a.shape), full_b.reshape((-1,) + own_b.shape)
+
+
+class Stream:
+    def __init__(self, order, count, start_piece, end_piece, bufs, dtype):
+        self.order, self.count = order, count
+        self.start_piece, self.end_piece = start_piece, end_piece
+        self.dtype = dtype
+        self.dims = len(order)
+        self.own, self.recv, self.acc, self.out = bufs[0], bufs[1 : 1 + self.dims], bufs[1 + self.dims : 2 * self.dims], bufs[2 * self.dims]
+        self.own_sem, self.send, self.got, self.credit, self.out_sem = bufs[2 * self.dims + 1 :]
+
+    @staticmethod
+    def buffers(dims, rows, cols, dtype):
+        shape = lambda n: (2,) * n + (rows, cols)
+        return (
+            [pltpu.VMEM((2,) + shape(dims - 1), dtype)]
+            + [pltpu.VMEM((2,) + shape(dims - 1 - k), dtype) for k in range(dims)]
+            + [pltpu.VMEM(shape(dims - 1 - k), dtype) for k in range(dims - 1)]
+            + [pltpu.VMEM((2, rows, cols), F32)]
+            + [
+                pltpu.SemaphoreType.DMA((2,)),
+                pltpu.SemaphoreType.DMA((dims, 2)),
+                pltpu.SemaphoreType.DMA((dims, 2)),
+                pltpu.SemaphoreType.REGULAR((dims,)),
+                pltpu.SemaphoreType.DMA((2,)),
+            ]
+        )
+
+    def half(self, stage, value):
+        left = [d for d in range(self.dims) if d not in self.order[:stage]]
+        return tuple(value if d == self.order[stage] else slice(None) for d in left)
+
+    def copy(self, stage, src, slot):
+        return remote(
+            src, self.recv[stage].at[slot], self.send.at[stage, slot], self.got.at[stage, slot], self.order[stage]
+        )
+
+    def sent_part(self, stage):
+        return self.acc[stage - 1].at[self.half(stage, 1 - bit_of(self.order[stage]))]
+
+    def credit_before(self, stage, piece):
+        @pl.when(piece >= 2)
+        def _():
+            pl.semaphore_wait(self.credit.at[stage], 1)
+
+    def pump(self, it):
+        dims = self.dims
+        for stage in reversed(range(dims)):
+            piece = it - 1 - stage
+
+            @pl.when((piece >= 0) & (piece < self.count))
+            def _(stage=stage, piece=piece):
+                slot = piece % 2
+                if stage == 0:
+                    self.copy(0, self.recv[0].at[slot], slot).wait()
+                    pltpu.make_async_copy(self.own.at[slot], self.own.at[slot], self.own_sem.at[slot]).wait()
+                    kept = self.own[slot]
+                else:
+                    self.copy(stage, self.sent_part(stage), slot).wait()
+                    kept = self.acc[stage - 1][self.half(stage, bit_of(self.order[stage]))]
+                total = kept.astype(F32) + self.recv[stage][slot].astype(F32)
+                if stage < dims - 1:
+                    self.acc[stage][...] = total.astype(self.dtype)
+                    self.credit_before(stage + 1, piece)
+                    self.copy(stage + 1, self.sent_part(stage + 1), slot).start()
+                else:
+                    @pl.when(piece >= 2)
+                    def _():
+                        pltpu.make_async_copy(self.out.at[slot], self.out.at[slot], self.out_sem.at[slot]).wait()
+                    self.out[slot] = total
+                    self.end_piece(piece, self.out.at[slot], self.out_sem.at[slot])
+
+                @pl.when(piece < self.count - 2)
+                def _():
+                    pl.semaphore_signal(
+                        self.credit.at[stage], inc=1, device_id=partner(self.order[stage]),
+                        device_id_type=pl.DeviceIdType.MESH,
+                    )
+
+        @pl.when(it < self.count)
+        def _():
+            slot = it % 2
+            self.credit_before(0, it)
+            self.start_piece(
+                it, self.own.at[slot], self.own_sem.at[slot],
+                lambda src: self.copy(0, src, slot), self.order[0],
+            )
+
+    def finish(self):
+        for piece in range(max(self.count - 2, 0), self.count):
+            slot = piece % 2
+            pltpu.make_async_copy(self.out.at[slot], self.out.at[slot], self.out_sem.at[slot]).wait()
+
+
+def piece_plan(arrays, outs, lane, lanes_used):
+    dims = len(place_bits())
+    spans, first = [], 0
+    for ref, out, subs, per in arrays:
+        spans.append((ref, out, subs, per, first))
+        first += subs * per
+
+    def at_cols(piece, first_it, per):
+        return pl.ds(pl.multiple_of(((piece - first_it) % per) * (PIECE * lanes_used) + lane * PIECE, PIECE), PIECE)
+
+    def start(piece, own, own_sem, send, dim):
+        for ref, out, subs, per, first_it in spans:
+            @pl.when((piece >= first_it) & (piece < first_it + subs * per))
+            def _(ref=ref, subs=subs, per=per, first_it=first_it):
+                tail = (slice(None), at_cols(piece, first_it, per))
+                if subs > 1:
+                    tail = ((piece - first_it) // per,) + tail
+                pick = lambda v: ref.at[tuple(v if d == dim else slice(None) for d in range(dims)) + tail]
+                send(pick(1 - bit_of(dim))).start()
+                pltpu.make_async_copy(pick(bit_of(dim)), own, own_sem).start()
+
+    def end(piece, src, sem):
+        for ref, out, subs, per, first_it in spans:
+            @pl.when((piece >= first_it) & (piece < first_it + subs * per))
+            def _(out=out, subs=subs, per=per, first_it=first_it):
+                at = (slice(None), at_cols(piece, first_it, per))
+                if subs > 1:
+                    at = ((piece - first_it) // per,) + at
+                pltpu.make_async_copy(src, out.at[at], sem).start()
+
+    return first, start, end
+
+
+def reduce_kernel(layout, n_in, *refs):
+    dims = len(place_bits())
+    ins, outs, bufs = refs[:n_in], refs[n_in : 2 * n_in], refs[2 * n_in :]
+    size = 2 * dims + 6
+    orders = halving_orders()
+    arrays = [(ins[j], outs[j], subs, per) for j, (subs, per) in enumerate(layout)]
+    streams = []
+    for lane in range(2):
+        count, start, end = piece_plan(arrays, outs, lane, 2)
+        streams.append(Stream(orders[lane], count, start, end, bufs[lane * size : (lane + 1) * size], BF))
+
+    def start_small(piece, own, own_sem, send, dim):
+        pick = lambda v: ins[-1].at[tuple(v if d == dim else slice(None) for d in range(dims))]
+        send(pick(1 - bit_of(dim))).start()
+        pltpu.make_async_copy(pick(bit_of(dim)), own, own_sem).start()
+
+    def end_small(piece, src, sem):
+        pltpu.make_async_copy(src, outs[-1], sem).start()
+
+    small = Stream(orders[0], 1, start_small, end_small, bufs[2 * size :], F32)
+    greet()
+
+    @pl.loop(0, count + dims)
+    def _(it):
+        for stream in streams:
+            stream.pump(it)
+        small.pump(it)
+
+    for stream in streams + [small]:
+        stream.finish()
+
+
+def reduce_all(arrays, small):
+    dims = len(place_bits())
+    lead = (2,) * dims
+    views, layout, outs = [], [], []
+    for a in arrays:
+        rows = a.shape[0] >> dims
+        subs = rows // 64
+        tail = (64, a.shape[1]) if subs == 1 else (subs, 64, a.shape[1])
+        views.append(a.reshape(lead + tail))
+        layout.append((subs, a.shape[1] // (2 * PIECE)))
+        outs.append(jax.ShapeDtypeStruct(tail, F32))
+    views.append(small)
+    outs.append(jax.ShapeDtypeStruct(small.shape[dims:], F32))
+    any_space = pl.BlockSpec(memory_space=pl.ANY)
+    scratch = Stream.buffers(dims, 64, PIECE, BF) * 2 + Stream.buffers(dims, *small.shape[dims:], F32)
+    got = pl.pallas_call(
+        partial(reduce_kernel, layout, len(views)),
+        in_specs=[any_space] * len(views),
+        out_specs=[any_space] * len(views),
+        out_shape=outs,
+        scratch_shapes=scratch,
+        compiler_params=pltpu.CompilerParams(
+            collective_id=1, has_side_effects=True, vmem_limit_bytes=40 * 1024 * 1024
+        ),
+        name="reduce_all",
+    )(*views)
+    return [g.reshape(-1, g.shape[-1]) for g in got[:-1]] + [got[-1]]
 
 
 def scatter_sum(part, rows, swap):
@@ -456,15 +751,22 @@
     chunks = length // Q
     in_rows, out_rows = in_weight.shape[0], out_weight.shape[0]
 
-    conv_own = in_weight[:, DI:]
+    own = conv_bias.shape[0]
+    fast = in_rows % 64 == 0 and out_rows % 64 == 0
+    conv_own = jnp.pad(in_weight[:, DI:], ((0, 0), (0, CD - (PROJ - DI))))
     gate_own = in_weight[:, :DI]
-    gains = lax.all_gather(
-        jnp.concatenate([norm_gain, gate_gain, conv_weight.reshape(-1), conv_bias]), BOTH
-    )
-    w_conv = lax.all_gather(conv_own, BOTH, axis=0, tiled=True)
+    gains_own = jnp.concatenate([norm_gain, gate_gain, conv_weight.reshape(-1), conv_bias])
+    if fast:
+        used = gains_own.shape[0]
+        gains_own = jnp.pad(gains_own, (0, 16 * 128 - used)).reshape(16, 128)
+        w_conv, gains = gather_first(conv_own, gains_own)
+        w_conv = w_conv.reshape(-1, CD)
+        gains = gains.reshape(-1, 16 * 128)[:, :used]
+    else:
+        w_conv = lax.all_gather(conv_own, BOTH, axis=0, tiled=True)
+        gains = lax.all_gather(gains_own, BOTH)
     w_gate = lax.all_gather(gate_own, BOTH, axis=0, tiled=True)
     w_out = lax.all_gather(out_weight, BOTH, axis=0, tiled=True)
-    own = conv_bias.shape[0]
     cut = in_rows + out_rows
     norm_full = gains[:, :in_rows].reshape(-1).astype(F32)
     gate_full = gains[:, in_rows:cut].reshape(1, DI).astype(F32)
@@ -587,9 +889,7 @@
     values = values[:total]
     output = (values + jnp.dot(mixed, w_out, preferred_element_type=F32)).astype(BF)
     dw_out = dot_tn(mixed, cotangent).astype(BF)
-    out_weight_grad = scatter_halves(dw_out, out_rows)
     dw_gate = dot_tn(hidden, dgate).astype(BF)
-    gate_cols_grad = scatter_halves(dw_gate, in_rows)
 
     back = lambda s, c: (s * chunks + chunks - 1 - c, 0)
     before = lambda s, c: jnp.where(
@@ -649,7 +949,6 @@
     dproj = lax.dynamic_update_slice(dproj, ends.astype(BF), (0, length - 8, 0)).reshape(total, CD)
 
     dw_conv = dot_tn(hidden, dproj).astype(BF)
-    conv_cols_grad = scatter_halves(dw_conv, in_rows)
     hidden_grad = lax.dot_general(
         dgate, w_gate, (((1,), (1,)), ((), ())), preferred_element_type=F32
     ) + lax.dot_general(dproj, w_conv, (((1,), (1,)), ((), ())), preferred_element_type=F32)
@@ -660,16 +959,29 @@
         weighted - normed * jnp.mean(weighted * normed, axis=-1, keepdims=True)
     )
 
-    in_weight_grad = jnp.concatenate([gate_cols_grad, conv_cols_grad], axis=1)
+    skip_grad = jnp.sum(skip_sums[0].reshape(H, HD), axis=1)
+    heads = jnp.concatenate([head_sums[0], head_sums[1], skip_grad])
+    if fast:
+        shares = conv_sums[:5].reshape(5, -1, own).transpose(1, 0, 2).reshape(-1, 5 * own)
+        small = jnp.concatenate([shares, jnp.broadcast_to(heads, (shares.shape[0], 3 * H))], axis=1)
+        small = jnp.pad(small, ((0, 0), (0, 1024 - small.shape[1])))
+        small = small.reshape((2,) * len(place_bits()) + (8, 128))
+        out_weight_grad, gate_cols_grad, conv_cols_grad, small = reduce_all([dw_out, dw_gate, dw_conv], small)
+        small = small.reshape(-1)
+        shares = small[: 5 * own].reshape(5, own)
+        heads = small[5 * own : 5 * own + 3 * H]
+    else:
+        out_weight_grad = scatter_halves(dw_out, out_rows)
+        gate_cols_grad = scatter_halves(dw_gate, in_rows)
+        conv_cols_grad = scatter_halves(dw_conv, in_rows)
+        small = lax.psum(jnp.concatenate([conv_sums[:5].reshape(-1), heads]), BOTH)
+        place = lax.axis_index("dp") * lax.axis_size("seq") + lax.axis_index("seq")
+        shares = lax.dynamic_slice(small[: 5 * XBC].reshape(5, XBC), (0, place * own), (5, own))
+        heads = small[5 * XBC :]
+    heads = heads.reshape(3, H)
+    in_weight_grad = jnp.concatenate([gate_cols_grad, conv_cols_grad[:, : PROJ - DI]], axis=1)
     norm_share = jnp.sum(in_weight_grad * in_weight.astype(F32), axis=1) / norm_gain.astype(F32)
     gate_share = jnp.sum(out_weight_grad * out_weight.astype(F32), axis=1) / gate_gain.astype(F32)
-
-    skip_grad = jnp.sum(skip_sums[0].reshape(H, HD), axis=1)
-    small = jnp.concatenate([conv_sums[:5].reshape(-1), head_sums[:2].reshape(-1), skip_grad])
-    small = lax.psum(small, BOTH)
-    place = lax.axis_index("dp") * lax.axis_size("seq") + lax.axis_index("seq")
-    shares = lax.dynamic_slice(small[: 5 * XBC].reshape(5, XBC), (0, place * own), (5, own))
-    heads = small[5 * XBC :].reshape(3, H)
     return (
         output.reshape(seqs, length, width),
         input_grad.astype(BF).reshape(seqs, length, width),

time: 1330 us -> 1060 us (0.80)
  waiting for transfers between devices: 457 us -> 6.88 us
  Pallas kernels: 328 us -> 737 us
  local copies, waits for them, and re-layouts: 129 us -> 19.5 us
  other arithmetic: 80.1 us -> 35.2 us
  blocking collectives: 41.4 us -> 0 us
  starting transfers between devices: 40.4 us -> 10.4 us
    pallas_call x0 -> x2, Pallas kernels: none -> 409 us  [the longest x1 228 us: reduce_all(): pl.pallas_call(partial(reduce_kernel, layout, len(views)), in_specs=[any_...]
    ppermute x30 -> x0, waiting for transfers between devices: 192 us -> none  [scatter_sum(): lax.ppermute(sent, axis, [(i, i ^ 1 << bit) for i in range(lax.axis_size(...]
    all_gather x1 -> x0, waiting for transfers between devices: 100 us -> none  [shards(): w_conv = lax.all_gather(conv_own, BOTH, axis=0, tiled=True)]
    psum x1 -> x0, waiting for transfers between devices: 92.1 us -> none  [shards(): small = lax.psum(small, BOTH)]
    slice x10 -> x3, local copies, waits for them, and re-layouts: 59.2 us -> 1.39 us  [the longest x1 1.1 us: shards(): conv_own = jnp.pad(in_weight[:, DI:], ((0, 0), (0, CD - (PROJ - DI))))]
    all_gather x1, waiting for transfers between devices: 47.7 us -> 0.01 us  [shards(): w_gate = lax.all_gather(gate_own, BOTH, axis=0, tiled=True)]
    convert_element_type x24 -> x0, other arithmetic: 47.3 us -> none  [scatter_sum(): blocks = blocks.astype(BF)]
    unnamed x1 -> x0, blocking collectives: 41.4 us -> none
  transfers between devices with their start and end apart: 38 -> 6, of which waited for: 21 -> 1; matrix products, arithmetic and copies ran while one was open for 29% -> 17% of each run, Pallas kernels for 18% -> 25%
where the time goes in v2:
time: 1060 us; the launch traced here: 1050 us
  Pallas kernels  737 us (70%)
  matrix products  224 us (21%)
  other arithmetic  35.2 us (3%)
  local copies, waits for them, and re-layouts  19.5 us (2%)
  between operations  14.9 us (1%)
    pallas_call x1, Pallas kernels, reduce_all(): pl.pallas_call(partial(reduce_kernel, layout, len(views)), in_specs=[any_...  228 us
    pallas_call x1, Pallas kernels, gather_first(): pl.pallas_call(partial(gather_kernel, pieces), in_specs=[any_space, any_s...  181 us
    pallas_call x1, Pallas kernels, shards(): pl.pallas_call(backward_kernel, grid=grid, in_specs=[pl.BlockSpec((Q, CD)...  156 us
    pallas_call x1, Pallas kernels, shards(): pl.pallas_call(gate_kernel, grid=grid, in_specs=[pl.BlockSpec((Q, DI), at...  88.6 us
    pallas_call x1, Pallas kernels, shards(): pl.pallas_call(forward_kernel, grid=grid, in_specs=[pl.BlockSpec((Q, CD),...  82.9 us
    dot_general x3, matrix products, dot_tn(): lax.dot_general(a, b, (((0,), (0,)), ((), ())), preferred_element_type=F32)  75.2 us
    dot_general x1, matrix products, shards(): projected = jnp.dot(hidden, w_conv, preferred_element_type=F32)  27.6 us
    dot_general x1, matrix products, shards(): lax.dot_general(dgate, w_gate, (((1,), (1,)), ((), ())), preferred_elemen...  26.1 us
  transfers between devices with their start and end apart: 6, of which 1 were waited for; matrix products, arithmetic and copies ran while one was open for 17% of the time, Pallas kernels for 25%

profile of v2, /device:TPU:0, one launch (start us, length us, event | category | flops | bytes accessed | tf_op | source)
XLA Modules:
  0.0 1048.1 jit_solution(13280348352190770441)
XLA Ops:
  7.2 1.9 slice.128
  9.2 0.7 all-gather.5.cloned.1.call-update
  9.9 0.7 reshape.379
  10.6 0.6 reduce-window.6
  11.2 0.2 slice_reduce_fusion.3
  11.4 0.2 reduce-window.9
  11.7 0.2 slice_reduce_fusion.4
  11.9 0.9 slice_select_fusion
  12.9 4.8 collective-permute-start
  17.7 1.1 slice.118
  18.8 0.8 reshape.382
  19.6 0.9 pad.33.own_a
  20.5 1.4 fusion.20.own_b
  21.8 181.0 %gather_first.1 = (bf16[2,2,2,2,2,64,4608]{6,5,4,3,2,1,0:T(8,128)(2,1)}, bf16[2,2,2,2,2,16,128]{6,5,4,3,2,1,0:T(8,128)(2,1)}) custom-call(bf16[64,4608]{1,0:T(8,128)(2,1)} %pad.33.own_a, bf16[16,128]{1,0:T(8,128)(2,1)} %fusion.20.own_b), custom_call_target="tpu_custom_call" | custom-call | tf_op jit(solution)/shard_map/gather_first/pallas_call | solution.py:499
  202.8 0.9 copy.58
  203.9 0.2 slice_reduce_fusion.2
  204.4 0.2 slice_reduce_fusion.1
  204.7 0.2 copy.44
  205.1 0.1 reshape.385
  205.4 0.8 pad.38.info_ref
  206.3 1.2 exponential_bitcast_fusion
  207.5 0.7 slice_convert_fusion
  208.2 1.2 compare_convert_fusion.spread_ref
  209.4 0.7 maximum_convert_fusion.1.cw_ref
  210.2 0.6 select_maximum_fusion.hp_ref
  210.8 2.7 multiply_reduce_fusion
  213.5 0.6 slice.154
  214.1 3.6 multiply_convert_fusion
  217.8 27.6 %fusion.22.pc_ref.front_ref.halo_ref = f32[1040,4608]{1,0:T(8,128)} fusion(bf16[1040,2048]{1,0:T(8,128)(2,1)S(1)} %multiply_convert_fusion, bf16[2048,4608]{1,0:T(8,128)(2,1)} %bitcast.132), kind=kOutput, calls=%fused_computation.82 | convolution fusion | flops 19629342720 | bytes 42303488 | tf_op jit(solution)/shard_map/dot_general | solution.py:785
  245.4 0.6 broadcast_in_dim.45.infot_ref
  246.0 82.9 %scan_forward.1 = (f32[1024,4096]{1,0:T(8,128)}, bf16[1024,4352]{1,0:T(8,128)(2,1)}, bf16[1024,4096]{1,0:T(8,128)(2,1)}, f32[1024,256]{1,0:T(8,128)}, bf16[256,4096]{1,0:T(8,128)(2,1)}) custom-call(f32[1040,4608]{1,0:T(8,128)} %fusion.22.pc_ref.front_ref.halo_ref, f32[1040,4608]{1,0:T(8,128)} %fusion.22.pc_ref.front_ref.halo_ref, f32[1024,128]{1,0:T(8,128)} %pad.38.info_ref, ...), custom_call_target="tpu_custom_call" | custom-call | tf_op jit(solution)/shard_map/scan_forward/pallas_call | solution.py:818
  328.9 2.5 collective-permute-start.1
  331.4 6.6 maximum_convert_fusion
  338.0 23.5 %fusion.2.gate_ref = f32[1024,4096]{1,0:T(8,128)} fusion(bf16[2048,4096]{1,0:T(8,128)(2,1)} %all-gather.3.cloned.1.call-done, bf16[1040,2048]{1,0:T(8,128)(2,1)} %copy-done.3), kind=kOutput, calls=%fused_computation.13 | convolution fusion | flops 17179869184 | bytes 37748736 | tf_op jit(solution)/shard_map/dot_general | solution.py:787
  361.4 23.6 %fusion.23.mg_ref = f32[1024,4096]{1,0:T(8,128)} fusion(bf16[1024,2048]{1,0:T(8,128)(2,1)} %bitcast.99, bf16[4096,2048]{1,0:T(8,128)(2,1)} %all-gather.5.cloned.1.call-done), kind=kOutput, calls=%fused_computation.83 | convolution fusion | flops 17179869184 | bytes 37748736 | tf_op jit(solution)/shard_map/dot_general | solution.py:789
  385.0 1.3 copy-done.1
  386.4 88.6 %gate_both.1 = (bf16[1024,4096]{1,0:T(8,128)(2,1)}, bf16[1024,4096]{1,0:T(8,128)(2,1)}, bf16[1024,4096]{1,0:T(8,128)(2,1)}, f32[1024,64]{1,0:T(8,128)}, f32[256,4096]{1,0:T(8,128)}, /*index=5*/f32[8,4096]{1,0:T(8,128)}) custom-call(f32[1024,4096]{1,0:T(8,128)} %get-tuple-element.34.y_ref, bf16[1024,4352]{1,0:T(8,128)(2,1)} %get-tuple-element.35.act_ref, ...), custom_call_target="tpu_custom_call" | custom-call | tf_op jit(solution)/shard_map/gate_both/pallas_call | solution.py:852
  474.9 3.8 convert_element_type.214
  478.8 1.7 collective-permute-start.2
  480.5 0.9 slice_reduce_fusion
  481.6 24.8 %convolution_convert_fusion.2 = bf16[4096,2048]{1,0:T(8,128)(2,1)} fusion(bf16[1024,4096]{1,0:T(8,128)(2,1)} %get-tuple-element.38, bf16[1024,2048]{1,0:T(8,128)(2,1)} %bitcast.100), kind=kOutput, calls=%fused_computation.2 | convolution fusion | flops 17188257792 | bytes 29360128 | tf_op jit(solution)/shard_map/dot_general | solution.py:39
  506.4 24.3 %add_convert_fusion.1 = bf16[1024,2048]{1,0:T(8,128)(2,1)} fusion(f32[1040,2048]{1,0:T(8,128)} %maximum_convert_fusion, bf16[1024,4096]{1,0:T(8,128)(2,1)} %get-tuple-element.38, bf16[4096,2048]{1,0:T(8,128)(2,1)} %all-gather.5.cloned.1.call-done), kind=kOutput, calls=%fused_computation.8 | convolution fusion | flops 17184063488 | bytes 37748736 | tf_op jit(solution)/shard_map/dot_general | solution.py:890
  530.7 23.9 %convolution_convert_fusion.1 = bf16[2048,4096]{1,0:T(8,128)(2,1)} fusion(bf16[1024,4096]{1,0:T(8,128)(2,1)} %get-tuple-element.39, bf16[1040,2048]{1,0:T(8,128)(2,1)S(1)} %bitcast.98), kind=kOutput, calls=%fused_computation.1 | convolution fusion | flops 17188257792 | bytes 29360128 | tf_op jit(solution)/shard_map/dot_general | solution.py:39
  554.6 1.3 copy-done.5
  556.0 156.3 %scan_backward.1 = (bf16[1024,4608]{1,0:T(8,128)(2,1)}, f32[16,4352]{1,0:T(8,128)}, f32[8,4352]{1,0:T(8,128)}, f32[8,64]{1,0:T(8,128)}) custom-call(f32[1040,4608]{1,0:T(8,128)} %fusion.22.pc_ref.front_ref.halo_ref, f32[1040,4608]{1,0:T(8,128)} %fusion.22.pc_ref.front_ref.halo_ref, f32[1024,128]{1,0:T(8,128)} %pad.38.info_ref, ...), custom_call_target="tpu_custom_call" | custom-call | tf_op jit(solution)/shard_map/scan_backward/pallas_call | solution.py:899
  712.2 0.7 slice_bitcast_fusion.1
  713.0 1.1 reshape.395
  714.2 0.1 reshape.396
  714.3 1.0 convert_element_type.216
  715.3 1.3 collective-permute-start.3
  716.8 6.2 collective-permute-done.3
  722.9 1.7 fusion.6
  724.6 26.5 %convolution_convert_fusion = bf16[2048,4608]{1,0:T(8,128)(2,1)} fusion(bf16[1024,4608]{1,0:T(8,128)(2,1)} %bitcast.128, bf16[1040,2048]{1,0:T(8,128)(2,1)} %copy-done.3), kind=kOutput, calls=%fused_computation | convolution fusion | flops 19336790016 | bytes 32505856 | tf_op jit(solution)/shard_map/dot_general | solution.py:39
  751.1 24.0 %fusion.24 = f32[1024,2048]{1,0:T(8,128)} fusion(bf16[1024,4608]{1,0:T(8,128)(2,1)S(1)} %bitcast.129, bf16[2048,4608]{1,0:T(8,128)(2,1)} %bitcast.133), kind=kOutput, calls=%fused_computation.84 | convolution fusion | flops 19327352832 | bytes 36700160 | tf_op jit(solution)/shard_map/dot_general | solution.py:954
  775.1 228.2 %reduce_all.1 = (f32[2,64,2048]{2,1,0:T(8,128)S(1)}, f32[64,4096]{1,0:T(8,128)S(1)}, f32[64,4608]{1,0:T(8,128)S(1)}, f32[8,128]{1,0:T(8,128)S(1)}) custom-call(bf16[2,2,2,2,2,2,64,2048]{7,6,5,4,3,2,1,0:T(8,128)(2,1)} %bitcast.95, bf16[2,2,2,2,2,64,4096]{6,5,4,3,2,1,0:T(8,128)(2,1)} %bitcast.96, bf16[2,2,2,2,2,64,4608]{6,5,4,3,2,1,0:T(8,128)(2,1)} %bitcast.94, ...), custom_call_target="tpu_custom_call" | custom-call | tf_op jit(solution)/shard_map/reduce_all/pallas_call | solution.py:690
  1003.5 0.6 slice.139
  1004.1 1.8 multiply_reduce_fusion.2
  1005.9 0.6 fusion.21
  1006.5 0.2 multiply_reduce_fusion.3
  1006.7 0.7 slice.138
  1007.4 0.5 convert_divide_fusion
  1007.9 26.1 %multiply_reduce_fusion.1 = (f32[1024]{0:T(1024)S(1)}, f32[1024,2048]{1,0:T(8,128)S(1)}) fusion(f32[1040,2048]{1,0:T(8,128)} %maximum_convert_fusion, f32[1024]{0:T(1024)S(1)} %copy-done.9, f32[2048]{0:T(1024)S(1)} %copy-done.8, f32[1024,2048]{1,0:T(8,128)} %fusion.24, bf16[1024,4096]{1,0:T(8,128)(2,1)} %get-tuple-element.39, ...), kind=kOutput, calls=%fused_computation.6 | convolution fusion | flops 17190354944 | bytes 50348032 | tf_op jit(solution)/shard_map/dot_general | solution.py:952
  1034.0 5.9 add_convert_fusion
  1039.9 1.0 copy.63
  (77 shorter events, 1.7 us)
Async XLA Ops:
  7.2 203.0 %copy-start.15 = (f32[64]{0:T(128)S(1)}, f32[64]{0:T(128)}, u32[]{:S(2)}) copy-start(f32[64]{0:T(128)} %param.20) | copy-start | bytes 772
  7.2 203.0 %copy-start.14 = (f32[64]{0:T(128)S(1)}, f32[64]{0:T(128)}, u32[]{:S(2)}) copy-start(f32[64]{0:T(128)} %param.22) | copy-start | bytes 772
  7.2 330.8 %all-gather.3.cloned.1.call-start = ((), (), s32[]{:S(2)}) async-start(), calls=%async_computation | async-start | bytes 17301504 | tf_op jit(solution)/shard_map/all_gather | solution.py:768
  9.1 352.3 %all-gather.5.cloned.1.call-start = ((), (), s32[]{:S(2)}) async-start(), calls=%async_computation.1 | async-start | bytes 17301504 | tf_op jit(solution)/shard_map/all_gather | solution.py:769
  11.9 192.2 %copy-start.10 = (pred[2,8]{1,0:T(4,128)(4,1)}, pred[2,8]{1,0:T(4,128)(4,1)S(1)}, u32[]{:S(2)}) copy-start(pred[2,8]{1,0:T(4,128)(4,1)S(1)} %slice_compare_fusion) | copy-start | bytes 52
  12.9 197.9 %collective-permute-start = (bf16[2,8,2048]{2,1,0:T(8,128)(2,1)S(1)}, bf16[2,8,2048]{2,1,0:T(8,128)(2,1)S(1)}, u32[]{:S(2)}, u32[]{:S(2)}) collective-permute-start(bf16[2,8,2048]{2,1,0:T(8,128)(2,1)S(1)} %slice_select_fusion), channel_id=1, source_target_pairs={{0,1},{2,3},{4,5},{6,7},{8,9},{10,11},{12,13},{14,15},{16,17},{18,... | collective-permute-start | bytes 196616 | tf_op jit(solution)/shard_map/ppermute | solution.py:398
  205.0 40.3 %copy-start.7 = (f32[2048]{0:T(1024)}, f32[2048]{0:T(1024)S(1)}, u32[]{:S(2)}) copy-start(f32[2048]{0:T(1024)S(1)} %reshape.400) | copy-start | bytes 24580
  205.4 8.7 copy-start
  217.7 27.6 %copy-start.3 = (bf16[1040,2048]{1,0:T(8,128)(2,1)}, bf16[1040,2048]{1,0:T(8,128)(2,1)S(1)}, u32[]{:S(2)}) copy-start(bf16[1040,2048]{1,0:T(8,128)(2,1)S(1)} %multiply_convert_fusion) | copy-start | bytes 12779524
  328.9 56.2 %collective-permute-start.1 = (bf16[256,4096]{1,0:T(8,128)(2,1)}, bf16[256,4096]{1,0:T(8,128)(2,1)S(1)}, u32[]{:S(2)}, u32[]{:S(2)}) collective-permute-start(bf16[256,4096]{1,0:T(8,128)(2,1)} %get-tuple-element.37), channel_id=1, source_target_pairs={{0,1},{2,3},{4,5},{6,7},{8,9},{10,11},{12,13},{14,15},{16,17},{18,... | collective-permute-start | bytes 6291464 | tf_op jit(solution)/shard_map/ppermute | solution.py:398
  385.0 1.3 copy-start.1
  474.9 55.7 %slice-start = ((s8[4259840]{0:T(1024)(128)(4,1)}), s8[65536]{0:T(1024)(128)(4,1)S(1)}, s32[]{:S(2)}) async-start(s8[4259840]{0:T(1024)(128)(4,1)} %bitcast.97), calls=%async_computation.2 | async-start | bytes 131072
  478.8 75.8 %collective-permute-start.2 = (bf16[256,4096]{1,0:T(8,128)(2,1)}, bf16[256,4096]{1,0:T(8,128)(2,1)S(1)}, u32[]{:S(2)}, u32[]{:S(2)}) collective-permute-start(bf16[256,4096]{1,0:T(8,128)(2,1)} %convert_element_type.214), channel_id=1, source_target_pairs={{1,0},{3,2},{5,4},{7,6},{9,8},{11,10},{13,12},{15,14},{17,16},{19,... | collective-permute-start | bytes 6291464 | tf_op jit(solution)/shard_map/ppermute | solution.py:398
  481.6 49.1 %slice-start.1 = ((s8[4259840]{0:T(1024)(128)(4,1)}), s8[4194304]{0:T(1024)(128)(4,1)S(1)}, s32[]{:S(2)}) async-start(s8[4259840]{0:T(1024)(128)(4,1)} %bitcast.97), calls=%async_computation.3 | async-start | bytes 8388608
  554.6 1.3 copy-start.5
  556.0 167.0 %copy-start.11 = (pred[2,8]{1,0:T(4,128)(4,1)S(1)}, pred[2,8]{1,0:T(4,128)(4,1)}, u32[]{:S(2)}) copy-start(pred[2,8]{1,0:T(4,128)(4,1)} %copy-done.10) | copy-start | bytes 52
  715.3 7.6 collective-permute-start.3
  724.6 26.5 %copy-start.12 = (bf16[2,512,4608]{2,1,0:T(8,128)(2,1)S(1)}, bf16[2,512,4608]{2,1,0:T(8,128)(2,1)}, u32[]{:S(2)}) copy-start(bf16[2,512,4608]{2,1,0:T(8,128)(2,1)} %fusion.6) | copy-start | bytes 28311556
  775.1 229.0 %copy-start.2 = (bf16[64,8512]{1,0:T(8,128)(2,1)S(1)}, bf16[64,8512]{1,0:T(8,128)(2,1)}, u32[]{:S(2)}) copy-start(bf16[64,8512]{1,0:T(8,128)(2,1)} %param.14) | copy-start | bytes 3268612
  775.1 230.8 %copy-start.13 = (bf16[64]{0:T(256)(128)(2,1)S(1)}, bf16[64]{0:T(256)(128)(2,1)}, u32[]{:S(2)}) copy-start(bf16[64]{0:T(256)(128)(2,1)} %param.15) | copy-start | bytes 388
  775.1 231.4 %copy-start.6 = (bf16[128,2048]{1,0:T(8,128)(2,1)S(1)}, bf16[128,2048]{1,0:T(8,128)(2,1)}, u32[]{:S(2)}) copy-start(bf16[128,2048]{1,0:T(8,128)(2,1)} %param.16) | copy-start | bytes 1572868
  1003.4 4.0 copy-start.16
  1003.4 4.5 copy-start.8
  1003.4 4.5 copy-start.9
  1007.9 26.1 %copy-start.4 = (bf16[2,512,2048]{2,1,0:T(8,128)(2,1)S(1)}, bf16[2,512,2048]{2,1,0:T(8,128)(2,1)}, u32[]{:S(2)}) copy-start(bf16[2,512,2048]{2,1,0:T(8,128)(2,1)} %param.23) | copy-start | bytes 12582916
Sparse Core Ops, SparseCore 0:
  11.6 161.7 all-gather.2
  176.4 114.2 all-gather.4

commit v3 on v2

--- a/solution.py
+++ b/solution.py
@@ -15,7 +15,13 @@
 XBC = 4352
 PROJ = 8512
 CD = 4608
-PIECE = 256
+LANES = (384, 384, 256)
+GROUP = 1024
+PIECE_ROWS = 32
+LAG = 2
+PUMPS = 3
+GATHER_PUMPS = 4
+IN_TILE = 512
 Q = 128
 LB = 256
 EPS = 1e-05
@@ -61,7 +67,7 @@
 
 
 def sigmoid(v):
-    return 1.0 / (1.0 + jnp.exp(-v))
+    return 0.5 * jnp.tanh(0.5 * v) + 0.5
 
 
 def softplus(z):
@@ -97,12 +103,21 @@
     return total, (t0, t1, t2, t3)
 
 
-def forward_kernel(
-    pc_ref, front_ref, info_ref, infot_ref, cw_ref, hp_ref, spread_ref,
-    y_ref, act_ref, st_ref, row_ref, fin_ref,
-    ext, state, pre,
-):
+def forward_kernel(shapes, *refs):
+    extra = len(shapes)
+    pc_ref, front_ref, info_ref, infot_ref, cw_ref, hp_ref, spread_ref = refs[:7]
+    own = refs[7 : 7 + extra]
+    y_ref, act_ref, st_ref, row_ref, fin_ref = refs[7 + extra : 12 + extra]
+    full = refs[12 + extra : 12 + 2 * extra]
+    ext, state, pre = refs[12 + 2 * extra : 15 + 2 * extra]
     chunk = pl.program_id(1)
+    step = pl.program_id(0) * pl.num_programs(1) + chunk
+    pump = lambda place: None
+    if extra:
+        gather = Gather(shapes, own, full, refs[15 + 2 * extra :])
+        pl.when(step == 0)(gather.begin)
+        pump = lambda place: gather.pump(step * GATHER_PUMPS + place)
+    pump(0)
 
     @pl.when(chunk == 0)
     def _():
@@ -124,6 +139,7 @@
         out, _ = conv_block(ext, cw_ref, taps, at)
         act_ref[:, at] = (out * sigmoid(out)).astype(BF)
 
+    pump(1)
     z = pc_ref[:, XBC : XBC + H] + hp_ref[0:1, :]
     dt = softplus(z)
     decay = -dt * hp_ref[1:2, :]
@@ -148,7 +164,7 @@
     in_parts = doubled(inflow)
     out_parts = doubled(outflow)
 
-    @pl.loop(0, DI // LB)
+    @pl.loop(0, DI // LB, unroll=DI // LB)
     def _(i):
         at = lanes(i)
         spread = spread_ref[:, at]
@@ -161,8 +177,11 @@
         given = (act_ref[:, at].astype(F32) * out_wide).astype(BF)
         state[:, at] = held * in_wide[Q - 1 : Q, :] + dot_tn(b_proj, given)
 
+    pump(2)
     left, right = pair_masks()
     for p in range(H // 2):
+        if p == H // 4:
+            pump(3)
         weights = []
         for h in (2 * p, 2 * p + 1):
             gap = (cs[:, h : h + 1] - turned[64 + h : 65 + h, :]) + bias
@@ -209,7 +228,7 @@
         return sums[0] + v * v, sums[1] + e * v
 
     zero = jnp.zeros((Q, LB), F32)
-    squares, cross = lax.fori_loop(0, DI // LB, first, (zero, zero))
+    squares, cross = lax.fori_loop(0, DI // LB, first, (zero, zero), unroll=True)
     rs = lax.rsqrt(jnp.sum(squares, axis=1, keepdims=True) * (1.0 / DI) + EPS)
     mean_eu = jnp.sum(cross, axis=1, keepdims=True) * rs * (1.0 / DI)
     rs = jnp.broadcast_to(rs, (Q, LB))
@@ -237,17 +256,30 @@
         skip_ref[0:1, at] += jnp.sum(dyf * x, axis=0, keepdims=True)
         return total + head_sum(dyf * y, spread[:H])
 
-    dot_ref[...] = lax.fori_loop(0, DI // LB, second, jnp.zeros((Q, H), F32))
-
-
-def backward_kernel(
-    pc_ref, halo_ref, info_ref, infot_ref, cw_ref, hp_ref, spread_ref,
-    dy_ref, st_ref, sin_ref, dsin_ref, row_ref, prev_ref, pdot_ref,
-    dproj_ref, front_ref, cwg_ref, hg_ref,
-    ext, act, slope, dact, d1, d2, d3, dstate, state,
-):
+    dot_ref[...] = lax.fori_loop(0, DI // LB, second, jnp.zeros((Q, H), F32), unroll=True)
+
+
+def backward_kernel(layout, *refs):
+    extra = len(layout)
+    pc_ref, halo_ref, info_ref, infot_ref, cw_ref, hp_ref, spread_ref = refs[:7]
+    dy_ref, st_ref, sin_ref, dsin_ref, row_ref, prev_ref, pdot_ref = refs[7:14]
+    dw = refs[14 : 14 + extra]
+    dproj_ref, front_ref, cwg_ref, hg_ref = refs[14 + extra : 18 + extra]
+    sums = refs[18 + extra : 18 + 2 * extra]
+    ext, act, slope, dact, d1, d2, d3, dstate = refs[18 + 2 * extra : 26 + 2 * extra]
     step = pl.program_id(1)
     chunk = pl.num_programs(1) - 1 - step
+    number = pl.program_id(0) * pl.num_programs(1) + step
+    pump = lambda place: None
+    if extra:
+        streams = make_streams(layout, dw, sums, refs[26 + 2 * extra :])
+        pl.when(number == 0)(greet)
+
+        def pump(place):
+            for stream in streams:
+                stream.pump(number * PUMPS + place)
+
+    pump(0)
 
     @pl.when((step == 0) & (pl.program_id(0) == 0))
     def _():
@@ -323,8 +355,9 @@
 
     zero = jnp.zeros((Q, N), F32)
     db, dc, rdep, kept = lax.fori_loop(
-        0, DI // LB, shared, (zero, zero, jnp.zeros((Q, H), F32), jnp.zeros((16, H), F32))
+        0, DI // LB, shared, (zero, zero, jnp.zeros((Q, H), F32), jnp.zeros((16, H), F32)), unroll=True
     )
+    pump(1)
     left, right = pair_masks()
     daff = jnp.zeros((Q, Q), F32)
     for p in range(H // 2):
@@ -350,7 +383,8 @@
         dact[:, at] = dx + dot(skip_parts, spread)[0:1, :] * dy_ref[:, at].astype(F32)
         return total + head_sum(x * dx, spread[:H])
 
-    rfull = lax.fori_loop(0, DI // LB, finish, jnp.zeros((Q, H), F32))
+    rfull = lax.fori_loop(0, DI // LB, finish, jnp.zeros((Q, H), F32), unroll=True)
+    pump(2)
     daff_low = daff.astype(BF)
     dact[:, DI : DI + N] = db + dot(daff_low, c_proj)
     dact[:, DI + N : XBC] = dc + dot_tn(daff_low, b_proj)
@@ -392,6 +426,12 @@
             w0, w1, w2 = (cw_ref[k : k + 1, at] for k in range(3))
             front_ref[:, at] = w2 * d1[1:9, at] + w1 * d2[2:10, at] + w0 * d3[3:11, at]
 
+    if extra:
+        @pl.when(number == pl.num_programs(0) * pl.num_programs(1) - 1)
+        def _():
+            for stream in streams:
+                stream.finish()
+
 
 def shift_along(block, distance):
     devices = range(lax.axis_size("seq"))
@@ -429,8 +469,9 @@
     seq_dims = [names.index(("seq", b)) for b in range(lax.axis_size("seq").bit_length() - 1)]
     dp_dims = [names.index(("dp", b)) for b in range(lax.axis_size("dp").bit_length() - 1)]
     return (
-        [dp_dims[0]] + seq_dims + dp_dims[1:],
+        dp_dims[:1] + seq_dims + dp_dims[1:],
         dp_dims[:2] + seq_dims + dp_dims[2:],
+        dp_dims[:1] + dp_dims[2:] + seq_dims + dp_dims[1:2],
     )
 
 
@@ -449,55 +490,67 @@
     )
 
 
-def gather_kernel(pieces, own_a, own_b, full_a, full_b, local, send, recv):
+def place_own(own, held, full, sems):
+    mine = tuple(bit_of(dim) for dim in range(len(place_bits())))
+    copies = [pltpu.make_async_copy(a, h, sems.at[j]) for j, (a, h) in enumerate(zip(own, held))]
+    for copy in copies:
+        copy.start()
+    for copy in copies:
+        copy.wait()
+    copies = [pltpu.make_async_copy(h, f.at[mine], sems.at[j]) for j, (h, f) in enumerate(zip(held, full))]
+    for copy in copies:
+        copy.start()
+    return copies
+
+
+def gather_kernel(groups, own_a, own_b, full_a, full_b, held_a, held_b, local, send, recv):
     dims = len(place_bits())
     orders = [list(reversed(order)) for order in halving_orders()]
     own, full = (own_a, own_b), (full_a, full_b)
     mine = tuple(bit_of(dim) for dim in range(dims))
     greet()
-    locals_ = [pltpu.make_async_copy(own[j], full[j].at[mine], local.at[j]) for j in range(2)]
-    for copy in locals_:
-        copy.start()
-
-    def step(number, stage):
-        which, start, size, order = pieces[number]
-        dim = orders[order][stage]
-        done = orders[order][:stage]
+    waiting = place_own(own, (held_a, held_b), full, local)
+
+    def step(piece, stage):
+        number, which, row, rows, start, size, lane = piece
+        dim = orders[lane][stage]
+        done = orders[lane][:stage]
         at = tuple(slice(None) if d in done else mine[d] for d in range(dims))
-        at = at + (slice(None), pl.ds(start, size))
-        src = own[which].at[:, pl.ds(start, size)] if stage == 0 else full[which].at[at]
+        at = at + (pl.ds(row, rows), pl.ds(start, size))
+        src = own[which].at[pl.ds(row, rows), pl.ds(start, size)] if stage == 0 else full[which].at[at]
         return remote(src, full[which].at[at], send.at[number, stage], recv.at[number, stage], dim)
 
-    count = len(pieces)
-    groups = (count + 1) // 2
-    for wave in range(groups + dims):
+    for wave in range(len(groups) + LAG * dims):
         for stage in reversed(range(dims + 1)):
-            group = wave - stage
-            if not 0 <= group < groups:
+            if not 0 <= wave - LAG * stage < len(groups):
                 continue
-            if stage == 1 and group == 0:
-                for copy in locals_:
+            if stage == 1:
+                for copy in waiting:
                     copy.wait()
-            for number in (2 * group, 2 * group + 1):
-                if number >= count:
-                    continue
+                waiting = []
+            for piece in groups[wave - LAG * stage]:
                 if stage > 0:
-                    step(number, stage - 1).wait()
+                    step(piece, stage - 1).wait()
                 if stage < dims:
-                    step(number, stage).start()
+                    step(piece, stage).start()
 
 
 def gather_first(own_a, own_b):
     dims = len(place_bits())
-    cols = own_a.shape[1]
-    width = cols // 8 // 128 * 128
-    cuts = [k * width for k in range(8)] + [cols]
-    pieces = [(1, 0, own_b.shape[1], 0)]
-    pieces += [(0, cuts[k], cuts[k + 1] - cuts[k], (k + 1) % 2) for k in range(8)]
+    rows, cols = own_a.shape
+    groups, number = [[(0, 1, 0, own_b.shape[0], 0, own_b.shape[1], 0)]], 1
+    for base in range(0, cols, GROUP):
+        lanes_here = LANES if base + GROUP <= cols else ((cols - base) // 2,) * 2
+        for row in range(0, rows, PIECE_ROWS):
+            groups.append([])
+            start = base
+            for lane, size in enumerate(lanes_here):
+                groups[-1].append((number, 0, row, PIECE_ROWS, start, size, lane))
+                number, start = number + 1, start + size
     any_space = pl.BlockSpec(memory_space=pl.ANY)
     lead = (2,) * dims
     full_a, full_b = pl.pallas_call(
-        partial(gather_kernel, pieces),
+        partial(gather_kernel, groups),
         in_specs=[any_space, any_space],
         out_specs=[any_space, any_space],
         out_shape=[
@@ -505,9 +558,11 @@
             jax.ShapeDtypeStruct(lead + own_b.shape, own_b.dtype),
         ],
         scratch_shapes=[
+            pltpu.VMEM(own_a.shape, own_a.dtype),
+            pltpu.VMEM(own_b.shape, own_b.dtype),
             pltpu.SemaphoreType.DMA((2,)),
-            pltpu.SemaphoreType.DMA((len(pieces), dims)),
-            pltpu.SemaphoreType.DMA((len(pieces), dims)),
+            pltpu.SemaphoreType.DMA((number, dims)),
+            pltpu.SemaphoreType.DMA((number, dims)),
         ],
         compiler_params=pltpu.CompilerParams(collective_id=0, has_side_effects=True),
         name="gather_first",
@@ -545,9 +600,10 @@
         left = [d for d in range(self.dims) if d not in self.order[:stage]]
         return tuple(value if d == self.order[stage] else slice(None) for d in left)
 
-    def copy(self, stage, src, slot):
+    def copy(self, stage, src, slot, into=()):
+        dst = self.recv[stage].at[slot]
         return remote(
-            src, self.recv[stage].at[slot], self.send.at[stage, slot], self.got.at[stage, slot], self.order[stage]
+            src, dst.at[into] if into else dst, self.send.at[stage, slot], self.got.at[stage, slot], self.order[stage]
         )
 
     def sent_part(self, stage):
@@ -598,7 +654,7 @@
             self.credit_before(0, it)
             self.start_piece(
                 it, self.own.at[slot], self.own_sem.at[slot],
-                lambda src: self.copy(0, src, slot), self.order[0],
+                lambda src, into=(): self.copy(0, src, slot, into), self.order[0],
             )
 
     def finish(self):
@@ -607,98 +663,219 @@
             pltpu.make_async_copy(self.out.at[slot], self.out.at[slot], self.out_sem.at[slot]).wait()
 
 
-def piece_plan(arrays, outs, lane, lanes_used):
+def piece_plan(arrays, lane):
     dims = len(place_bits())
+    width, offset = LANES[lane], sum(LANES[:lane])
     spans, first = [], 0
-    for ref, out, subs, per in arrays:
-        spans.append((ref, out, subs, per, first))
-        first += subs * per
-
-    def at_cols(piece, first_it, per):
-        return pl.ds(pl.multiple_of(((piece - first_it) % per) * (PIECE * lanes_used) + lane * PIECE, PIECE), PIECE)
+    for ref, out, rows, cols in arrays:
+        subs = rows // PIECE_ROWS
+        whole = cols // GROUP * subs
+        spans.append((ref, out, first, whole, lambda n, subs=subs: [
+            (0, width, n % subs * PIECE_ROWS, pl.multiple_of(n // subs * GROUP + offset, 128))
+        ]))
+        first += whole
+        if cols % GROUP:
+            base = cols // GROUP * GROUP
+            if lane < 2:
+                parts = [(0, width, lane * PIECE_ROWS, base)]
+            else:
+                parts = [(k * 128, 128, k * PIECE_ROWS, base + LANES[0]) for k in range(2)]
+            spans.append((ref, out, first, 1, lambda n, parts=parts: parts))
+            first += 1
+
+    def each(piece, act):
+        for ref, out, start, count, parts in spans:
+            @pl.when((piece >= start) & (piece < start + count))
+            def _(ref=ref, out=out, start=start, parts=parts):
+                for col, size, row, at in parts(piece - start):
+                    held = (pl.ds(col, size),)
+                    act(ref, out, held, (pl.ds(pl.multiple_of(row, PIECE_ROWS), PIECE_ROWS), pl.ds(at, size)))
 
     def start(piece, own, own_sem, send, dim):
-        for ref, out, subs, per, first_it in spans:
-            @pl.when((piece >= first_it) & (piece < first_it + subs * per))
-            def _(ref=ref, subs=subs, per=per, first_it=first_it):
-                tail = (slice(None), at_cols(piece, first_it, per))
-                if subs > 1:
-                    tail = ((piece - first_it) // per,) + tail
-                pick = lambda v: ref.at[tuple(v if d == dim else slice(None) for d in range(dims)) + tail]
-                send(pick(1 - bit_of(dim))).start()
-                pltpu.make_async_copy(pick(bit_of(dim)), own, own_sem).start()
+        def act(ref, out, held, at):
+            pick = lambda v: ref.at[tuple(v if d == dim else slice(None) for d in range(dims)) + at]
+            into = (slice(None),) * dims + held
+            send(pick(1 - bit_of(dim)), into).start()
+            pltpu.make_async_copy(pick(bit_of(dim)), own.at[into], own_sem).start()
+
+        each(piece, act)
 
     def end(piece, src, sem):
-        for ref, out, subs, per, first_it in spans:
-            @pl.when((piece >= first_it) & (piece < first_it + subs * per))
-            def _(out=out, subs=subs, per=per, first_it=first_it):
-                at = (slice(None), at_cols(piece, first_it, per))
-                if subs > 1:
-                    at = ((piece - first_it) // per,) + at
-                pltpu.make_async_copy(src, out.at[at], sem).start()
+        each(piece, lambda ref, out, held, at: pltpu.make_async_copy(src.at[(slice(None),) + held], out.at[at], sem).start())
 
     return first, start, end
 
 
-def reduce_kernel(layout, n_in, *refs):
+def make_streams(layout, ins, outs, bufs):
+    size = 2 * len(place_bits()) + 6
+    arrays = [(ins[j], outs[j]) + shape for j, shape in enumerate(layout)]
+    streams = []
+    for lane, order in enumerate(halving_orders()):
+        count, start, end = piece_plan(arrays, lane)
+        streams.append(Stream(order, count, start, end, bufs[lane * size : (lane + 1) * size], BF))
+    return streams
+
+
+def piece_count(layout):
+    return sum(rows // PIECE_ROWS * cols // GROUP for rows, cols in layout)
+
+
+def reduce_views(arrays):
+    lead = (2,) * len(place_bits())
+    views, layout, outs = [], [], []
+    for a in arrays:
+        shape = (a.shape[0] >> len(lead), a.shape[1])
+        views.append(a.reshape(lead + shape))
+        layout.append(shape)
+        outs.append(jax.ShapeDtypeStruct(shape, F32))
+    return views, layout, outs
+
+
+def reduce_buffers():
+    return sum((Stream.buffers(len(place_bits()), PIECE_ROWS, width, BF) for width in LANES), [])
+
+
+class Gather:
+    def __init__(self, shapes, own, full, scratch):
+        self.dims = len(place_bits())
+        self.orders = [list(reversed(order)) for order in halving_orders()]
+        self.own, self.full = own, full
+        self.held, (self.local, self.send, self.recv) = scratch[: len(own)], scratch[len(own) :]
+        self.spans, self.count = [], 0
+        for j, (rows, cols) in enumerate(shapes):
+            subs = rows // PIECE_ROWS
+            self.spans.append((j, self.count, subs, subs * cols // GROUP))
+            self.count += subs * cols // GROUP
+
+    @staticmethod
+    def scratch(shapes):
+        count = sum(rows // PIECE_ROWS * cols // GROUP for rows, cols in shapes)
+        lanes_count, dims = len(LANES), len(place_bits())
+        return [pltpu.VMEM(shape, BF) for shape in shapes] + [
+            pltpu.SemaphoreType.DMA((len(shapes),)),
+            pltpu.SemaphoreType.DMA((lanes_count * count, dims)),
+            pltpu.SemaphoreType.DMA((lanes_count * count, dims)),
+        ]
+
+    def begin(self):
+        greet()
+        for copy in place_own(self.own, self.held, self.full, self.local):
+            copy.wait()
+
+    def copy(self, span, group, lane, stage):
+        j, first, subs, _ = span
+        dim = self.orders[lane][stage]
+        done = self.orders[lane][:stage]
+        col = (group - first) // subs * GROUP + sum(LANES[:lane])
+        rows = pl.ds(pl.multiple_of((group - first) % subs * PIECE_ROWS, PIECE_ROWS), PIECE_ROWS)
+        cols = pl.ds(pl.multiple_of(col, 128), LANES[lane])
+        at = tuple(slice(None) if d in done else bit_of(d) for d in range(self.dims)) + (rows, cols)
+        src = self.own[j].at[rows, cols] if stage == 0 else self.full[j].at[at]
+        number = group * len(LANES) + lane
+        return remote(src, self.full[j].at[at], self.send.at[number, stage], self.recv.at[number, stage], dim)
+
+    def pump(self, wave):
+        for stage in reversed(range(self.dims + 1)):
+            group = wave - LAG * stage
+            for span in self.spans:
+                @pl.when((group >= span[1]) & (group < span[1] + span[3]))
+                def _(stage=stage, group=group, span=span):
+                    for lane in range(len(LANES)):
+                        if stage > 0:
+                            self.copy(span, group, lane, stage - 1).wait()
+                        if stage < self.dims:
+                            self.copy(span, group, lane, stage).start()
+
+
+def input_kernel(layout, *refs):
+    extra = len(layout)
+    dgate_ref, wgate_ref, dproj_ref, wconv_ref, tok_ref, cot_ref, gain_ref = refs[:7]
+    dw = refs[7 : 8 + extra]
+    grad_ref = refs[8 + extra]
+    sums = refs[9 + extra : 10 + 2 * extra]
+    acc = refs[10 + 2 * extra]
+    bufs = refs[11 + 2 * extra :]
+    k = pl.program_id(0)
     dims = len(place_bits())
-    ins, outs, bufs = refs[:n_in], refs[n_in : 2 * n_in], refs[2 * n_in :]
-    size = 2 * dims + 6
-    orders = halving_orders()
-    arrays = [(ins[j], outs[j], subs, per) for j, (subs, per) in enumerate(layout)]
-    streams = []
-    for lane in range(2):
-        count, start, end = piece_plan(arrays, outs, lane, 2)
-        streams.append(Stream(orders[lane], count, start, end, bufs[lane * size : (lane + 1) * size], BF))
+    streams = make_streams(layout, dw[:-1], sums[:-1], bufs)
 
     def start_small(piece, own, own_sem, send, dim):
-        pick = lambda v: ins[-1].at[tuple(v if d == dim else slice(None) for d in range(dims))]
+        pick = lambda v: dw[-1].at[tuple(v if d == dim else slice(None) for d in range(dims))]
         send(pick(1 - bit_of(dim))).start()
         pltpu.make_async_copy(pick(bit_of(dim)), own, own_sem).start()
 
     def end_small(piece, src, sem):
-        pltpu.make_async_copy(src, outs[-1], sem).start()
-
-    small = Stream(orders[0], 1, start_small, end_small, bufs[2 * size :], F32)
-    greet()
-
-    @pl.loop(0, count + dims)
-    def _(it):
+        pltpu.make_async_copy(src, sums[-1], sem).start()
+
+    streams.append(Stream(halving_orders()[0], 1, start_small, end_small, bufs[len(LANES) * (2 * dims + 6) :], F32))
+
+    @pl.when(k == 0)
+    def _():
+        greet()
+        acc[...] = jnp.zeros_like(acc)
+
+    for stream in streams:
+        stream.pump(k)
+
+    def add(left_ref, right_ref):
+        rows, depth = acc.shape[1] // 4, left_ref.shape[1]
+        for n in range(4):
+            at = pl.ds(n * rows, rows)
+            acc[:, at] += dot_nt(left_ref[...], right_ref[at, :])
+
+    pl.when(k < DI // IN_TILE)(lambda: add(dgate_ref, wgate_ref))
+    pl.when(k >= DI // IN_TILE)(lambda: add(dproj_ref, wconv_ref))
+
+    @pl.when(k == pl.num_programs(0) - 1)
+    def _():
+        @pl.loop(0, acc.shape[0] // 64)
+        def _(i):
+            at = pl.ds(pl.multiple_of(i * 64, 64), 64)
+            values = tok_ref[at, :].astype(F32)
+            scale = lax.rsqrt(jnp.mean(values * values, axis=-1, keepdims=True) + EPS)
+            normed = values * scale
+            weighted = acc[at, :] * gain_ref[...]
+            inner = jnp.mean(weighted * normed, axis=-1, keepdims=True)
+            grad_ref[at, :] = (cot_ref[at, :].astype(F32) + scale * (weighted - normed * inner)).astype(BF)
+
         for stream in streams:
-            stream.pump(it)
-        small.pump(it)
-
-    for stream in streams + [small]:
-        stream.finish()
-
-
-def reduce_all(arrays, small):
+            stream.finish()
+
+
+def input_grad_and_reduce(dgate, w_gate, dproj, w_conv, tokens, cotangent, gain, arrays, small):
+    rows, width = tokens.shape
     dims = len(place_bits())
-    lead = (2,) * dims
-    views, layout, outs = [], [], []
-    for a in arrays:
-        rows = a.shape[0] >> dims
-        subs = rows // 64
-        tail = (64, a.shape[1]) if subs == 1 else (subs, 64, a.shape[1])
-        views.append(a.reshape(lead + tail))
-        layout.append((subs, a.shape[1] // (2 * PIECE)))
-        outs.append(jax.ShapeDtypeStruct(tail, F32))
-    views.append(small)
-    outs.append(jax.ShapeDtypeStruct(small.shape[dims:], F32))
+    views, layout, outs = reduce_views(arrays)
+    n_gate, n_conv = DI // IN_TILE, CD // IN_TILE
     any_space = pl.BlockSpec(memory_space=pl.ANY)
-    scratch = Stream.buffers(dims, 64, PIECE, BF) * 2 + Stream.buffers(dims, *small.shape[dims:], F32)
+    gate_at = lambda k: (0, jnp.minimum(k, n_gate - 1))
+    conv_at = lambda k: (0, jnp.maximum(k - n_gate, 0))
+    once = lambda shape: pl.BlockSpec(shape, lambda k: (0, 0), pipeline_mode=pl.Buffered(1))
+    assert n_gate + n_conv >= piece_count(layout) + dims
     got = pl.pallas_call(
-        partial(reduce_kernel, layout, len(views)),
-        in_specs=[any_space] * len(views),
-        out_specs=[any_space] * len(views),
-        out_shape=outs,
-        scratch_shapes=scratch,
+        partial(input_kernel, layout),
+        grid=(n_gate + n_conv,),
+        in_specs=[
+            pl.BlockSpec((rows, IN_TILE), gate_at),
+            pl.BlockSpec((width, IN_TILE), gate_at),
+            pl.BlockSpec((rows, IN_TILE), conv_at),
+            pl.BlockSpec((width, IN_TILE), conv_at),
+            once((rows, width)),
+            once((rows, width)),
+            once((1, width)),
+        ]
+        + [any_space] * (len(views) + 1),
+        out_specs=[once((rows, width))] + [any_space] * (len(views) + 1),
+        out_shape=[jax.ShapeDtypeStruct((rows, width), BF)] + outs + [jax.ShapeDtypeStruct(small.shape[dims:], F32)],
+        scratch_shapes=[pltpu.VMEM((rows, width), F32)]
+        + reduce_buffers()
+        + Stream.buffers(dims, *small.shape[dims:], F32),
         compiler_params=pltpu.CompilerParams(
-            collective_id=1, has_side_effects=True, vmem_limit_bytes=40 * 1024 * 1024
+            dimension_semantics=("arbitrary",), collective_id=1, has_side_effects=True, vmem_limit_bytes=VMEM_LIMIT
         ),
-        name="reduce_all",
-    )(*views)
-    return [g.reshape(-1, g.shape[-1]) for g in got[:-1]] + [got[-1]]
+        name="input_grad",
+    )(dgate, w_gate, dproj, w_conv, tokens, cotangent, gain, *views, small)
+    return got
 
 
 def scatter_sum(part, rows, swap):
@@ -708,10 +885,11 @@
     blocks = part.reshape((2,) * (dp_bits + seq_bits) + (rows, cols))
     left = [("dp", b) for b in reversed(range(dp_bits))] + [("seq", b) for b in reversed(range(seq_bits))]
     seq_order = [("seq", b) for b in range(seq_bits)]
+    dp_order = [("dp", b) for b in range(dp_bits)]
     if swap:
-        order = [("dp", 0), ("dp", 1)] + seq_order + [("dp", b) for b in range(2, dp_bits)]
+        order = dp_order[:2] + seq_order + dp_order[2:]
     else:
-        order = [("dp", 0)] + seq_order + [("dp", b) for b in range(1, dp_bits)]
+        order = dp_order[:1] + seq_order + dp_order[1:]
     for number, (axis, bit) in enumerate(order):
         at = left.index((axis, bit))
         left.pop(at)
@@ -736,9 +914,12 @@
     return lambda n: pl.BlockSpec((height, width), lambda s, c: (at(s, c, n), 0))
 
 
-def params():
+def params(collective=None):
     return pltpu.CompilerParams(
-        dimension_semantics=("arbitrary", "arbitrary"), vmem_limit_bytes=VMEM_LIMIT
+        dimension_semantics=("arbitrary", "arbitrary"),
+        vmem_limit_bytes=VMEM_LIMIT,
+        collective_id=collective,
+        has_side_effects=collective is not None,
     )
 
 
@@ -752,7 +933,7 @@
     in_rows, out_rows = in_weight.shape[0], out_weight.shape[0]
 
     own = conv_bias.shape[0]
-    fast = in_rows % 64 == 0 and out_rows % 64 == 0
+    fast = in_rows == 64 and out_rows == 128
     conv_own = jnp.pad(in_weight[:, DI:], ((0, 0), (0, CD - (PROJ - DI))))
     gate_own = in_weight[:, :DI]
     gains_own = jnp.concatenate([norm_gain, gate_gain, conv_weight.reshape(-1), conv_bias])
@@ -765,8 +946,8 @@
     else:
         w_conv = lax.all_gather(conv_own, BOTH, axis=0, tiled=True)
         gains = lax.all_gather(gains_own, BOTH)
-    w_gate = lax.all_gather(gate_own, BOTH, axis=0, tiled=True)
-    w_out = lax.all_gather(out_weight, BOTH, axis=0, tiled=True)
+        w_gate = lax.all_gather(gate_own, BOTH, axis=0, tiled=True)
+        w_out = lax.all_gather(out_weight, BOTH, axis=0, tiled=True)
     cut = in_rows + out_rows
     norm_full = gains[:, :in_rows].reshape(-1).astype(F32)
     gate_full = gains[:, in_rows:cut].reshape(1, DI).astype(F32)
@@ -784,11 +965,7 @@
     hidden = (values * scale * norm_full[None, :]).astype(BF)
     projected = jnp.dot(hidden, w_conv, preferred_element_type=F32)
     hidden = hidden[:total]
-    gate_part = jnp.dot(hidden, w_gate, preferred_element_type=F32)
     cotangent = out_grad.reshape(total, width)
-    mixed_grad = lax.dot_general(
-        cotangent, w_out, (((1,), (1,)), ((), ())), preferred_element_type=F32
-    )
 
     by_chunk = counts.reshape(seqs, chunks, Q)
     entered = jnp.concatenate([jnp.zeros((seqs, 1), counts.dtype), by_chunk[:, :-1, -1]], axis=1)[:, :, None]
@@ -815,39 +992,54 @@
         pl.BlockSpec((8, H), fixed),
         pl.BlockSpec((2 * H, DI), fixed),
     ]
-    y, act, states, rowp, final = pl.pallas_call(
-        forward_kernel,
+    any_space = pl.BlockSpec(memory_space=pl.ANY)
+    lead = (2,) * len(place_bits())
+    later = [gate_own, out_weight] if fast else []
+    shapes = [a.shape for a in later]
+    assert piece_count(shapes) + LAG * len(lead) <= GATHER_PUMPS * seqs * chunks or not fast
+    y, act, states, rowp, final, *gathered = pl.pallas_call(
+        partial(forward_kernel, shapes),
         grid=grid,
         in_specs=[
             pl.BlockSpec((Q, CD), at_row),
             pl.BlockSpec((8, CD), lambda s, c: (total // 8 + s, 0)),
         ]
-        + common_specs,
+        + common_specs
+        + [any_space] * len(later),
         out_specs=[
             pl.BlockSpec((Q, DI), at_row),
             pl.BlockSpec((Q, XBC), at_row),
             pl.BlockSpec((N, DI), at_row),
             pl.BlockSpec((Q, 256), at_row),
             pl.BlockSpec((N, DI), per_seq),
-        ],
+        ]
+        + [any_space] * len(later),
         out_shape=[
             jax.ShapeDtypeStruct((total, DI), F32),
             jax.ShapeDtypeStruct((total, XBC), BF),
             jax.ShapeDtypeStruct((seqs * chunks * N, DI), BF),
             jax.ShapeDtypeStruct((total, 256), F32),
             jax.ShapeDtypeStruct((seqs * N, DI), BF),
-        ],
+        ]
+        + [jax.ShapeDtypeStruct(lead + a.shape, a.dtype) for a in later],
         scratch_shapes=[
             pltpu.VMEM((136, XBC), F32),
             pltpu.VMEM((N, DI), F32),
             pltpu.VMEM((8, H), F32),
-        ],
-        compiler_params=params(),
+        ]
+        + (Gather.scratch(shapes) if fast else []),
+        compiler_params=params(3 if fast else None),
         name="scan_forward",
-    )(projected, projected, info, infot, cw, hp, spread)
+    )(projected, projected, info, infot, cw, hp, spread, *later)
+    if fast:
+        w_gate, w_out = (g.reshape(-1, g.shape[-1]) for g in gathered)
 
     keep = rowp.reshape(seqs, length, 256)[:, length - 1, 128:192]
     entering = chained(final, keep, 1)
+    gate_part = jnp.dot(hidden, w_gate, preferred_element_type=F32)
+    mixed_grad = lax.dot_general(
+        cotangent, w_out, (((1,), (1,)), ((), ())), preferred_element_type=F32
+    )
 
     mixed, dy, dgate, pdot, dsin, skip_sums = pl.pallas_call(
         gate_kernel,
@@ -896,8 +1088,13 @@
         c == chunks - 1, total // 8 + s, (s * chunks + chunks - 1 - c) * (Q // 8) - 1
     )
     before_row = lambda s, c: jnp.maximum((s * chunks + chunks - 1 - c) * (Q // 8) - 1, 0)
-    dproj, front_grad, conv_sums, head_sums = pl.pallas_call(
-        backward_kernel,
+    views, layout, sum_shapes, reduce_scratch = [], [], [], []
+    if fast:
+        views, layout, sum_shapes = reduce_views([dw_out, dw_gate])
+        reduce_scratch = reduce_buffers()
+        assert piece_count(layout) + len(lead) <= PUMPS * seqs * chunks
+    dproj, front_grad, conv_sums, head_sums, *early = pl.pallas_call(
+        partial(backward_kernel, layout),
         grid=grid,
         in_specs=[
             pl.BlockSpec((Q, CD), back),
@@ -914,19 +1111,22 @@
             pl.BlockSpec((Q, 256), back),
             pl.BlockSpec((8, 256), lambda s, c: (before_row(s, c), 0)),
             pl.BlockSpec((Q, H), back),
-        ],
+        ]
+        + [any_space] * len(views),
         out_specs=[
             pl.BlockSpec((Q, CD), back),
             pl.BlockSpec((8, XBC), per_seq),
             pl.BlockSpec((8, XBC), fixed),
             pl.BlockSpec((8, H), fixed),
-        ],
+        ]
+        + [any_space] * len(views),
         out_shape=[
             jax.ShapeDtypeStruct((total, CD), BF),
             jax.ShapeDtypeStruct((seqs * 8, XBC), F32),
             jax.ShapeDtypeStruct((8, XBC), F32),
             jax.ShapeDtypeStruct((8, H), F32),
-        ],
+        ]
+        + sum_shapes,
         scratch_shapes=[
             pltpu.VMEM((136, XBC), F32),
             pltpu.VMEM((Q, XBC), BF),
@@ -936,11 +1136,11 @@
             pltpu.VMEM((144, XBC), F32),
             pltpu.VMEM((144, XBC), F32),
             pltpu.VMEM((N, DI), F32),
-            pltpu.VMEM((8, H), F32),
-        ],
-        compiler_params=params(),
+        ]
+        + reduce_scratch,
+        compiler_params=params(2 if fast else None),
         name="scan_backward",
-    )(projected, projected, info, infot, cw, hp, spread, dy, states, entering, leaving, rowp, rowp, pdot)
+    )(projected, projected, info, infot, cw, hp, spread, dy, states, entering, leaving, rowp, rowp, pdot, *views)
 
     tail_back = shift_along(front_grad.astype(BF), -1).reshape(seqs, 8, XBC)
     tail_back = jnp.where(tail_mask, tail_back.astype(F32), 0.0)
@@ -949,16 +1149,6 @@
     dproj = lax.dynamic_update_slice(dproj, ends.astype(BF), (0, length - 8, 0)).reshape(total, CD)
 
     dw_conv = dot_tn(hidden, dproj).astype(BF)
-    hidden_grad = lax.dot_general(
-        dgate, w_gate, (((1,), (1,)), ((), ())), preferred_element_type=F32
-    ) + lax.dot_general(dproj, w_conv, (((1,), (1,)), ((), ())), preferred_element_type=F32)
-    scale = scale[:total]
-    normed = values * scale
-    weighted = hidden_grad * norm_full[None, :]
-    input_grad = cotangent.astype(F32) + scale * (
-        weighted - normed * jnp.mean(weighted * normed, axis=-1, keepdims=True)
-    )
-
     skip_grad = jnp.sum(skip_sums[0].reshape(H, HD), axis=1)
     heads = jnp.concatenate([head_sums[0], head_sums[1], skip_grad])
     if fast:
@@ -966,11 +1156,23 @@
         small = jnp.concatenate([shares, jnp.broadcast_to(heads, (shares.shape[0], 3 * H))], axis=1)
         small = jnp.pad(small, ((0, 0), (0, 1024 - small.shape[1])))
         small = small.reshape((2,) * len(place_bits()) + (8, 128))
-        out_weight_grad, gate_cols_grad, conv_cols_grad, small = reduce_all([dw_out, dw_gate, dw_conv], small)
+        input_grad, conv_cols_grad, small = input_grad_and_reduce(
+            dgate, w_gate, dproj, w_conv, tokens.reshape(total, width), cotangent, norm_full[None, :], [dw_conv], small
+        )
+        out_weight_grad, gate_cols_grad = early
         small = small.reshape(-1)
         shares = small[: 5 * own].reshape(5, own)
         heads = small[5 * own : 5 * own + 3 * H]
     else:
+        hidden_grad = lax.dot_general(
+            dgate, w_gate, (((1,), (1,)), ((), ())), preferred_element_type=F32
+        ) + lax.dot_general(dproj, w_conv, (((1,), (1,)), ((), ())), preferred_element_type=F32)
+        scale = scale[:total]
+        normed = values * scale
+        weighted = hidden_grad * norm_full[None, :]
+        input_grad = cotangent.astype(F32) + scale * (
+            weighted - normed * jnp.mean(weighted * normed, axis=-1, keepdims=True)
+        )
         out_weight_grad = scatter_halves(dw_out, out_rows)
         gate_cols_grad = scatter_halves(dw_gate, in_rows)
         conv_cols_grad = scatter_halves(dw_conv, in_rows)

time: 1060 us -> 823 us (0.78)
  Pallas kernels: 737 us -> 575 us
  matrix products: 224 us -> 172 us
  between operations: 14.9 us -> 1.25 us
    pallas_call x4, Pallas kernels: 648 us -> 530 us  [the longest x1 179 us: shards(): pl.pallas_call(partial(backward_kernel, layout), grid=grid, in_specs=[pl....]
    dot_general x2 -> x0, matrix products: 50 us -> none  [the longest x1 26.1 us: shards(): lax.dot_general(dgate, w_gate, (((1,), (1,)), ((), ())), preferred_elemen...]
    pallas_call x1, Pallas kernels: 88.6 us -> 44.9 us  [shards(): pl.pallas_call(gate_kernel, grid=grid, in_specs=[pl.BlockSpec((Q, DI), at...]
  transfers between devices with their start and end apart: 6 -> 4, of which waited for: 1 -> 1; matrix products, arithmetic and copies ran while one was open for 17% -> 14% of each run, Pallas kernels for 25% -> 10%
where the time goes in v3:
time: 823 us; the launch traced here: 815 us
  Pallas kernels  575 us (70%)
  matrix products  172 us (21%)
  other arithmetic  26.3 us (3%)
  local copies, waits for them, and re-layouts  26.1 us (3%)
  starting transfers between devices  9 us (1%)
    pallas_call x1, Pallas kernels, shards(): pl.pallas_call(partial(backward_kernel, layout), grid=grid, in_specs=[pl....  179 us
    pallas_call x1, Pallas kernels, shards(): pl.pallas_call(partial(forward_kernel, shapes), grid=grid, in_specs=[pl.B...  158 us
    pallas_call x1, Pallas kernels, input_grad_and_reduce(): pl.pallas_call(partial(input_kernel, layout), grid=(n_gate + n_conv,), in...  108 us
    pallas_call x1, Pallas kernels, gather_first(): pl.pallas_call(partial(gather_kernel, groups), in_specs=[any_space, any_s...  84.9 us
    dot_general x3, matrix products, dot_tn(): lax.dot_general(a, b, (((0,), (0,)), ((), ())), preferred_element_type=F32)  74.8 us
    pallas_call x1, Pallas kernels, shards(): pl.pallas_call(gate_kernel, grid=grid, in_specs=[pl.BlockSpec((Q, DI), at...  44.9 us
    dot_general x1, matrix products, shards(): projected = jnp.dot(hidden, w_conv, preferred_element_type=F32)  27.5 us
    dot_general x1, matrix products, shards(): jnp.dot(mixed, w_out, preferred_element_type=F32)  24.6 us
  transfers between devices with their start and end apart: 4, of which 1 were waited for; matrix products, arithmetic and copies ran while one was open for 14% of the time, Pallas kernels for 10%

profile of v3, /device:TPU:0, one launch (start us, length us, event | category | flops | bytes accessed | tf_op | source)
XLA Modules:
  0.0 815.0 jit_solution(16011612346508418543)
XLA Ops:
  0.6 0.7 reshape.372
  1.3 0.6 reduce-window.6
  2.0 0.2 slice_reduce_fusion.3
  2.2 0.2 reduce-window.9
  2.4 0.2 slice_reduce_fusion.4
  2.7 0.9 slice_select_fusion
  3.6 4.8 collective-permute-start
  8.5 0.2 slice_reduce_fusion.2
  8.7 0.2 slice_reduce_fusion.1
  9.0 1.1 slice.114
  10.1 0.8 reshape.375
  10.9 0.9 pad.33.own_a
  11.7 1.4 fusion.21.own_b
  13.1 84.9 %gather_first.1 = (bf16[2,2,2,2,2,64,4608]{6,5,4,3,2,1,0:T(8,128)(2,1)}, bf16[2,2,2,2,2,16,128]{6,5,4,3,2,1,0:T(8,128)(2,1)}) custom-call(bf16[64,4608]{1,0:T(8,128)(2,1)} %pad.33.own_a, bf16[16,128]{1,0:T(8,128)(2,1)} %fusion.21.own_b), custom_call_target="tpu_custom_call" | custom-call | tf_op jit(solution)/shard_map/gather_first/pallas_call | solution.py:552
  98.0 0.9 copy.63
  99.1 1.9 slice.123.refs_7_
  101.0 0.7 slice_convert_fusion
  101.7 0.7 reshape.403.refs_6_
  102.6 0.2 copy.47
  103.0 0.1 reshape.378
  103.1 0.1 reshape.379
  103.3 0.8 exponential_bitcast_fusion
  104.1 0.8 pad.38.refs_2_
  105.0 1.2 compare_convert_fusion.refs_6_.spread_ref
  106.2 0.7 maximum_convert_fusion.1.refs_4_
  107.0 1.3 select_maximum_fusion.refs_5_.hp_ref
  108.2 2.7 multiply_reduce_fusion
  111.0 3.6 multiply_convert_fusion
  114.7 27.5 %fusion.23.refs_0_.refs_1_ = f32[1040,4608]{1,0:T(8,128)} fusion(bf16[1040,2048]{1,0:T(8,128)(2,1)S(1)} %multiply_convert_fusion, bf16[2048,4608]{1,0:T(8,128)(2,1)} %bitcast.87), kind=kOutput, calls=%fused_computation.79 | convolution fusion | flops 19629342720 | bytes 42303488 | tf_op jit(solution)/shard_map/dot_general | solution.py:966
  142.1 0.6 broadcast_in_dim.44.refs_3_
  142.7 158.1 %scan_forward.1 = (f32[1024,4096]{1,0:T(8,128)}, bf16[1024,4352]{1,0:T(8,128)(2,1)}, bf16[1024,4096]{1,0:T(8,128)(2,1)}, f32[1024,256]{1,0:T(8,128)}, bf16[256,4...) custom-call(f32[1040,4608]{1,0:T(8,128)} %fusion.23.refs_0_.refs_1_, ...), custom_call_target="tpu_custom_call" | custom-call | tf_op jit(solution)/shard_map/scan_forward/pallas_call | solution.py:1000
  300.9 1.6 collective-permute-start.1
  302.5 24.2 %convolution_bitcast_fusion.mg_ref = f32[1024,4096]{1,0:T(8,128)} fusion(bf16[4096,2048]{1,0:T(8,128)(2,1)} %bitcast.136, bf16[1024,2048]{1,0:T(8,128)(2,1)} %bitcast.102), kind=kOutput, calls=%fused_computation.3 | convolution fusion | flops 17179869184 | bytes 37748736 | tf_op jit(solution)/shard_map/dot_general | solution.py:1040
  326.7 20.9 %fusion.3.gate_ref = f32[1024,4096]{1,0:T(8,128)} fusion(bf16[2048,4096]{1,0:T(8,128)(2,1)S(1)} %bitcast.91, bf16[1040,2048]{1,0:T(8,128)(2,1)S(1)} %bitcast.98), kind=kOutput, calls=%fused_computation.11 | convolution fusion | flops 17179869184 | bytes 37748736 | tf_op jit(solution)/shard_map/dot_general | solution.py:1039
  347.6 4.4 maximum_convert_fusion
  352.1 1.3 copy-done.3
  353.4 44.9 %gate_both.1 = (bf16[1024,4096]{1,0:T(8,128)(2,1)}, bf16[1024,4096]{1,0:T(8,128)(2,1)}, bf16[1024,4096]{1,0:T(8,128)(2,1)}, f32[1024,64]{1,0:T(8,128)}, f32[256,4096]{1,0:T(8,128)}, /*index=5*/f32[8,4096]{1,0:T(8,128)}) custom-call(f32[1024,4096]{1,0:T(8,128)} %get-tuple-element.37.y_ref, bf16[1024,4352]{1,0:T(8,128)(2,1)} %get-tuple-element.38.act_ref, ...), custom_call_target="tpu_custom_call" | custom-call | tf_op jit(solution)/shard_map/gate_both/pallas_call | solution.py:1044
  398.3 24.9 %convolution_convert_fusion.2 = bf16[4096,2048]{1,0:T(8,128)(2,1)} fusion(bf16[1024,4096]{1,0:T(8,128)(2,1)} %get-tuple-element.43, bf16[1024,2048]{1,0:T(8,128)(2,1)} %bitcast.103), kind=kOutput, calls=%fused_computation.2 | convolution fusion | flops 17188257792 | bytes 29360128 | tf_op jit(solution)/shard_map/dot_general | solution.py:45
  423.3 0.3 convert_element_type.216
  423.5 1.3 collective-permute-start.2
  424.8 0.9 slice_reduce_fusion
  425.9 0.1 reduce_sum.37
  426.0 24.6 %fusion = bf16[1024,2048]{1,0:T(8,128)(2,1)} fusion(f32[1040,2048]{1,0:T(8,128)} %maximum_convert_fusion, bf16[1024,4096]{1,0:T(8,128)(2,1)} %get-tuple-element.43, bf16[4096,2048]{1,0:T(8,128)(2,1)} %bitcast.137), kind=kOutput, calls=%fused_computation.7 | convolution fusion | flops 17184063488 | bytes 37748736 | tf_op jit(solution)/shard_map/dot_general | solution.py:1082
  450.6 23.8 %convolution_convert_fusion.1 = bf16[2048,4096]{1,0:T(8,128)(2,1)} fusion(bf16[1024,4096]{1,0:T(8,128)(2,1)} %get-tuple-element.44.refs_0_, bf16[1040,2048]{1,0:T(8,128)(2,1)S(1)} %bitcast.100), kind=kOutput, calls=%fused_computation.1 | convolution fusion | flops 17188257792 | bytes 29360128 | tf_op jit(solution)/shard_map/dot_general | solution.py:45
  474.4 179.1 %scan_backward.1 = (bf16[1024,4608]{1,0:T(8,128)(2,1)}, f32[16,4352]{1,0:T(8,128)}, f32[8,4352]{1,0:T(8,128)}, f32[8,64]{1,0:T(8,128)}, f32[128,2048]{1,0:T(8,128)}, /*index=5*/f32[64,4096]{1,0:T(8,128)}) custom-call(f32[1040,4608]{1,0:T(8,128)} %fusion.23.refs_0_.refs_1_, f32[1040,4608]{1,0:T(8,128)} %fusion.23.refs_0_.refs_1_, f32[1024,128]{1,0:T(8,128)} %pad.38.refs_2_, ...), custom_call_target="tpu_custom_call" | custom-call | tf_op jit(solution)/shard_map/scan_backward/pallas_call | solution.py:1096
  653.6 1.4 multiply_reduce_fusion.2
  655.0 0.8 slice_bitcast_fusion.1
  655.7 1.1 reshape.389
  657.0 0.1 reshape.390
  657.2 0.7 copy.57
  657.9 1.0 convert_element_type.220
  658.9 1.3 collective-permute-start.3
  660.2 0.5 convert_divide_fusion
  660.7 5.1 collective-permute-done.3
  665.8 1.7 fusion.7
  667.5 26.1 %convolution_convert_fusion = bf16[2048,4608]{1,0:T(8,128)(2,1)} fusion(bf16[1024,4608]{1,0:T(8,128)(2,1)} %bitcast.95, bf16[1040,2048]{1,0:T(8,128)(2,1)} %copy-done.5), kind=kOutput, calls=%fused_computation | convolution fusion | flops 19336790016 | bytes 32505856 | tf_op jit(solution)/shard_map/dot_general | solution.py:45
  693.6 108.1 %input_grad.1 = (bf16[1024,2048]{1,0:T(8,128)(2,1)}, f32[64,4608]{1,0:T(8,128)}, f32[8,128]{1,0:T(8,128)}) custom-call(bf16[1024,4096]{1,0:T(8,128)(2,1)} %get-tuple-element.44.refs_0_, bf16[2048,4096]{1,0:T(8,128)(2,1)} %bitcast.90, bf16[1024,4608]{1,0:T(8,128)(2,1)} %bitcast.96, bf16[2048,4608]{1,0:T(8,128)(2,1)} %bitcast.88, bf16[1024,2048]{1,0:T(8,128)(2,1)} %bitcast.84, ...), custom_call_target="tpu_custom_call" | custom-call | tf_op jit(solution)/shard_map/input_grad/pallas_call | solution.py:855
  801.7 1.4 slice.131
  803.1 1.3 slice.134
  804.5 1.8 multiply_reduce_fusion.1
  806.2 1.4 fusion.22
  807.6 1.4 slice.133
  809.0 4.8 copy.69
  813.8 1.0 copy.70
  (67 shorter events, 1.3 us)
Async XLA Ops:
  2.7 6.0 copy-start.10
  3.6 104.6 %collective-permute-start = (bf16[2,8,2048]{2,1,0:T(8,128)(2,1)S(1)}, bf16[2,8,2048]{2,1,0:T(8,128)(2,1)S(1)}, u32[]{:S(2)}, u32[]{:S(2)}) collective-permute-start(bf16[2,8,2048]{2,1,0:T(8,128)(2,1)S(1)} %slice_select_fusion), channel_id=1, source_target_pairs={{0,1},{2,3},{4,5},{6,7},{8,9},{10,11},{12,13},{14,15},{16,17},{18,... | collective-permute-start | bytes 196616 | tf_op jit(solution)/shard_map/ppermute | solution.py:438
  103.3 7.7 copy-start
  114.6 27.5 %copy-start.5 = (bf16[1040,2048]{1,0:T(8,128)(2,1)}, bf16[1040,2048]{1,0:T(8,128)(2,1)S(1)}, u32[]{:S(2)}) copy-start(bf16[1040,2048]{1,0:T(8,128)(2,1)S(1)} %multiply_convert_fusion) | copy-start | bytes 12779524
  142.7 183.9 %slice-start = ((s8[4259840]{0:T(1024)(128)(4,1)}), s8[65536]{0:T(1024)(128)(4,1)S(1)}, s32[]{:S(2)}) async-start(s8[4259840]{0:T(1024)(128)(4,1)} %bitcast.97), calls=%async_computation | async-start | bytes 131072
  300.9 51.1 %collective-permute-start.1 = (bf16[256,4096]{1,0:T(8,128)(2,1)}, bf16[256,4096]{1,0:T(8,128)(2,1)S(1)}, u32[]{:S(2)}, u32[]{:S(2)}) collective-permute-start(bf16[256,4096]{1,0:T(8,128)(2,1)} %get-tuple-element.40), channel_id=1, source_target_pairs={{0,1},{2,3},{4,5},{6,7},{8,9},{10,11},{12,13},{14,15},{16,17},{18,... | collective-permute-start | bytes 6291464 | tf_op jit(solution)/shard_map/ppermute | solution.py:438
  302.5 24.2 %copy-start.2 = (bf16[2,2,2,2,2,64,4096]{6,5,4,3,2,1,0:T(8,128)(2,1)S(1)}, bf16[2,2,2,2,2,64,4096]{6,5,4,3,2,1,0:T(8,128)(2,1)}, u32[]{:S(2)}) copy-start(bf16[2,2,2,2,2,64,4096]{6,5,4,3,2,1,0:T(8,128)(2,1)} %get-tuple-element.41) | copy-start | bytes 50331652
  302.5 24.2 %slice-start.1 = ((s8[4259840]{0:T(1024)(128)(4,1)}), s8[4194304]{0:T(1024)(128)(4,1)S(1)}, s32[]{:S(2)}) async-start(s8[4259840]{0:T(1024)(128)(4,1)} %bitcast.97), calls=%async_computation.1 | async-start | bytes 8388608
  326.7 20.9 %copy-start.1 = (bf16[2,512,2048]{2,1,0:T(8,128)(2,1)S(1)}, bf16[2,512,2048]{2,1,0:T(8,128)(2,1)}, u32[]{:S(2)}) copy-start(bf16[2,512,2048]{2,1,0:T(8,128)(2,1)} %param.12) | copy-start | bytes 12582916
  352.0 1.3 copy-start.3
  398.3 24.9 %copy-start.6 = (f32[256,4096]{1,0:T(8,128)S(1)}, f32[256,4096]{1,0:T(8,128)}, u32[]{:S(2)}) copy-start(f32[256,4096]{1,0:T(8,128)} %get-tuple-element.47) | copy-start | bytes 12582916
  423.3 27.4 %slice-start.2 = ((s8[4259840]{0:T(1024)(128)(4,1)}), s8[65536]{0:T(1024)(128)(4,1)S(1)}, s32[]{:S(2)}) async-start(s8[4259840]{0:T(1024)(128)(4,1)} %bitcast.99), calls=%async_computation.2 | async-start | bytes 131072
  423.5 50.8 %collective-permute-start.2 = (bf16[256,4096]{1,0:T(8,128)(2,1)S(1)}, bf16[256,4096]{1,0:T(8,128)(2,1)}, u32[]{:S(2)}, u32[]{:S(2)}) collective-permute-start(bf16[256,4096]{1,0:T(8,128)(2,1)S(1)} %convert_element_type.216), channel_id=1, source_target_pairs={{1,0},{3,2},{5,4},{7,6},{9,8},{11,10},{13,12},{15,14},{17,16},{19,... | collective-permute-start | bytes 6291464 | tf_op jit(solution)/shard_map/ppermute | solution.py:438
  426.0 24.6 %slice-start.3 = ((s8[4259840]{0:T(1024)(128)(4,1)}), s8[4194304]{0:T(1024)(128)(4,1)S(1)}, s32[]{:S(2)}) async-start(s8[4259840]{0:T(1024)(128)(4,1)} %bitcast.99), calls=%async_computation.3 | async-start | bytes 8388608
  474.4 179.2 %copy-start.8 = (bf16[128,2048]{1,0:T(8,128)(2,1)S(1)}, bf16[128,2048]{1,0:T(8,128)(2,1)}, u32[]{:S(2)}) copy-start(bf16[128,2048]{1,0:T(8,128)(2,1)} %refs_8_.1) | copy-start | bytes 1572868
  474.4 185.8 %copy-start.13 = (bf16[128]{0:T(256)(128)(2,1)S(1)}, bf16[128]{0:T(256)(128)(2,1)}, u32[]{:S(2)}) copy-start(bf16[128]{0:T(256)(128)(2,1)} %param.17) | copy-start | bytes 772
  474.4 191.4 %copy-start.11 = (pred[2,8]{1,0:T(4,128)(4,1)S(1)}, pred[2,8]{1,0:T(4,128)(4,1)}, u32[]{:S(2)}) copy-start(pred[2,8]{1,0:T(4,128)(4,1)} %copy-done.10) | copy-start | bytes 52
  658.9 6.9 collective-permute-start.3
  693.6 110.9 %copy-start.4 = (bf16[64,8512]{1,0:T(8,128)(2,1)S(1)}, bf16[64,8512]{1,0:T(8,128)(2,1)}, u32[]{:S(2)}) copy-start(bf16[64,8512]{1,0:T(8,128)(2,1)} %param.14) | copy-start | bytes 3268612
  693.6 110.9 %copy-start.9 = (f32[64,4096]{1,0:T(8,128)S(1)}, f32[64,4096]{1,0:T(8,128)}, u32[]{:S(2)}) copy-start(f32[64,4096]{1,0:T(8,128)} %get-tuple-element.55) | copy-start | bytes 3145732
  693.6 112.6 %copy-start.12 = (bf16[64]{0:T(256)(128)(2,1)S(1)}, bf16[64]{0:T(256)(128)(2,1)}, u32[]{:S(2)}) copy-start(bf16[64]{0:T(256)(128)(2,1)} %param.15) | copy-start | bytes 388
  801.7 12.1 %copy-start.7 = (f32[128,2048]{1,0:T(8,128)S(1)}, f32[128,2048]{1,0:T(8,128)}, u32[]{:S(2)}) copy-start(f32[128,2048]{1,0:T(8,128)} %get-tuple-element.89) | copy-start | bytes 3145732

commit v4 on v3

--- a/solution.py
+++ b/solution.py
@@ -19,8 +19,8 @@
 GROUP = 1024
 PIECE_ROWS = 32
 LAG = 2
-PUMPS = 3
-GATHER_PUMPS = 4
+PUMPS = 4
+SLOTS = 4
 IN_TILE = 512
 Q = 128
 LB = 256
@@ -103,21 +103,82 @@
     return total, (t0, t1, t2, t3)
 
 
-def forward_kernel(shapes, *refs):
+def forward_kernel(shapes, chunks, before, *refs):
     extra = len(shapes)
-    pc_ref, front_ref, info_ref, infot_ref, cw_ref, hp_ref, spread_ref = refs[:7]
-    own = refs[7 : 7 + extra]
-    y_ref, act_ref, st_ref, row_ref, fin_ref = refs[7 + extra : 12 + extra]
-    full = refs[12 + extra : 12 + 2 * extra]
-    ext, state, pre = refs[12 + 2 * extra : 15 + 2 * extra]
-    chunk = pl.program_id(1)
-    step = pl.program_id(0) * pl.num_programs(1) + chunk
-    pump = lambda place: None
-    if extra:
-        gather = Gather(shapes, own, full, refs[15 + 2 * extra :])
-        pl.when(step == 0)(gather.begin)
-        pump = lambda place: gather.pump(step * GATHER_PUMPS + place)
-    pump(0)
+    i = pl.program_id(0)
+    if not extra:
+        scan_step(i % chunks, chunks, refs[0], refs[1], refs[2:7], refs[7:13], *refs[13:16], lambda place: None)
+        return
+    common, (hid_ref, wconv_ref), own, refs = refs[:5], refs[5:7], refs[7 : 7 + extra], refs[7 + extra :]
+    outputs, proj_ref, full, refs = refs[:6], refs[6], refs[7 : 7 + extra], refs[7 + extra :]
+    (ext, state, pre), (tile, result, rows_in, front_in, moved), refs = refs[:3], refs[3:8], refs[8:]
+    gather = Gather(shapes, own, full, refs)
+    count, cols = proj_ref.shape
+    scans = pl.num_programs(0) - before
+    total = scans * Q
+    left = cols % GROUP or GROUP
+    j = i - before
+
+    def at_cols(n, width):
+        return pl.ds(pl.multiple_of(n * GROUP, GROUP), width)
+
+    def load(n, width):
+        return pltpu.make_async_copy(
+            wconv_ref.at[:, at_cols(n, width)], tile.at[n % 2, :, pl.ds(0, width)], moved.at[n % 2]
+        )
+
+    def store(n, width):
+        return pltpu.make_async_copy(result.at[:, pl.ds(0, width)], proj_ref.at[:, at_cols(n, width)], moved.at[2])
+
+    def fetch(n):
+        return pltpu.make_async_copy(
+            proj_ref.at[pl.ds(pl.multiple_of(n * Q, Q), Q), :], rows_in.at[n % 2], moved.at[3 + n % 2]
+        )
+
+    @pl.when(i == 0)
+    def _():
+        gather.begin()
+        load(0, GROUP).start()
+
+    gather.pump(2 * i)
+
+    def project(width):
+        load(i, width).wait()
+        pl.when(i < before - 2)(lambda: load(i + 1, GROUP).start())
+        pl.when(i == before - 2)(lambda: load(i + 1, left).start())
+        pl.when(i > 0)(lambda: store(i - 1, GROUP).wait())
+        for start in range(0, width, LB):
+            result[:, start : start + LB] = dot(hid_ref[...], tile[i % 2, :, start : start + LB])
+        store(i, width).start()
+
+    pl.when(i < before - 1)(lambda: project(GROUP))
+    pl.when(i == before - 1)(lambda: project(left))
+    pl.when(i < before)(lambda: gather.pump(2 * i + 1))
+
+    @pl.when(j == 0)
+    def _():
+        store(before - 1, left).wait()
+        fetch(0).start()
+
+    @pl.when(j >= 0)
+    def _():
+        fetch(j).wait()
+        pl.when(j + 1 < scans)(lambda: fetch(j + 1).start())
+
+        @pl.when(j % chunks == 0)
+        def _():
+            at = pl.ds(pl.multiple_of(total + j // chunks * 8, 8), 8)
+            copy = pltpu.make_async_copy(proj_ref.at[at, :], front_in, moved.at[5])
+            copy.start()
+            copy.wait()
+
+        pump = lambda place: gather.pump(2 * i + 1) if place == 2 else None
+        scan_step(j % chunks, chunks, rows_in.at[j % 2], front_in, common, outputs, ext, state, pre, pump)
+
+
+def scan_step(chunk, chunks, pc_ref, front_ref, inputs, outputs, ext, state, pre, pump):
+    info_ref, infot_ref, cw_ref, hp_ref, spread_ref = inputs
+    y_ref, act_ref, slope_ref, st_ref, row_ref, fin_ref = outputs
 
     @pl.when(chunk == 0)
     def _():
@@ -137,9 +198,11 @@
     def _(i):
         at = lanes(i)
         out, _ = conv_block(ext, cw_ref, taps, at)
-        act_ref[:, at] = (out * sigmoid(out)).astype(BF)
-
-    pump(1)
+        sig = sigmoid(out)
+        sl = out * sig
+        act_ref[:, at] = sl.astype(BF)
+        slope_ref[:, at] = (sig + sl * (1.0 - sig)).astype(BF)
+
     z = pc_ref[:, XBC : XBC + H] + hp_ref[0:1, :]
     dt = softplus(z)
     decay = -dt * hp_ref[1:2, :]
@@ -180,8 +243,6 @@
     pump(2)
     left, right = pair_masks()
     for p in range(H // 2):
-        if p == H // 4:
-            pump(3)
         weights = []
         for h in (2 * p, 2 * p + 1):
             gap = (cs[:, h : h + 1] - turned[64 + h : 65 + h, :]) + bias
@@ -190,15 +251,15 @@
         blocks = jnp.concatenate([x * left, x * right], axis=0)
         y_ref[:, p * 128 : (p + 1) * 128] += dot(jnp.concatenate(weights, axis=1), blocks)
 
-    @pl.when(chunk == pl.num_programs(1) - 1)
+    @pl.when(chunk == chunks - 1)
     def _():
         fin_ref[...] = state[...].astype(BF)
 
 
 def gate_kernel(
     y_ref, act_ref, row_ref, sin_ref, gate_ref, mg_ref, gain_ref, hp_ref, spread_ref,
-    mixed_ref, dy_ref, dgate_ref, dot_ref, dsin_ref, skip_ref,
-    full, gated,
+    mixed_ref, dy_ref, dgate_ref, dot_ref, leave_ref, skip_ref,
+    full, gated, dsin_ref,
 ):
     chunk = pl.program_id(1)
 
@@ -258,28 +319,59 @@
 
     dot_ref[...] = lax.fori_loop(0, DI // LB, second, jnp.zeros((Q, H), F32), unroll=True)
 
+    @pl.when(chunk == pl.num_programs(1) - 1)
+    def _():
+        leave_ref[...] = dsin_ref[...].astype(BF)
+
 
 def backward_kernel(layout, *refs):
     extra = len(layout)
     pc_ref, halo_ref, info_ref, infot_ref, cw_ref, hp_ref, spread_ref = refs[:7]
-    dy_ref, st_ref, sin_ref, dsin_ref, row_ref, prev_ref, pdot_ref = refs[7:14]
-    dw = refs[14 : 14 + extra]
-    dproj_ref, front_ref, cwg_ref, hg_ref = refs[14 + extra : 18 + extra]
-    sums = refs[18 + extra : 18 + 2 * extra]
-    ext, act, slope, dact, d1, d2, d3, dstate = refs[18 + 2 * extra : 26 + 2 * extra]
+    dy_ref, st_ref, sin_ref, dsin_ref, row_ref, prev_ref, pdot_ref, act, slope = refs[7:16]
+    given, refs = refs[16 : 16 + 3 * min(extra, 1)], refs[16 + 3 * min(extra, 1) :]
+    (dproj_ref, front_ref, cwg_ref, hg_ref), refs = refs[:4], refs[4:]
+    made, sums, refs = refs[: extra // 2], refs[extra // 2 : extra // 2 + extra], refs[extra // 2 + extra :]
+    (ext, dact, ahead, turns, dstate), refs = refs[:5], refs[5:]
     step = pl.program_id(1)
     chunk = pl.num_programs(1) - 1 - step
     number = pl.program_id(0) * pl.num_programs(1) + step
     pump = lambda place: None
     if extra:
-        streams = make_streams(layout, dw, sums, refs[26 + 2 * extra :])
+        hidt_ref, dgate_ref, dw_out = given
+        tile, product, moved = refs[:3]
+        dw_gate = made[0]
+        dims = len(place_bits())
+        every = (slice(None),) * (dims + 1)
+        streams = make_streams(layout, (dw_out, dw_gate), sums, refs[3:])
+        tiles = DI // GROUP
         pl.when(number == 0)(greet)
+
+        def columns(j):
+            return pl.ds(pl.multiple_of(j * GROUP, GROUP), GROUP)
+
+        def load():
+            return pltpu.make_async_copy(dgate_ref.at[:, columns(number)], tile, moved.at[0])
+
+        def store(j):
+            return pltpu.make_async_copy(product, dw_gate.at[every + (columns(j),)], moved.at[1])
 
         def pump(place):
             for stream in streams:
                 stream.pump(number * PUMPS + place)
 
+        pl.when(number < tiles)(lambda: load().start())
+
     pump(0)
+    if extra:
+        @pl.when(number < tiles)
+        def _():
+            load().wait()
+            lead, rows = product.shape[:dims], product.shape[dims]
+            for start in range(0, GROUP, LB):
+                part = dot(hidt_ref[...], tile[:, start : start + LB]).astype(BF)
+                product[every + (slice(start, start + LB),)] = part.reshape(lead + (rows, LB))
+            store(number).start()
+
 
     @pl.when((step == 0) & (pl.program_id(0) == 0))
     def _():
@@ -289,29 +381,16 @@
     @pl.when(step == 0)
     def _():
         dstate[...] = dsin_ref[...].astype(F32)
-        for d in (d1, d2, d3):
-            d[0:8, :] = jnp.zeros((8, XBC), F32)
-            d[136:144, :] = jnp.zeros((8, XBC), F32)
-
-    @pl.when(step > 0)
-    def _():
-        for d in (d1, d2, d3):
-            d[136:144, :] = d[8:16, :]
+        for k in range(3):
+            ahead[k] = jnp.zeros((8, XBC), F32)
+            turns[k, 0:8, :] = jnp.zeros((8, LB), F32)
 
     ext[0:8, :] = halo_ref[:, :XBC]
     ext[8:136, :] = pc_ref[:, :XBC]
     info = info_ref[...]
     taps = [jnp.broadcast_to(info[:, k : k + 1], (Q, LB)) for k in (1, 2, 3)]
 
-    @pl.loop(0, XBC // LB)
-    def _(i):
-        at = lanes(i)
-        out, _ = conv_block(ext, cw_ref, taps, at)
-        sig = sigmoid(out)
-        sl = out * sig
-        act[:, at] = sl.astype(BF)
-        slope[:, at] = sig + sl * (1.0 - sig)
-
+    pump(1)
     cs = row_ref[:, 0:64]
     shifted = row_ref[:, 64:128]
     z = row_ref[:, 192:256]
@@ -357,7 +436,9 @@
     db, dc, rdep, kept = lax.fori_loop(
         0, DI // LB, shared, (zero, zero, jnp.zeros((Q, H), F32), jnp.zeros((16, H), F32)), unroll=True
     )
-    pump(1)
+    if extra:
+        pl.when(number < tiles)(lambda: store(number).wait())
+    pump(2)
     left, right = pair_masks()
     daff = jnp.zeros((Q, Q), F32)
     for p in range(H // 2):
@@ -384,7 +465,7 @@
         return total + head_sum(x * dx, spread[:H])
 
     rfull = lax.fori_loop(0, DI // LB, finish, jnp.zeros((Q, H), F32), unroll=True)
-    pump(2)
+    pump(3)
     daff_low = daff.astype(BF)
     dact[:, DI : DI + N] = db + dot(daff_low, c_proj)
     dact[:, DI + N : XBC] = dc + dot_tn(daff_low, b_proj)
@@ -406,11 +487,12 @@
         at = lanes(i)
         g = dact[:, at] * slope[:, at]
         g1, g2, g3 = taps[0] * g, taps[1] * g, taps[2] * g
-        d1[8:136, at] = g1
-        d2[8:136, at] = g2
-        d3[8:136, at] = g3
+        for k, part in enumerate((g1, g2, g3)):
+            turns[k, 8:136, :] = part
+            turns[k, 136:144, :] = ahead[k, :, at]
+            ahead[k, :, at] = part[0:8]
         w0, w1, w2, w3 = (cw_ref[k : k + 1, at] for k in range(4))
-        total = w3 * g + w2 * d1[9:137, at] + w1 * d2[10:138, at] + w0 * d3[11:139, at]
+        total = w3 * g + w2 * turns[0, 9:137, :] + w1 * turns[1, 10:138, :] + w0 * turns[2, 11:139, :]
         dproj_ref[:, at] = total.astype(BF)
         for k, (grad, shift) in enumerate(((g3, 3), (g2, 2), (g1, 1), (g, 0))):
             cwg_ref[k : k + 1, at] += jnp.sum(
@@ -418,13 +500,9 @@
             )
         cwg_ref[4:5, at] += jnp.sum(g, axis=0, keepdims=True)
 
-    @pl.when(chunk == 0)
-    def _():
-        @pl.loop(0, XBC // LB)
-        def _(i):
-            at = lanes(i)
-            w0, w1, w2 = (cw_ref[k : k + 1, at] for k in range(3))
-            front_ref[:, at] = w2 * d1[1:9, at] + w1 * d2[2:10, at] + w0 * d3[3:11, at]
+        @pl.when(chunk == 0)
+        def _():
+            front_ref[:, at] = w2 * turns[0, 1:9, :] + w1 * turns[1, 2:10, :] + w0 * turns[2, 3:11, :]
 
     if extra:
         @pl.when(number == pl.num_programs(0) * pl.num_programs(1) - 1)
@@ -503,23 +581,72 @@
     return copies
 
 
-def gather_kernel(groups, own_a, own_b, full_a, full_b, held_a, held_b, local, send, recv):
+def first_kernel(
+    groups, tok_ref, tail_ref, own_a, own_b, hid_ref, hidt_ref, full_a, full_b,
+    held_a, held_b, front, gains, gain, scaled, local, send, recv, moved, near,
+):
     dims = len(place_bits())
     orders = [list(reversed(order)) for order in halving_orders()]
     own, full = (own_a, own_b), (full_a, full_b)
     mine = tuple(bit_of(dim) for dim in range(dims))
+    rows = own_a.shape[0]
+    total = tok_ref.shape[0]
+    quarter = total // 128
     greet()
+    tail = remote(tail_ref, front, near.at[0], near.at[1], dims - 1)
+    tail.start()
     waiting = place_own(own, (held_a, held_b), full, local)
 
     def step(piece, stage):
-        number, which, row, rows, start, size, lane = piece
+        number, which, row, count, start, size, lane = piece
         dim = orders[lane][stage]
         done = orders[lane][:stage]
         at = tuple(slice(None) if d in done else mine[d] for d in range(dims))
-        at = at + (pl.ds(row, rows), pl.ds(start, size))
-        src = own[which].at[pl.ds(row, rows), pl.ds(start, size)] if stage == 0 else full[which].at[at]
+        at = at + (pl.ds(row, count), pl.ds(start, size))
+        src = own[which].at[pl.ds(row, count), pl.ds(start, size)] if stage == 0 else full[which].at[at]
         return remote(src, full[which].at[at], send.at[number, stage], recv.at[number, stage], dim)
 
+    def gains_in():
+        load = pltpu.make_async_copy(full_b, gains, moved)
+        load.start()
+        load.wait()
+        for pair in range(1 << (dims - 1)):
+            bits = tuple((pair >> (dims - 2 - k)) & 1 for k in range(dims - 1))
+            both = [gains[bits + (k,)].astype(F32)[0:1, 0:rows] for k in (0, 1)]
+            gain[0:1, pair * 128 : (pair + 1) * 128] = jnp.concatenate(both, axis=1)
+
+    def normed(values):
+        return values * lax.rsqrt(jnp.mean(values * values, axis=-1, keepdims=True) + EPS)
+
+    def norm(part):
+        @pl.loop(part * quarter, (part + 1) * quarter)
+        def _(i):
+            at = pl.ds(pl.multiple_of(i * 32, 32), 32)
+            scaled[at, :] = normed(tok_ref[at, :].astype(F32))
+
+        if part == 3:
+            tail.wait()
+            later = (lax.axis_index("seq") > 0).astype(F32)
+            scaled[total:, :] = normed(front[...].astype(F32) * later)
+
+    def gained(first, last):
+        @pl.loop(first, last)
+        def _(i):
+            at = pl.ds(pl.multiple_of(i * 16, 16), 16)
+            hid_ref[at, :] = (scaled[at, :] * gain[0:1, :]).astype(BF)
+
+    def turn(i):
+        at = pl.ds(i * 128, 128)
+        hidt_ref[:, at] = jnp.transpose(hid_ref[at, :])
+
+    strips = scaled.shape[0] // 16
+    ready = LAG * dims
+    tasks = {wave: [partial(norm, wave)] for wave in range(4)}
+    tasks[ready] = [gains_in]
+    for k in range(4):
+        tasks[ready + 1 + k] = [partial(gained, strips * k // 4, strips * (k + 1) // 4)]
+    for k in range(total // 128):
+        tasks.setdefault(ready + 5 + k // 2, []).append(partial(turn, k))
     for wave in range(len(groups) + LAG * dims):
         for stage in reversed(range(dims + 1)):
             if not 0 <= wave - LAG * stage < len(groups):
@@ -533,41 +660,60 @@
                     step(piece, stage - 1).wait()
                 if stage < dims:
                     step(piece, stage).start()
-
-
-def gather_first(own_a, own_b):
+        for task in tasks.pop(wave, []):
+            task()
+    for wave in sorted(tasks):
+        for task in tasks[wave]:
+            task()
+
+
+def gather_first(own_a, own_b, tokens, tail):
     dims = len(place_bits())
     rows, cols = own_a.shape
+    total, width = tokens.shape
+    count = total + tail.shape[0]
     groups, number = [[(0, 1, 0, own_b.shape[0], 0, own_b.shape[1], 0)]], 1
     for base in range(0, cols, GROUP):
         lanes_here = LANES if base + GROUP <= cols else ((cols - base) // 2,) * 2
         for row in range(0, rows, PIECE_ROWS):
-            groups.append([])
             start = base
+            if number > 1:
+                groups.append([])
             for lane, size in enumerate(lanes_here):
                 groups[-1].append((number, 0, row, PIECE_ROWS, start, size, lane))
                 number, start = number + 1, start + size
     any_space = pl.BlockSpec(memory_space=pl.ANY)
+    whole = pl.BlockSpec(memory_space=pltpu.VMEM)
     lead = (2,) * dims
-    full_a, full_b = pl.pallas_call(
-        partial(gather_kernel, groups),
-        in_specs=[any_space, any_space],
-        out_specs=[any_space, any_space],
+    hidden, hidden_t, full_a, full_b = pl.pallas_call(
+        partial(first_kernel, groups),
+        in_specs=[whole, any_space, any_space, any_space],
+        out_specs=[whole, whole, any_space, any_space],
         out_shape=[
-            jax.ShapeDtypeStruct(lead + own_a.shape, own_a.dtype),
-            jax.ShapeDtypeStruct(lead + own_b.shape, own_b.dtype),
+            jax.ShapeDtypeStruct((count, width), BF),
+            jax.ShapeDtypeStruct((width, total), BF),
+            jax.ShapeDtypeStruct(lead + own_a.shape, BF),
+            jax.ShapeDtypeStruct(lead + own_b.shape, BF),
         ],
         scratch_shapes=[
-            pltpu.VMEM(own_a.shape, own_a.dtype),
-            pltpu.VMEM(own_b.shape, own_b.dtype),
+            pltpu.VMEM(own_a.shape, BF),
+            pltpu.VMEM(own_b.shape, BF),
+            pltpu.VMEM(tail.shape, BF),
+            pltpu.VMEM(lead + own_b.shape, BF),
+            pltpu.VMEM((8, width), F32),
+            pltpu.VMEM((count, width), F32),
             pltpu.SemaphoreType.DMA((2,)),
             pltpu.SemaphoreType.DMA((number, dims)),
             pltpu.SemaphoreType.DMA((number, dims)),
+            pltpu.SemaphoreType.DMA,
+            pltpu.SemaphoreType.DMA((2,)),
         ],
-        compiler_params=pltpu.CompilerParams(collective_id=0, has_side_effects=True),
+        compiler_params=pltpu.CompilerParams(
+            collective_id=0, has_side_effects=True, vmem_limit_bytes=VMEM_LIMIT
+        ),
         name="gather_first",
-    )(own_a, own_b)
-    return full_a.reshape((-1,) + own_a.shape), full_b.reshape((-1,) + own_b.shape)
+    )(tokens, tail, own_a, own_b)
+    return hidden, hidden_t, full_a.reshape(-1, cols), full_b.reshape((-1,) + own_b.shape)
 
 
 class Stream:
@@ -584,13 +730,13 @@
         shape = lambda n: (2,) * n + (rows, cols)
         return (
             [pltpu.VMEM((2,) + shape(dims - 1), dtype)]
-            + [pltpu.VMEM((2,) + shape(dims - 1 - k), dtype) for k in range(dims)]
-            + [pltpu.VMEM(shape(dims - 1 - k), dtype) for k in range(dims - 1)]
+            + [pltpu.VMEM((SLOTS,) + shape(dims - 1 - k), dtype) for k in range(dims)]
+            + [pltpu.VMEM((2,) + shape(dims - 1 - k), dtype) for k in range(dims - 1)]
             + [pltpu.VMEM((2, rows, cols), F32)]
             + [
                 pltpu.SemaphoreType.DMA((2,)),
                 pltpu.SemaphoreType.DMA((dims, 2)),
-                pltpu.SemaphoreType.DMA((dims, 2)),
+                pltpu.SemaphoreType.DMA((dims, SLOTS)),
                 pltpu.SemaphoreType.REGULAR((dims,)),
                 pltpu.SemaphoreType.DMA((2,)),
             ]
@@ -600,48 +746,52 @@
         left = [d for d in range(self.dims) if d not in self.order[:stage]]
         return tuple(value if d == self.order[stage] else slice(None) for d in left)
 
-    def copy(self, stage, src, slot, into=()):
-        dst = self.recv[stage].at[slot]
+    def copy(self, stage, src, piece, into=()):
+        dst = self.recv[stage].at[piece % SLOTS]
         return remote(
-            src, dst.at[into] if into else dst, self.send.at[stage, slot], self.got.at[stage, slot], self.order[stage]
+            src,
+            dst.at[into] if into else dst,
+            self.send.at[stage, piece % 2],
+            self.got.at[stage, piece % SLOTS],
+            self.order[stage],
         )
 
-    def sent_part(self, stage):
-        return self.acc[stage - 1].at[self.half(stage, 1 - bit_of(self.order[stage]))]
+    def sent_part(self, stage, piece):
+        return self.acc[stage - 1].at[(piece % 2,) + self.half(stage, 1 - bit_of(self.order[stage]))]
 
     def credit_before(self, stage, piece):
-        @pl.when(piece >= 2)
+        @pl.when(piece >= SLOTS)
         def _():
             pl.semaphore_wait(self.credit.at[stage], 1)
 
     def pump(self, it):
         dims = self.dims
         for stage in reversed(range(dims)):
-            piece = it - 1 - stage
+            piece = it - LAG * (stage + 1)
 
             @pl.when((piece >= 0) & (piece < self.count))
             def _(stage=stage, piece=piece):
                 slot = piece % 2
                 if stage == 0:
-                    self.copy(0, self.recv[0].at[slot], slot).wait()
+                    self.copy(0, self.recv[0].at[piece % SLOTS], piece).wait()
                     pltpu.make_async_copy(self.own.at[slot], self.own.at[slot], self.own_sem.at[slot]).wait()
                     kept = self.own[slot]
                 else:
-                    self.copy(stage, self.sent_part(stage), slot).wait()
-                    kept = self.acc[stage - 1][self.half(stage, bit_of(self.order[stage]))]
-                total = kept.astype(F32) + self.recv[stage][slot].astype(F32)
+                    self.copy(stage, self.sent_part(stage, piece), piece).wait()
+                    kept = self.acc[stage - 1][(slot,) + self.half(stage, bit_of(self.order[stage]))]
+                got = self.recv[stage][piece % SLOTS]
                 if stage < dims - 1:
-                    self.acc[stage][...] = total.astype(self.dtype)
+                    self.acc[stage][slot] = kept + got
                     self.credit_before(stage + 1, piece)
-                    self.copy(stage + 1, self.sent_part(stage + 1), slot).start()
+                    self.copy(stage + 1, self.sent_part(stage + 1, piece), piece).start()
                 else:
                     @pl.when(piece >= 2)
                     def _():
                         pltpu.make_async_copy(self.out.at[slot], self.out.at[slot], self.out_sem.at[slot]).wait()
-                    self.out[slot] = total
+                    self.out[slot] = kept.astype(F32) + got.astype(F32)
                     self.end_piece(piece, self.out.at[slot], self.out_sem.at[slot])
 
-                @pl.when(piece < self.count - 2)
+                @pl.when(piece < self.count - SLOTS)
                 def _():
                     pl.semaphore_signal(
                         self.credit.at[stage], inc=1, device_id=partner(self.order[stage]),
@@ -654,7 +804,7 @@
             self.credit_before(0, it)
             self.start_piece(
                 it, self.own.at[slot], self.own_sem.at[slot],
-                lambda src, into=(): self.copy(0, src, slot, into), self.order[0],
+                lambda src, into=(): self.copy(0, src, it, into), self.order[0],
             )
 
     def finish(self):
@@ -725,7 +875,7 @@
     views, layout, outs = [], [], []
     for a in arrays:
         shape = (a.shape[0] >> len(lead), a.shape[1])
-        views.append(a.reshape(lead + shape))
+        views.append(a.reshape(lead + shape) if isinstance(a, jax.Array) else None)
         layout.append(shape)
         outs.append(jax.ShapeDtypeStruct(shape, F32))
     return views, layout, outs
@@ -787,25 +937,24 @@
                             self.copy(span, group, lane, stage).start()
 
 
-def input_kernel(layout, *refs):
-    extra = len(layout)
-    dgate_ref, wgate_ref, dproj_ref, wconv_ref, tok_ref, cot_ref, gain_ref = refs[:7]
-    dw = refs[7 : 8 + extra]
-    grad_ref = refs[8 + extra]
-    sums = refs[9 + extra : 10 + 2 * extra]
-    acc = refs[10 + 2 * extra]
-    bufs = refs[11 + 2 * extra :]
+def input_kernel(layout, pump_at, *refs):
+    hidt_ref, dgate_ref, wgate_ref, dproj_ref, wconv_ref, tok_ref, cot_ref, gain_ref, small_ref = refs[:9]
+    grad_ref, dw, conv_sum, small_sum = refs[9:13]
+    acc, product, moved = refs[13:16]
+    bufs = refs[16:]
     k = pl.program_id(0)
     dims = len(place_bits())
-    streams = make_streams(layout, dw[:-1], sums[:-1], bufs)
+    every = (slice(None),) * (dims + 1)
+    streams = make_streams(layout, (dw,), (conv_sum,), bufs)
+    n_conv, n_gate = CD // IN_TILE, DI // IN_TILE
 
     def start_small(piece, own, own_sem, send, dim):
-        pick = lambda v: dw[-1].at[tuple(v if d == dim else slice(None) for d in range(dims))]
+        pick = lambda v: small_ref.at[tuple(v if d == dim else slice(None) for d in range(dims))]
         send(pick(1 - bit_of(dim))).start()
         pltpu.make_async_copy(pick(bit_of(dim)), own, own_sem).start()
 
     def end_small(piece, src, sem):
-        pltpu.make_async_copy(src, sums[-1], sem).start()
+        pltpu.make_async_copy(src, small_sum, sem).start()
 
     streams.append(Stream(halving_orders()[0], 1, start_small, end_small, bufs[len(LANES) * (2 * dims + 6) :], F32))
 
@@ -814,17 +963,42 @@
         greet()
         acc[...] = jnp.zeros_like(acc)
 
-    for stream in streams:
-        stream.pump(k)
-
-    def add(left_ref, right_ref):
-        rows, depth = acc.shape[1] // 4, left_ref.shape[1]
+    def store(j):
+        at = pl.ds(pl.multiple_of(j * IN_TILE, IN_TILE), IN_TILE)
+        return pltpu.make_async_copy(product, dw.at[every + (at,)], moved.at[0])
+
+    @pl.when((k > 0) & (k <= n_conv))
+    def _():
+        store(k - 1).wait()
+
+    def pump(slot):
+        piece = pump_at(slot)
+
+        @pl.when((slot == 0) | ((slot > 0) & (piece != pump_at(slot - 1))))
+        def _():
+            for stream in streams:
+                stream.pump(piece)
+
+    pump(jnp.where(k < n_conv, k - 2, 2 * k - n_conv - 2))
+
+    @pl.when(k < n_conv)
+    def _():
+        for start in range(0, IN_TILE, LB):
+            part = dot(hidt_ref[...], dproj_ref[:, start : start + LB]).astype(BF)
+            product[every + (slice(start, start + LB),)] = part.reshape(product.shape[:-1] + (LB,))
+        store(k).start()
+
+    def add(pairs):
+        rows = acc.shape[1] // 4
         for n in range(4):
+            if n == 2:
+                pump(2 * k - n_conv - 1)
             at = pl.ds(n * rows, rows)
-            acc[:, at] += dot_nt(left_ref[...], right_ref[at, :])
-
-    pl.when(k < DI // IN_TILE)(lambda: add(dgate_ref, wgate_ref))
-    pl.when(k >= DI // IN_TILE)(lambda: add(dproj_ref, wconv_ref))
+            acc[:, at] += sum(dot_nt(left[...], right[at, :]) for left, right in pairs)
+
+    gate_pair, conv_pair = (dgate_ref, wgate_ref), (dproj_ref, wconv_ref)
+    pl.when((k >= n_conv) & (k < n_conv + n_gate))(lambda: add([gate_pair, conv_pair]))
+    pl.when(k >= n_conv + n_gate)(lambda: add([conv_pair]))
 
     @pl.when(k == pl.num_programs(0) - 1)
     def _():
@@ -842,40 +1016,57 @@
             stream.finish()
 
 
-def input_grad_and_reduce(dgate, w_gate, dproj, w_conv, tokens, cotangent, gain, arrays, small):
+def input_grad_and_reduce(hidden_t, dgate, w_gate, dproj, w_conv, tokens, cotangent, gain, small):
     rows, width = tokens.shape
     dims = len(place_bits())
-    views, layout, outs = reduce_views(arrays)
+    in_rows = width >> dims
+    lead = (2,) * dims
+    layout = [(in_rows, CD)]
     n_gate, n_conv = DI // IN_TILE, CD // IN_TILE
+    steps = 2 * n_conv
+    pumps = piece_count(layout) + LAG * dims
+    span = 3 * n_conv - 2
+    pump_at = lambda slot: slot * pumps // span
+    assert pumps <= span and n_conv == n_gate + 1
     any_space = pl.BlockSpec(memory_space=pl.ANY)
-    gate_at = lambda k: (0, jnp.minimum(k, n_gate - 1))
-    conv_at = lambda k: (0, jnp.maximum(k - n_gate, 0))
+    gate_at = lambda k: (0, jnp.clip(k - n_conv, 0, n_gate - 1))
+    conv_at = lambda k: (0, jnp.maximum(k - n_conv, 0))
+    both_at = lambda k: (0, k % n_conv)
     once = lambda shape: pl.BlockSpec(shape, lambda k: (0, 0), pipeline_mode=pl.Buffered(1))
-    assert n_gate + n_conv >= piece_count(layout) + dims
-    got = pl.pallas_call(
-        partial(input_kernel, layout),
-        grid=(n_gate + n_conv,),
+    grad, _, conv_sum, small_sum = pl.pallas_call(
+        partial(input_kernel, layout, pump_at),
+        grid=(steps,),
         in_specs=[
+            once((width, rows)),
             pl.BlockSpec((rows, IN_TILE), gate_at),
             pl.BlockSpec((width, IN_TILE), gate_at),
-            pl.BlockSpec((rows, IN_TILE), conv_at),
+            pl.BlockSpec((rows, IN_TILE), both_at),
             pl.BlockSpec((width, IN_TILE), conv_at),
             once((rows, width)),
             once((rows, width)),
             once((1, width)),
+            any_space,
+        ],
+        out_specs=[once((rows, width))] + [any_space] * 3,
+        out_shape=[
+            jax.ShapeDtypeStruct((rows, width), BF),
+            jax.ShapeDtypeStruct(lead + (in_rows, CD), BF),
+            jax.ShapeDtypeStruct((in_rows, CD), F32),
+            jax.ShapeDtypeStruct(small.shape[dims:], F32),
+        ],
+        scratch_shapes=[
+            pltpu.VMEM((rows, width), F32),
+            pltpu.VMEM(lead + (in_rows, IN_TILE), BF),
+            pltpu.SemaphoreType.DMA((1,)),
         ]
-        + [any_space] * (len(views) + 1),
-        out_specs=[once((rows, width))] + [any_space] * (len(views) + 1),
-        out_shape=[jax.ShapeDtypeStruct((rows, width), BF)] + outs + [jax.ShapeDtypeStruct(small.shape[dims:], F32)],
-        scratch_shapes=[pltpu.VMEM((rows, width), F32)]
         + reduce_buffers()
         + Stream.buffers(dims, *small.shape[dims:], F32),
         compiler_params=pltpu.CompilerParams(
             dimension_semantics=("arbitrary",), collective_id=1, has_side_effects=True, vmem_limit_bytes=VMEM_LIMIT
         ),
         name="input_grad",
-    )(dgate, w_gate, dproj, w_conv, tokens, cotangent, gain, *views, small)
-    return got
+    )(hidden_t, dgate, w_gate, dproj, w_conv, tokens, cotangent, gain, small)
+    return grad, conv_sum, small_sum
 
 
 def scatter_sum(part, rows, swap):
@@ -914,9 +1105,9 @@
     return lambda n: pl.BlockSpec((height, width), lambda s, c: (at(s, c, n), 0))
 
 
-def params(collective=None):
+def params(collective=None, grid_dims=2):
     return pltpu.CompilerParams(
-        dimension_semantics=("arbitrary", "arbitrary"),
+        dimension_semantics=("arbitrary",) * grid_dims,
         vmem_limit_bytes=VMEM_LIMIT,
         collective_id=collective,
         has_side_effects=collective is not None,
@@ -933,15 +1124,20 @@
     in_rows, out_rows = in_weight.shape[0], out_weight.shape[0]
 
     own = conv_bias.shape[0]
-    fast = in_rows == 64 and out_rows == 128
+    fast = in_rows == 64 and out_rows == 128 and lax.axis_size("seq") == 2
     conv_own = jnp.pad(in_weight[:, DI:], ((0, 0), (0, CD - (PROJ - DI))))
     gate_own = in_weight[:, :DI]
     gains_own = jnp.concatenate([norm_gain, gate_gain, conv_weight.reshape(-1), conv_bias])
+    counts = jnp.cumsum(doc_start, axis=1)
+    last = counts[:, length - 1 :]
+    tail_mask = (counts[:, length - 8 :] == last)[:, :, None]
+    tail = jnp.where(tail_mask, tokens[:, length - 8 :], jnp.zeros((), BF))
     if fast:
         used = gains_own.shape[0]
         gains_own = jnp.pad(gains_own, (0, 16 * 128 - used)).reshape(16, 128)
-        w_conv, gains = gather_first(conv_own, gains_own)
-        w_conv = w_conv.reshape(-1, CD)
+        hidden, hidden_t, w_conv, gains = gather_first(
+            conv_own, gains_own, tokens.reshape(total, width), tail.reshape(seqs * 8, width)
+        )
         gains = gains.reshape(-1, 16 * 128)[:, :used]
     else:
         w_conv = lax.all_gather(conv_own, BOTH, axis=0, tiled=True)
@@ -955,16 +1151,13 @@
     bias_full = gains[:, cut + CONV * own :].reshape(1, XBC)
     cw = jnp.concatenate([taps_full, bias_full, jnp.zeros((3, XBC), BF)]).astype(F32)
 
-    counts = jnp.cumsum(doc_start, axis=1)
-    last = counts[:, length - 1 :]
-    tail_mask = (counts[:, length - 8 :] == last)[:, :, None]
-    tail = jnp.where(tail_mask, tokens[:, length - 8 :], jnp.zeros((), BF))
-    front = shift_along(tail, 1)
-    values = jnp.concatenate([tokens.reshape(total, width), front.reshape(seqs * 8, width)]).astype(F32)
-    scale = lax.rsqrt(jnp.mean(values * values, axis=-1, keepdims=True) + EPS)
-    hidden = (values * scale * norm_full[None, :]).astype(BF)
-    projected = jnp.dot(hidden, w_conv, preferred_element_type=F32)
-    hidden = hidden[:total]
+    if not fast:
+        front = shift_along(tail, 1).reshape(seqs * 8, width)
+        values = jnp.concatenate([tokens.reshape(total, width), front]).astype(F32)
+        scale = lax.rsqrt(jnp.mean(values * values, axis=-1, keepdims=True) + EPS)
+        hidden = (values * scale * norm_full[None, :]).astype(BF)
+        projected = jnp.dot(hidden, w_conv, preferred_element_type=F32)
+        hidden = hidden[:total]
     cotangent = out_grad.reshape(total, width)
 
     by_chunk = counts.reshape(seqs, chunks, Q)
@@ -994,49 +1187,68 @@
     ]
     any_space = pl.BlockSpec(memory_space=pl.ANY)
     lead = (2,) * len(place_bits())
-    later = [gate_own, out_weight] if fast else []
-    shapes = [a.shape for a in later]
-    assert piece_count(shapes) + LAG * len(lead) <= GATHER_PUMPS * seqs * chunks or not fast
-    y, act, states, rowp, final, *gathered = pl.pallas_call(
-        partial(forward_kernel, shapes),
-        grid=grid,
-        in_specs=[
-            pl.BlockSpec((Q, CD), at_row),
-            pl.BlockSpec((8, CD), lambda s, c: (total // 8 + s, 0)),
-        ]
-        + common_specs
-        + [any_space] * len(later),
-        out_specs=[
-            pl.BlockSpec((Q, DI), at_row),
-            pl.BlockSpec((Q, XBC), at_row),
-            pl.BlockSpec((N, DI), at_row),
-            pl.BlockSpec((Q, 256), at_row),
-            pl.BlockSpec((N, DI), per_seq),
-        ]
-        + [any_space] * len(later),
-        out_shape=[
-            jax.ShapeDtypeStruct((total, DI), F32),
-            jax.ShapeDtypeStruct((total, XBC), BF),
-            jax.ShapeDtypeStruct((seqs * chunks * N, DI), BF),
-            jax.ShapeDtypeStruct((total, 256), F32),
-            jax.ShapeDtypeStruct((seqs * N, DI), BF),
-        ]
-        + [jax.ShapeDtypeStruct(lead + a.shape, a.dtype) for a in later],
-        scratch_shapes=[
-            pltpu.VMEM((136, XBC), F32),
-            pltpu.VMEM((N, DI), F32),
-            pltpu.VMEM((8, H), F32),
-        ]
-        + (Gather.scratch(shapes) if fast else []),
-        compiler_params=params(3 if fast else None),
+    scan_steps = seqs * chunks
+    once = lambda shape: pl.BlockSpec(shape, lambda *i: (0, 0), pipeline_mode=pl.Buffered(1))
+    later = [out_weight, gate_own] if fast else []
+    shapes = [w.shape for w in later]
+    before = -(-CD // GROUP) if fast else 0
+    at_scan = lambda i: jnp.clip(i - before, 0, scan_steps - 1)
+    now_row = lambda i: (at_scan(i), 0)
+    now_seq = lambda i: (at_scan(i) // chunks, 0)
+    assert not fast or piece_count(shapes) + LAG * len(lead) <= 2 * (before + scan_steps)
+    common_in = [
+        pl.BlockSpec((Q, 128), now_row),
+        pl.BlockSpec((8, Q), lambda i: (0, at_scan(i))),
+        once((8, XBC)),
+        once((8, H)),
+        once((2 * H, DI)),
+    ]
+    common_scratch = [
+        pltpu.VMEM((136, XBC), F32),
+        pltpu.VMEM((N, DI), F32),
+        pltpu.VMEM((8, H), F32),
+    ]
+    scan_out = [(Q, DI, F32), (Q, XBC, BF), (Q, XBC, BF), (N, DI, BF), (Q, 256, F32), (N, DI, BF)]
+    out_specs = [pl.BlockSpec((r, c), now_row) for r, c, _ in scan_out[:-1]] + [pl.BlockSpec((N, DI), now_seq)]
+    out_shapes = [jax.ShapeDtypeStruct((scan_steps * r, c), kind) for r, c, kind in scan_out[:-1]]
+    out_shapes.append(jax.ShapeDtypeStruct((seqs * N, DI), BF))
+    if fast:
+        arguments = [info, infot, cw, hp, spread, hidden, w_conv] + later
+        in_specs = common_in + [once(hidden.shape)] + [any_space] * (1 + len(later))
+        out_specs += [any_space] * (1 + len(later))
+        out_shapes.append(jax.ShapeDtypeStruct((hidden.shape[0], CD), F32))
+        out_shapes += [jax.ShapeDtypeStruct(lead + w.shape, BF) for w in later]
+        scratch = common_scratch + [
+            pltpu.VMEM((2, width, GROUP), BF),
+            pltpu.VMEM((hidden.shape[0], GROUP), F32),
+            pltpu.VMEM((2, Q, CD), F32),
+            pltpu.VMEM((8, CD), F32),
+            pltpu.SemaphoreType.DMA((6,)),
+        ] + Gather.scratch(shapes)
+    else:
+        arguments = [projected, projected, info, infot, cw, hp, spread]
+        in_specs = [
+            pl.BlockSpec((Q, CD), now_row),
+            pl.BlockSpec((8, CD), lambda i: (total // 8 + i // chunks, 0)),
+        ] + common_in
+        scratch = common_scratch
+    y, act, slope, states, rowp, final, *gathered = pl.pallas_call(
+        partial(forward_kernel, shapes, chunks, before),
+        grid=(before + scan_steps,),
+        in_specs=in_specs,
+        out_specs=out_specs,
+        out_shape=out_shapes,
+        scratch_shapes=scratch,
+        compiler_params=params(3 if fast else None, 1),
         name="scan_forward",
-    )(projected, projected, info, infot, cw, hp, spread, *later)
+    )(*arguments)
     if fast:
-        w_gate, w_out = (g.reshape(-1, g.shape[-1]) for g in gathered)
+        projected = gathered[0]
+        w_out, w_gate = (g.reshape(-1, g.shape[-1]) for g in gathered[1:])
 
     keep = rowp.reshape(seqs, length, 256)[:, length - 1, 128:192]
     entering = chained(final, keep, 1)
-    gate_part = jnp.dot(hidden, w_gate, preferred_element_type=F32)
+    gate_part = jnp.dot(hidden[:total], w_gate, preferred_element_type=F32)
     mixed_grad = lax.dot_general(
         cotangent, w_out, (((1,), (1,)), ((), ())), preferred_element_type=F32
     )
@@ -1068,31 +1280,43 @@
             jax.ShapeDtypeStruct((total, DI), BF),
             jax.ShapeDtypeStruct((total, DI), BF),
             jax.ShapeDtypeStruct((total, H), F32),
-            jax.ShapeDtypeStruct((seqs * N, DI), F32),
+            jax.ShapeDtypeStruct((seqs * N, DI), BF),
             jax.ShapeDtypeStruct((8, DI), F32),
         ],
-        scratch_shapes=[pltpu.VMEM((Q, DI), F32), pltpu.VMEM((Q, DI), F32)],
+        scratch_shapes=[pltpu.VMEM((Q, DI), F32), pltpu.VMEM((Q, DI), F32), pltpu.VMEM((N, DI), F32)],
         compiler_params=params(),
         name="gate_both",
     )(y, act, rowp, entering, gate_part, mixed_grad, gate_full, hp, spread)
 
-    leaving = chained(dsin.astype(BF), keep, -1)
-
-    values = values[:total]
+    if fast:
+        half = seqs // 2
+        leaving = shift_along(dsin[: half * N], -1)
+        later, leaving = lax.optimization_barrier((dsin[half * N :], leaving))
+        leaving = jnp.concatenate([leaving, shift_along(later, -1)])
+    else:
+        leaving = chained(dsin, keep, -1)
+
+    values = tokens.reshape(total, width).astype(F32)
     output = (values + jnp.dot(mixed, w_out, preferred_element_type=F32)).astype(BF)
     dw_out = dot_tn(mixed, cotangent).astype(BF)
-    dw_gate = dot_tn(hidden, dgate).astype(BF)
 
     back = lambda s, c: (s * chunks + chunks - 1 - c, 0)
     before = lambda s, c: jnp.where(
         c == chunks - 1, total // 8 + s, (s * chunks + chunks - 1 - c) * (Q // 8) - 1
     )
     before_row = lambda s, c: jnp.maximum((s * chunks + chunks - 1 - c) * (Q // 8) - 1, 0)
-    views, layout, sum_shapes, reduce_scratch = [], [], [], []
+    given, given_specs, layout, early_shapes, reduce_scratch = [], [], [], [], []
     if fast:
-        views, layout, sum_shapes = reduce_views([dw_out, dw_gate])
-        reduce_scratch = reduce_buffers()
-        assert piece_count(layout) + len(lead) <= PUMPS * seqs * chunks
+        views, layout, sum_shapes = reduce_views([dw_out, jax.ShapeDtypeStruct((width, DI), BF)])
+        given = [hidden_t, dgate, views[0]]
+        given_specs = [once((width, total)), any_space, any_space]
+        early_shapes = [jax.ShapeDtypeStruct(lead + (in_rows, DI), BF)] + sum_shapes
+        reduce_scratch = [
+            pltpu.VMEM((total, GROUP), BF),
+            pltpu.VMEM(lead + (in_rows, GROUP), BF),
+            pltpu.SemaphoreType.DMA((2,)),
+        ] + reduce_buffers()
+        assert piece_count(layout) + LAG * len(lead) <= PUMPS * seqs * chunks
     dproj, front_grad, conv_sums, head_sums, *early = pl.pallas_call(
         partial(backward_kernel, layout),
         grid=grid,
@@ -1111,36 +1335,35 @@
             pl.BlockSpec((Q, 256), back),
             pl.BlockSpec((8, 256), lambda s, c: (before_row(s, c), 0)),
             pl.BlockSpec((Q, H), back),
+            pl.BlockSpec((Q, XBC), back),
+            pl.BlockSpec((Q, XBC), back),
         ]
-        + [any_space] * len(views),
+        + given_specs,
         out_specs=[
             pl.BlockSpec((Q, CD), back),
             pl.BlockSpec((8, XBC), per_seq),
             pl.BlockSpec((8, XBC), fixed),
             pl.BlockSpec((8, H), fixed),
         ]
-        + [any_space] * len(views),
+        + [any_space] * len(early_shapes),
         out_shape=[
             jax.ShapeDtypeStruct((total, CD), BF),
             jax.ShapeDtypeStruct((seqs * 8, XBC), F32),
             jax.ShapeDtypeStruct((8, XBC), F32),
             jax.ShapeDtypeStruct((8, H), F32),
         ]
-        + sum_shapes,
+        + early_shapes,
         scratch_shapes=[
             pltpu.VMEM((136, XBC), F32),
-            pltpu.VMEM((Q, XBC), BF),
             pltpu.VMEM((Q, XBC), F32),
-            pltpu.VMEM((Q, XBC), F32),
-            pltpu.VMEM((144, XBC), F32),
-            pltpu.VMEM((144, XBC), F32),
-            pltpu.VMEM((144, XBC), F32),
+            pltpu.VMEM((3, 8, XBC), F32),
+            pltpu.VMEM((3, 144, LB), F32),
             pltpu.VMEM((N, DI), F32),
         ]
         + reduce_scratch,
         compiler_params=params(2 if fast else None),
         name="scan_backward",
-    )(projected, projected, info, infot, cw, hp, spread, dy, states, entering, leaving, rowp, rowp, pdot, *views)
+    )(projected, projected, info, infot, cw, hp, spread, dy, states, entering, leaving, rowp, rowp, pdot, act, slope, *given)
 
     tail_back = shift_along(front_grad.astype(BF), -1).reshape(seqs, 8, XBC)
     tail_back = jnp.where(tail_mask, tail_back.astype(F32), 0.0)
@@ -1148,7 +1371,6 @@
     ends = dproj[:, length - 8 :, :XBC].astype(F32) + tail_back
     dproj = lax.dynamic_update_slice(dproj, ends.astype(BF), (0, length - 8, 0)).reshape(total, CD)
 
-    dw_conv = dot_tn(hidden, dproj).astype(BF)
     skip_grad = jnp.sum(skip_sums[0].reshape(H, HD), axis=1)
     heads = jnp.concatenate([head_sums[0], head_sums[1], skip_grad])
     if fast:
@@ -1157,9 +1379,9 @@
         small = jnp.pad(small, ((0, 0), (0, 1024 - small.shape[1])))
         small = small.reshape((2,) * len(place_bits()) + (8, 128))
         input_grad, conv_cols_grad, small = input_grad_and_reduce(
-            dgate, w_gate, dproj, w_conv, tokens.reshape(total, width), cotangent, norm_full[None, :], [dw_conv], small
+            hidden_t, dgate, w_gate, dproj, w_conv, tokens.reshape(total, width), cotangent, norm_full[None, :], small
         )
-        out_weight_grad, gate_cols_grad = early
+        out_weight_grad, gate_cols_grad = early[1:]
         small = small.reshape(-1)
         shares = small[: 5 * own].reshape(5, own)
         heads = small[5 * own : 5 * own + 3 * H]
@@ -1173,6 +1395,8 @@
         input_grad = cotangent.astype(F32) + scale * (
             weighted - normed * jnp.mean(weighted * normed, axis=-1, keepdims=True)
         )
+        dw_gate = dot_tn(hidden, dgate).astype(BF)
+        dw_conv = dot_tn(hidden, dproj).astype(BF)
         out_weight_grad = scatter_halves(dw_out, out_rows)
         gate_cols_grad = scatter_halves(dw_gate, in_rows)
         conv_cols_grad = scatter_halves(dw_conv, in_rows)

time: 823 us -> 754 us (0.916)
  matrix products: 172 us -> 93.9 us
  Pallas kernels: 575 us -> 602 us
  other arithmetic: 26.3 us -> 16.7 us
    dot_general x3 -> x1, matrix products: 74.8 us -> 23.8 us  [dot_tn(): lax.dot_general(a, b, (((0,), (0,)), ((), ())), preferred_element_type=F32)]
    dot_general x2 -> x1, matrix products: 48.4 us -> 21.8 us  [shards(): gate_part = jnp.dot(hidden[:total], w_gate, preferred_element_type=F32)]
    pallas_call x3, Pallas kernels: 351 us -> 376 us  [the longest x1 161 us: shards(): pl.pallas_call(partial(forward_kernel, shapes, chunks, before), grid=(bef...]
    convert_element_type x3 -> x0, other arithmetic: 8.34 us -> none  [the longest x1 4.42 us: shards(): jnp.concatenate([tokens.reshape(total, width), front.reshape(seqs * 8, wi...]
  transfers between devices with their start and end apart: 4 -> 4, of which waited for: 1 -> 1; matrix products, arithmetic and copies ran while one was open for 14% -> 13% of each run, Pallas kernels for 10% -> 0%
where the time goes in v4:
time: 754 us; the launch traced here: 748 us
  Pallas kernels  602 us (80%)
  matrix products  93.9 us (12%)
  local copies, waits for them, and re-layouts  24.2 us (3%)
  other arithmetic  16.7 us (2%)
    pallas_call x1, Pallas kernels, shards(): pl.pallas_call(partial(backward_kernel, layout), grid=grid, in_specs=[pl....  181 us
    pallas_call x1, Pallas kernels, shards(): pl.pallas_call(partial(forward_kernel, shapes, chunks, before), grid=(bef...  161 us
    pallas_call x1, Pallas kernels, input_grad_and_reduce(): pl.pallas_call(partial(input_kernel, layout, pump_at), grid=(steps,), in_...  122 us
    pallas_call x1, Pallas kernels, gather_first(): pl.pallas_call(partial(first_kernel, groups), in_specs=[whole, any_space,...  93.7 us
    pallas_call x1, Pallas kernels, shards(): pl.pallas_call(gate_kernel, grid=grid, in_specs=[pl.BlockSpec((Q, DI), at...  45.5 us
    dot_general x1, matrix products, shards(): lax.dot_general(cotangent, w_out, (((1,), (1,)), ((), ())), preferred_ele...  24.1 us
    dot_general x1, matrix products, shards(): jnp.dot(mixed, w_out, preferred_element_type=F32)  24.1 us
    dot_general x1, matrix products, dot_tn(): lax.dot_general(a, b, (((0,), (0,)), ((), ())), preferred_element_type=F32)  23.8 us
  transfers between devices with their start and end apart: 4, of which 1 were waited for; matrix products, arithmetic and copies ran while one was open for 13% of the time, Pallas kernels for 0%

profile of v4, /device:TPU:0, one launch (start us, length us, event | category | flops | bytes accessed | tf_op | source)
XLA Modules:
  0.0 748.0 jit_solution(7232420756678826750)
XLA Ops:
  0.7 0.7 reshape.359
  1.4 0.6 reduce-window.6
  2.0 0.2 slice_reduce_fusion.3
  2.2 0.2 reduce-window.9
  2.4 0.2 slice_reduce_fusion.1
  2.7 0.2 slice_reduce_fusion.2
  3.0 0.1 fusion.14
  3.1 1.9 slice.124.refs_8_
  5.0 1.1 slice.121
  6.1 0.8 reshape.362
  6.8 0.1 copy.44
  6.9 0.1 slice_compare_fusion
  7.0 1.6 select_bitcast_fusion.tail_ref
  8.5 0.9 pad.37.own_a
  9.4 1.4 fusion.18.own_b
  10.8 93.7 %gather_first.1 = (bf16[1040,2048]{1,0:T(8,128)(2,1)}, bf16[2048,1024]{1,0:T(8,128)(2,1)}, bf16[2,2,2,2,2,64,4608]{6,5,4,3,2,1,0:T(8,128)(2,1)}, bf16[2,2,2,2,2,16,128]{6,5,4,3,2,1,0:T(8,128)(2,1)}) custom-call(bf16[1024,2048]{1,0:T(8,128)(2,1)} %bitcast.81, bf16[16,2048]{1,0:T(8,128)(2,1)} %select_bitcast_fusion.tail_ref, bf16[64,4608]{1,0:T(8,128)(2,1)} %pad.37.own_a, ...), custom_call_target="tpu_custom_call" | custom-call | tf_op jit(solution)/shard_map/gather_first/pallas_call | solution.py:688
  104.5 0.9 copy.56
  105.5 0.1 slice.148
  105.6 0.1 slice.147
  105.9 0.2 copy.38
  106.1 0.1 reshape.366
  106.2 0.1 reshape.364
  106.4 0.1 reshape.365
  106.6 0.8 pad.36.refs_0_.refs_2_
  107.4 1.2 compare_convert_fusion.refs_4_.spread_ref.refs_6_
  108.7 0.6 select_maximum_fusion.refs_3_.hp_ref.refs_5_
  109.3 0.7 maximum_convert_fusion.refs_2_.refs_4_
  110.0 0.6 broadcast_in_dim.40.refs_1_.refs_3_
  110.6 160.6 %scan_forward.1 = (f32[1024,4096]{1,0:T(8,128)}, bf16[1024,4352]{1,0:T(8,128)(2,1)}, bf16[1024,4352]{1,0:T(8,128)(2,1)}, bf16[1024,4096]{1,0:T(8,128)(2,1)}, f32...) custom-call(f32[1024,128]{1,0:T(8,128)} %pad.36.refs_0_.refs_2_, ...), custom_call_target="tpu_custom_call" | custom-call | tf_op jit(solution)/shard_map/scan_forward/pallas_call | solution.py:1235
  271.2 2.6 collective-permute-start
  273.8 0.7 slice_convert_fusion.1
  274.4 0.7 reshape.388.refs_7_
  275.1 24.1 %convolution_bitcast_fusion.mg_ref = f32[1024,4096]{1,0:T(8,128)} fusion(bf16[4096,2048]{1,0:T(8,128)(2,1)} %bitcast.122, bf16[1024,2048]{1,0:T(8,128)(2,1)} %bitcast.89), kind=kOutput, calls=%fused_computation.1 | convolution fusion | flops 17179869184 | bytes 37748736 | tf_op jit(solution)/shard_map/dot_general | solution.py:1252
  299.2 21.8 %fusion.gate_ref = f32[1024,4096]{1,0:T(8,128)} fusion(bf16[2048,4096]{1,0:T(8,128)(2,1)S(1)} %bitcast.85, bf16[1040,2048]{1,0:T(8,128)(2,1)} %get-tuple-element.42.refs_5_), kind=kOutput, calls=%fused_computation.3 | convolution fusion | flops 17179869184 | bytes 37748736 | tf_op jit(solution)/shard_map/dot_general | solution.py:1251
  321.0 1.3 copy-done.1
  322.4 45.5 %gate_both.1 = (bf16[1024,4096]{1,0:T(8,128)(2,1)}, bf16[1024,4096]{1,0:T(8,128)(2,1)}, bf16[1024,4096]{1,0:T(8,128)(2,1)}, f32[1024,64]{1,0:T(8,128)}, bf16[256,4096]{1,0:T(8,128)(2,1)}, /*index=5*/f32[8,4096]{1,0:T(8,128)}) custom-call(f32[1024,4096]{1,0:T(8,128)} %get-tuple-element.44.y_ref, bf16[1024,4352]{1,0:T(8,128)(2,1)} %get-tuple-element.45.act_ref.refs_14_, ...), custom_call_target="tpu_custom_call" | custom-call | tf_op jit(solution)/shard_map/gate_both/pallas_call | solution.py:1256
  367.9 1.7 fusion.19
  369.6 1.5 collective-permute-start.1
  371.1 24.1 %add_convert_fusion = bf16[1024,2048]{1,0:T(8,128)(2,1)} fusion(bf16[1024,2048]{1,0:T(8,128)(2,1)} %bitcast.82, bf16[1024,4096]{1,0:T(8,128)(2,1)} %get-tuple-element.50, bf16[4096,2048]{1,0:T(8,128)(2,1)} %bitcast.123), kind=kOutput, calls=%fused_computation.2 | convolution fusion | flops 17186160640 | bytes 33554432 | tf_op jit(solution)/shard_map/dot_general | solution.py:1300
  395.2 1.3 collective-permute-start.2
  396.5 23.8 %convolution_convert_fusion = bf16[4096,2048]{1,0:T(8,128)(2,1)} fusion(bf16[1024,4096]{1,0:T(8,128)(2,1)} %get-tuple-element.50, bf16[1024,2048]{1,0:T(8,128)(2,1)S(1)} %bitcast.91), kind=kOutput, calls=%fused_computation | convolution fusion | flops 17188257792 | bytes 29360128 | tf_op jit(solution)/shard_map/dot_general | solution.py:45
  420.4 0.9 slice_reduce_fusion
  421.4 0.1 reduce_sum.27
  421.5 1.5 pad_maximum_fusion.1.refs_10_
  423.0 180.8 %scan_backward.1 = (bf16[1024,4608]{1,0:T(8,128)(2,1)}, f32[16,4352]{1,0:T(8,128)}, f32[8,4352]{1,0:T(8,128)}, f32[8,64]{1,0:T(8,128)}, bf16[2,2,2,2,2,64,4096]{...) custom-call(f32[1040,4608]{1,0:T(8,128)} %get-tuple-element.53.refs_0_.refs_1_, ...), custom_call_target="tpu_custom_call" | custom-call | tf_op jit(solution)/shard_map/scan_backward/pallas_call | solution.py:1320
  603.8 1.4 multiply_reduce_fusion.1
  605.2 0.7 slice_bitcast_fusion.1
  606.0 1.0 convert_element_type.197
  606.9 1.3 collective-permute-start.3
  608.2 1.1 reshape.375
  609.4 0.1 copy.55
  609.5 0.1 reshape.376
  609.7 0.7 copy.50
  610.4 0.5 convert_divide_fusion
  610.9 3.2 collective-permute-done.3
  614.1 1.7 fusion.4
  615.8 121.6 %input_grad.1 = (bf16[1024,2048]{1,0:T(8,128)(2,1)}, bf16[2,2,2,2,2,64,4608]{6,5,4,3,2,1,0:T(8,128)(2,1)}, f32[64,4608]{1,0:T(8,128)}, f32[8,128]{1,0:T(8,128)}) custom-call(bf16[2048,1024]{1,0:T(8,128)(2,1)} %get-tuple-element.51.refs_16_.refs_0_, bf16[1024,4096]{1,0:T(8,128)(2,1)} %get-tuple-element.52.refs_17_.refs_1_, bf16[2048,4096]{1,0:T(8,128)(2,1)} %bitcast.84, ...), custom_call_target="tpu_custom_call" | custom-call | tf_op jit(solution)/shard_map/input_grad/pallas_call | solution.py:1036
  737.5 1.3 slice.138
  738.8 1.4 slice.137
  740.2 1.5 slice.135
  741.7 1.8 multiply_reduce_fusion
  743.5 1.4 fusion.20
  744.9 2.0 copy.62
  746.9 1.0 copy.63
  (53 shorter events, 0.7 us)
Async XLA Ops:
  3.1 102.6 %copy-start.14 = (f32[64]{0:T(128)S(1)}, f32[64]{0:T(128)}, u32[]{:S(2)}) copy-start(f32[64]{0:T(128)} %param.21) | copy-start | bytes 772
  7.0 98.5 %copy-start.8 = (pred[2,8]{1,0:T(4,128)(4,1)}, pred[2,8]{1,0:T(4,128)(4,1)S(1)}, u32[]{:S(2)}) copy-start(pred[2,8]{1,0:T(4,128)(4,1)S(1)} %slice_compare_fusion) | copy-start | bytes 52
  9.4 99.2 %copy-start.11 = (f32[64]{0:T(128)S(1)}, f32[64]{0:T(128)}, u32[]{:S(2)}) copy-start(f32[64]{0:T(128)} %param.22) | copy-start | bytes 772
  9.4 99.2 %copy-start.12 = (f32[64]{0:T(128)S(1)}, f32[64]{0:T(128)}, u32[]{:S(2)}) copy-start(f32[64]{0:T(128)} %param.20) | copy-start | bytes 772
  271.2 49.9 %collective-permute-start = (bf16[256,4096]{1,0:T(8,128)(2,1)}, bf16[256,4096]{1,0:T(8,128)(2,1)S(1)}, u32[]{:S(2)}, u32[]{:S(2)}) collective-permute-start(bf16[256,4096]{1,0:T(8,128)(2,1)} %get-tuple-element.47), channel_id=1, source_target_pairs={{0,1},{2,3},{4,5},{6,7},{8,9},{10,11},{12,13},{14,15},{16,17},{18,... | collective-permute-start | bytes 6291464 | tf_op jit(solution)/shard_map/ppermute | solution.py:516
  275.1 24.1 %copy-start = (bf16[2,2,2,2,2,64,4096]{6,5,4,3,2,1,0:T(8,128)(2,1)S(1)}, bf16[2,2,2,2,2,64,4096]{6,5,4,3,2,1,0:T(8,128)(2,1)}, u32[]{:S(2)}) copy-start(bf16[2,2,2,2,2,64,4096]{6,5,4,3,2,1,0:T(8,128)(2,1)} %get-tuple-element.48) | copy-start | bytes 50331652
  321.0 1.3 copy-start.1
  369.6 25.6 %collective-permute-start.1 = (bf16[128,4096]{1,0:T(8,128)(2,1)S(1)}, bf16[128,4096]{1,0:T(8,128)(2,1)S(1)}, u32[]{:S(2)}, u32[]{:S(2)}) collective-permute-start(bf16[128,4096]{1,0:T(8,128)(2,1)S(1)} %get-tuple-element.75), channel_id=1, source_target_pairs={{1,0},{3,2},{5,4},{7,6},{9,8},{11,10},{13,12},{15,14},{17,16},{19,... | collective-permute-start | bytes 3145736 | tf_op jit(solution)/shard_map/ppermute | solution.py:516
  371.1 25.4 %copy-start.3 = (bf16[2,512,2048]{2,1,0:T(8,128)(2,1)S(1)}, bf16[2,512,2048]{2,1,0:T(8,128)(2,1)}, u32[]{:S(2)}) copy-start(bf16[2,512,2048]{2,1,0:T(8,128)(2,1)} %param.23) | copy-start | bytes 12582916
  395.2 26.3 %collective-permute-start.2 = (bf16[128,4096]{1,0:T(8,128)(2,1)S(1)}, bf16[128,4096]{1,0:T(8,128)(2,1)S(1)}, u32[]{:S(2)}, u32[]{:S(2)}) collective-permute-start(bf16[128,4096]{1,0:T(8,128)(2,1)S(1)} %get-tuple-element.58), channel_id=1, source_target_pairs={{1,0},{3,2},{5,4},{7,6},{9,8},{11,10},{13,12},{15,14},{17,16},{19,... | collective-permute-start | bytes 3145736 | tf_op jit(solution)/shard_map/ppermute | solution.py:516
  423.0 180.8 %copy-start.6 = (bf16[128,2048]{1,0:T(8,128)(2,1)S(1)}, bf16[128,2048]{1,0:T(8,128)(2,1)}, u32[]{:S(2)}) copy-start(bf16[128,2048]{1,0:T(8,128)(2,1)} %refs_7_.1) | copy-start | bytes 1572868
  423.0 187.4 %copy-start.13 = (bf16[128]{0:T(256)(128)(2,1)S(1)}, bf16[128]{0:T(256)(128)(2,1)}, u32[]{:S(2)}) copy-start(bf16[128]{0:T(256)(128)(2,1)} %param.17) | copy-start | bytes 772
  423.0 191.2 %copy-start.9 = (pred[2,8]{1,0:T(4,128)(4,1)S(1)}, pred[2,8]{1,0:T(4,128)(4,1)}, u32[]{:S(2)}) copy-start(pred[2,8]{1,0:T(4,128)(4,1)} %copy-done.8) | copy-start | bytes 52
  606.9 7.2 collective-permute-start.3
  615.8 125.8 %copy-start.2 = (bf16[64,8512]{1,0:T(8,128)(2,1)S(1)}, bf16[64,8512]{1,0:T(8,128)(2,1)}, u32[]{:S(2)}) copy-start(bf16[64,8512]{1,0:T(8,128)(2,1)} %param.14) | copy-start | bytes 3268612
  615.8 125.8 %copy-start.7 = (f32[64,4096]{1,0:T(8,128)S(1)}, f32[64,4096]{1,0:T(8,128)}, u32[]{:S(2)}) copy-start(f32[64,4096]{1,0:T(8,128)} %get-tuple-element.67) | copy-start | bytes 3145732
  737.5 6.0 copy-start.10
  740.2 4.7 copy-start.4
  743.4 3.4 copy-start.5

commit v5 on v4

--- a/solution.py
+++ b/solution.py
@@ -19,6 +19,7 @@
 GROUP = 1024
 PIECE_ROWS = 32
 LAG = 2
+R_LAG = 2
 PUMPS = 4
 SLOTS = 4
 IN_TILE = 512
@@ -64,6 +65,22 @@
 def head_sum(v, spread):
     high, low = two_parts(v)
     return dot_nt(high, spread) + dot_nt(low, spread)
+
+
+def stacked_dot(parts, right):
+    rows = [p.shape[0] for p in parts]
+    out = dot(jnp.concatenate(parts, axis=0), right)
+    cuts = [sum(rows[:k]) for k in range(len(rows) + 1)]
+    return [out[a:b] for a, b in zip(cuts, cuts[1:])]
+
+
+def head_sums(values, spread):
+    parts = [part for v in values for part in two_parts(v)]
+    rows = [p.shape[0] for p in parts]
+    out = dot_nt(jnp.concatenate(parts, axis=0), spread)
+    cuts = [sum(rows[:k]) for k in range(len(rows) + 1)]
+    pieces = [out[a:b] for a, b in zip(cuts, cuts[1:])]
+    return [pieces[k] + pieces[k + 1] for k in range(0, len(pieces), 2)]
 
 
 def sigmoid(v):
@@ -226,19 +243,19 @@
     affinity = dot_nt(c_proj, b_proj)
     in_parts = doubled(inflow)
     out_parts = doubled(outflow)
+    b_turned = jnp.transpose(b_proj)
 
     @pl.loop(0, DI // LB, unroll=DI // LB)
     def _(i):
         at = lanes(i)
         spread = spread_ref[:, at]
-        in_wide = dot(in_parts, spread)
-        out_wide = dot(out_parts, spread)
+        in_wide, out_wide = stacked_dot((in_parts, out_parts), spread)
         held = state[:, at]
         low = held.astype(BF)
         st_ref[:, at] = low
         y_ref[:, at] = dot(c_proj, low) * in_wide
         given = (act_ref[:, at].astype(F32) * out_wide).astype(BF)
-        state[:, at] = held * in_wide[Q - 1 : Q, :] + dot_tn(b_proj, given)
+        state[:, at] = held * in_wide[Q - 1 : Q, :] + dot(b_turned, given)
 
     pump(2)
     left, right = pair_masks()
@@ -259,7 +276,7 @@
 def gate_kernel(
     y_ref, act_ref, row_ref, sin_ref, gate_ref, mg_ref, gain_ref, hp_ref, spread_ref,
     mixed_ref, dy_ref, dgate_ref, dot_ref, leave_ref, skip_ref,
-    full, gated, dsin_ref,
+    full, gated, dsin_ref, flows, skips,
 ):
     chunk = pl.program_id(1)
 
@@ -272,16 +289,19 @@
         skip_ref[...] = jnp.zeros_like(skip_ref)
 
     c_proj = act_ref[:, DI + N : XBC]
+    c_turned = jnp.transpose(c_proj)
     parts = doubled(row_ref[:, 128:192])
     skip_parts = doubled(jnp.broadcast_to(hp_ref[2:3, :], (16, H)))
 
     def first(i, sums):
         at = lanes(i)
         spread = spread_ref[:, at]
-        flow = dot(parts, spread)
+        flow, skip = stacked_dot((parts, skip_parts), spread)
         y = y_ref[:, at] + dot(c_proj, sin_ref[:, at]) * flow
         full[:, at] = y
-        out = y + dot(skip_parts, spread)[0:1, :] * act_ref[:, at].astype(F32)
+        flows[:, at] = flow.astype(BF)
+        skips[:, at] = skip[0:8]
+        out = y + skip[0:1, :] * act_ref[:, at].astype(F32)
         g = gate_ref[:, at]
         v = out * (g * sigmoid(g))
         gated[:, at] = v
@@ -298,10 +318,10 @@
     def second(i, total):
         at = lanes(i)
         spread = spread_ref[:, at]
-        flow = dot(parts, spread)
+        flow = flows[:, at].astype(F32)
         y = full[:, at]
         x = act_ref[:, at].astype(F32)
-        out = y + dot(skip_parts, spread)[0:1, :] * x
+        out = y + skips[0:1, at] * x
         g = gate_ref[:, at]
         sig = sigmoid(g)
         sl = g * sig
@@ -313,9 +333,9 @@
         dy = (grad * sl).astype(BF)
         dy_ref[:, at] = dy
         dyf = dy.astype(F32)
-        dsin_ref[:, at] += dot_tn(c_proj, (dyf * flow).astype(BF))
+        dsin_ref[:, at] += dot(c_turned, (dyf * flow).astype(BF))
         skip_ref[0:1, at] += jnp.sum(dyf * x, axis=0, keepdims=True)
-        return total + head_sum(dyf * y, spread[:H])
+        return total + head_sums((dyf * y,), spread[:H])[0]
 
     dot_ref[...] = lax.fori_loop(0, DI // LB, second, jnp.zeros((Q, H), F32), unroll=True)
 
@@ -352,8 +372,11 @@
         def load():
             return pltpu.make_async_copy(dgate_ref.at[:, columns(number)], tile, moved.at[0])
 
-        def store(j):
-            return pltpu.make_async_copy(product, dw_gate.at[every + (columns(j),)], moved.at[1])
+        def store(j, n):
+            at = pl.ds(pl.multiple_of(j * GROUP + n * LB, LB), LB)
+            return pltpu.make_async_copy(
+                product.at[every + (pl.ds(n * LB, LB),)], dw_gate.at[every + (at,)], moved.at[1 + n]
+            )
 
         def pump(place):
             for stream in streams:
@@ -370,7 +393,7 @@
             for start in range(0, GROUP, LB):
                 part = dot(hidt_ref[...], tile[:, start : start + LB]).astype(BF)
                 product[every + (slice(start, start + LB),)] = part.reshape(lead + (rows, LB))
-            store(number).start()
+                store(number, start // LB).start()
 
 
     @pl.when((step == 0) & (pl.program_id(0) == 0))
@@ -437,7 +460,11 @@
         0, DI // LB, shared, (zero, zero, jnp.zeros((Q, H), F32), jnp.zeros((16, H), F32)), unroll=True
     )
     if extra:
-        pl.when(number < tiles)(lambda: store(number).wait())
+        @pl.when(number < tiles)
+        def _():
+            for n in range(GROUP // LB):
+                store(number, n).wait()
+
     pump(2)
     left, right = pair_masks()
     daff = jnp.zeros((Q, Q), F32)
@@ -767,7 +794,7 @@
     def pump(self, it):
         dims = self.dims
         for stage in reversed(range(dims)):
-            piece = it - LAG * (stage + 1)
+            piece = it - R_LAG * (stage + 1)
 
             @pl.when((piece >= 0) & (piece < self.count))
             def _(stage=stage, piece=piece):
@@ -965,11 +992,11 @@
 
     def store(j):
         at = pl.ds(pl.multiple_of(j * IN_TILE, IN_TILE), IN_TILE)
-        return pltpu.make_async_copy(product, dw.at[every + (at,)], moved.at[0])
-
-    @pl.when((k > 0) & (k <= n_conv))
+        return pltpu.make_async_copy(product.at[j % 2], dw.at[every + (at,)], moved.at[j % 2])
+
+    @pl.when((k > 1) & (k <= n_conv + 1))
     def _():
-        store(k - 1).wait()
+        store(k - 2).wait()
 
     def pump(slot):
         piece = pump_at(slot)
@@ -979,20 +1006,20 @@
             for stream in streams:
                 stream.pump(piece)
 
-    pump(jnp.where(k < n_conv, k - 2, 2 * k - n_conv - 2))
+    pump(jnp.where(k < n_conv, k - 3, 2 * k - n_conv - 3))
 
     @pl.when(k < n_conv)
     def _():
         for start in range(0, IN_TILE, LB):
             part = dot(hidt_ref[...], dproj_ref[:, start : start + LB]).astype(BF)
-            product[every + (slice(start, start + LB),)] = part.reshape(product.shape[:-1] + (LB,))
+            product[(k % 2,) + every + (slice(start, start + LB),)] = part.reshape(product.shape[1:-1] + (LB,))
         store(k).start()
 
     def add(pairs):
         rows = acc.shape[1] // 4
         for n in range(4):
             if n == 2:
-                pump(2 * k - n_conv - 1)
+                pump(2 * k - n_conv - 2)
             at = pl.ds(n * rows, rows)
             acc[:, at] += sum(dot_nt(left[...], right[at, :]) for left, right in pairs)
 
@@ -1024,8 +1051,8 @@
     layout = [(in_rows, CD)]
     n_gate, n_conv = DI // IN_TILE, CD // IN_TILE
     steps = 2 * n_conv
-    pumps = piece_count(layout) + LAG * dims
-    span = 3 * n_conv - 2
+    pumps = piece_count(layout) + R_LAG * dims
+    span = 3 * n_conv - 3
     pump_at = lambda slot: slot * pumps // span
     assert pumps <= span and n_conv == n_gate + 1
     any_space = pl.BlockSpec(memory_space=pl.ANY)
@@ -1056,8 +1083,8 @@
         ],
         scratch_shapes=[
             pltpu.VMEM((rows, width), F32),
-            pltpu.VMEM(lead + (in_rows, IN_TILE), BF),
-            pltpu.SemaphoreType.DMA((1,)),
+            pltpu.VMEM((2,) + lead + (in_rows, IN_TILE), BF),
+            pltpu.SemaphoreType.DMA((2,)),
         ]
         + reduce_buffers()
         + Stream.buffers(dims, *small.shape[dims:], F32),
@@ -1283,7 +1310,13 @@
             jax.ShapeDtypeStruct((seqs * N, DI), BF),
             jax.ShapeDtypeStruct((8, DI), F32),
         ],
-        scratch_shapes=[pltpu.VMEM((Q, DI), F32), pltpu.VMEM((Q, DI), F32), pltpu.VMEM((N, DI), F32)],
+        scratch_shapes=[
+            pltpu.VMEM((Q, DI), F32),
+            pltpu.VMEM((Q, DI), F32),
+            pltpu.VMEM((N, DI), F32),
+            pltpu.VMEM((Q, DI), BF),
+            pltpu.VMEM((8, DI), F32),
+        ],
         compiler_params=params(),
         name="gate_both",
     )(y, act, rowp, entering, gate_part, mixed_grad, gate_full, hp, spread)
@@ -1314,9 +1347,9 @@
         reduce_scratch = [
             pltpu.VMEM((total, GROUP), BF),
             pltpu.VMEM(lead + (in_rows, GROUP), BF),
-            pltpu.SemaphoreType.DMA((2,)),
+            pltpu.SemaphoreType.DMA((1 + GROUP // LB,)),
         ] + reduce_buffers()
-        assert piece_count(layout) + LAG * len(lead) <= PUMPS * seqs * chunks
+        assert piece_count(layout) + R_LAG * len(lead) <= PUMPS * seqs * chunks
     dproj, front_grad, conv_sums, head_sums, *early = pl.pallas_call(
         partial(backward_kernel, layout),
         grid=grid,

time: 754 us -> 736 us (0.976)
  Pallas kernels: 602 us -> 585 us
    pallas_call x1, Pallas kernels: 122 us -> 113 us  [input_grad_and_reduce(): pl.pallas_call(partial(input_kernel, layout, pump_at), grid=(steps,), in_...]
  transfers between devices with their start and end apart: 4 -> 4, of which waited for: 1 -> 1; matrix products, arithmetic and copies ran while one was open for 13% -> 14% of each run, Pallas kernels for 0% -> 0%
where the time goes in v5:
time: 736 us; the launch traced here: 730 us
  Pallas kernels  585 us (79%)
  matrix products  93.7 us (13%)
  local copies, waits for them, and re-layouts  24.2 us (3%)
  other arithmetic  16.7 us (2%)
    pallas_call x1, Pallas kernels, shards(): pl.pallas_call(partial(backward_kernel, layout), grid=grid, in_specs=[pl....  182 us
    pallas_call x1, Pallas kernels, shards(): pl.pallas_call(partial(forward_kernel, shapes, chunks, before), grid=(bef...  156 us
    pallas_call x1, Pallas kernels, input_grad_and_reduce(): pl.pallas_call(partial(input_kernel, layout, pump_at), grid=(steps,), in_...  113 us
    pallas_call x1, Pallas kernels, gather_first(): pl.pallas_call(partial(first_kernel, groups), in_specs=[whole, any_space,...  93.7 us
    pallas_call x1, Pallas kernels, shards(): pl.pallas_call(gate_kernel, grid=grid, in_specs=[pl.BlockSpec((Q, DI), at...  41.3 us
    dot_general x1, matrix products, shards(): jnp.dot(mixed, w_out, preferred_element_type=F32)  24.1 us
    dot_general x1, matrix products, shards(): lax.dot_general(cotangent, w_out, (((1,), (1,)), ((), ())), preferred_ele...  23.9 us
    dot_general x1, matrix products, dot_tn(): lax.dot_general(a, b, (((0,), (0,)), ((), ())), preferred_element_type=F32)  23.8 us
  transfers between devices with their start and end apart: 4, of which 1 were waited for; matrix products, arithmetic and copies ran while one was open for 14% of the time, Pallas kernels for 0%

profile of v5, /device:TPU:0, one launch (start us, length us, event | category | flops | bytes accessed | tf_op | source)
XLA Modules:
  0.0 730.2 jit_solution(14373649001539162609)
XLA Ops:
  0.7 0.7 reshape.359
  1.4 0.6 reduce-window.6
  2.0 0.2 slice_reduce_fusion.3
  2.2 0.2 reduce-window.9
  2.4 0.2 slice_reduce_fusion.1
  2.7 0.2 slice_reduce_fusion.2
  3.0 0.1 fusion.14
  3.1 1.9 slice.124.refs_8_
  5.0 1.1 slice.121
  6.1 0.8 reshape.362
  6.8 0.1 copy.44
  6.9 0.1 slice_compare_fusion
  7.0 1.6 select_bitcast_fusion.tail_ref
  8.5 0.9 pad.37.own_a
  9.4 1.4 fusion.18.own_b
  10.8 93.7 %gather_first.1 = (bf16[1040,2048]{1,0:T(8,128)(2,1)}, bf16[2048,1024]{1,0:T(8,128)(2,1)}, bf16[2,2,2,2,2,64,4608]{6,5,4,3,2,1,0:T(8,128)(2,1)}, bf16[2,2,2,2,2,16,128]{6,5,4,3,2,1,0:T(8,128)(2,1)}) custom-call(bf16[1024,2048]{1,0:T(8,128)(2,1)} %bitcast.81, bf16[16,2048]{1,0:T(8,128)(2,1)} %select_bitcast_fusion.tail_ref, bf16[64,4608]{1,0:T(8,128)(2,1)} %pad.37.own_a, ...), custom_call_target="tpu_custom_call" | custom-call | tf_op jit(solution)/shard_map/gather_first/pallas_call | solution.py:715
  104.5 0.9 copy.56
  105.5 0.1 slice.148
  105.6 0.1 slice.147
  105.9 0.2 copy.38
  106.1 0.1 reshape.366
  106.2 0.1 reshape.364
  106.4 0.1 reshape.365
  106.6 0.8 pad.36.refs_0_.refs_2_
  107.4 1.2 compare_convert_fusion.refs_4_.spread_ref.refs_6_
  108.7 0.6 select_maximum_fusion.refs_3_.hp_ref.refs_5_
  109.3 0.7 maximum_convert_fusion.refs_2_.refs_4_
  110.0 0.6 broadcast_in_dim.40.refs_1_.refs_3_
  110.6 155.6 %scan_forward.1 = (f32[1024,4096]{1,0:T(8,128)}, bf16[1024,4352]{1,0:T(8,128)(2,1)}, bf16[1024,4352]{1,0:T(8,128)(2,1)}, bf16[1024,4096]{1,0:T(8,128)(2,1)}, f32...) custom-call(f32[1024,128]{1,0:T(8,128)} %pad.36.refs_0_.refs_2_, ...), custom_call_target="tpu_custom_call" | custom-call | tf_op jit(solution)/shard_map/scan_forward/pallas_call | solution.py:1262
  266.3 2.6 collective-permute-start
  268.9 0.7 slice_convert_fusion.1
  269.5 0.7 reshape.388.refs_7_
  270.2 23.9 %convolution_bitcast_fusion.mg_ref = f32[1024,4096]{1,0:T(8,128)} fusion(bf16[4096,2048]{1,0:T(8,128)(2,1)} %bitcast.122, bf16[1024,2048]{1,0:T(8,128)(2,1)} %bitcast.89), kind=kOutput, calls=%fused_computation.1 | convolution fusion | flops 17179869184 | bytes 37748736 | tf_op jit(solution)/shard_map/dot_general | solution.py:1279
  294.1 21.8 %fusion.gate_ref = f32[1024,4096]{1,0:T(8,128)} fusion(bf16[2048,4096]{1,0:T(8,128)(2,1)S(1)} %bitcast.85, bf16[1040,2048]{1,0:T(8,128)(2,1)} %get-tuple-element.42.refs_5_), kind=kOutput, calls=%fused_computation.3 | convolution fusion | flops 17179869184 | bytes 37748736 | tf_op jit(solution)/shard_map/dot_general | solution.py:1278
  315.9 1.3 copy-done.1
  317.2 41.3 %gate_both.1 = (bf16[1024,4096]{1,0:T(8,128)(2,1)}, bf16[1024,4096]{1,0:T(8,128)(2,1)}, bf16[1024,4096]{1,0:T(8,128)(2,1)}, f32[1024,64]{1,0:T(8,128)}, bf16[256,4096]{1,0:T(8,128)(2,1)}, /*index=5*/f32[8,4096]{1,0:T(8,128)}) custom-call(f32[1024,4096]{1,0:T(8,128)} %get-tuple-element.44.y_ref, bf16[1024,4352]{1,0:T(8,128)(2,1)} %get-tuple-element.45.act_ref.refs_14_, ...), custom_call_target="tpu_custom_call" | custom-call | tf_op jit(solution)/shard_map/gate_both/pallas_call | solution.py:1283
  358.6 1.7 fusion.19
  360.3 1.3 collective-permute-start.1
  361.6 24.1 %add_convert_fusion = bf16[1024,2048]{1,0:T(8,128)(2,1)} fusion(bf16[1024,2048]{1,0:T(8,128)(2,1)} %bitcast.82, bf16[1024,4096]{1,0:T(8,128)(2,1)} %get-tuple-element.50, bf16[4096,2048]{1,0:T(8,128)(2,1)} %bitcast.123), kind=kOutput, calls=%fused_computation.2 | convolution fusion | flops 17186160640 | bytes 33554432 | tf_op jit(solution)/shard_map/dot_general | solution.py:1333
  385.7 1.3 collective-permute-start.2
  387.0 23.8 %convolution_convert_fusion = bf16[4096,2048]{1,0:T(8,128)(2,1)} fusion(bf16[1024,4096]{1,0:T(8,128)(2,1)} %get-tuple-element.50, bf16[1024,2048]{1,0:T(8,128)(2,1)S(1)} %bitcast.91), kind=kOutput, calls=%fused_computation | convolution fusion | flops 17188257792 | bytes 29360128 | tf_op jit(solution)/shard_map/dot_general | solution.py:46
  410.9 0.9 slice_reduce_fusion
  411.9 0.1 reduce_sum.27
  412.0 1.5 pad_maximum_fusion.1.refs_10_
  413.5 181.7 %scan_backward.1 = (bf16[1024,4608]{1,0:T(8,128)(2,1)}, f32[16,4352]{1,0:T(8,128)}, f32[8,4352]{1,0:T(8,128)}, f32[8,64]{1,0:T(8,128)}, bf16[2,2,2,2,2,64,4096]{...) custom-call(f32[1040,4608]{1,0:T(8,128)} %get-tuple-element.53.refs_0_.refs_1_, ...), custom_call_target="tpu_custom_call" | custom-call | tf_op jit(solution)/shard_map/scan_backward/pallas_call | solution.py:1353
  595.2 1.4 multiply_reduce_fusion.1
  596.6 0.7 slice_bitcast_fusion.1
  597.4 1.0 convert_element_type.197
  598.3 1.3 collective-permute-start.3
  599.6 1.1 reshape.375
  600.8 0.1 copy.55
  600.9 0.1 reshape.376
  601.1 0.7 copy.50
  601.8 0.5 convert_divide_fusion
  602.3 3.1 collective-permute-done.3
  605.4 1.7 fusion.4
  607.1 112.6 %input_grad.1 = (bf16[1024,2048]{1,0:T(8,128)(2,1)}, bf16[2,2,2,2,2,64,4608]{6,5,4,3,2,1,0:T(8,128)(2,1)}, f32[64,4608]{1,0:T(8,128)}, f32[8,128]{1,0:T(8,128)}) custom-call(bf16[2048,1024]{1,0:T(8,128)(2,1)} %get-tuple-element.51.refs_16_.refs_0_, bf16[1024,4096]{1,0:T(8,128)(2,1)} %get-tuple-element.52.refs_17_.refs_1_, bf16[2048,4096]{1,0:T(8,128)(2,1)} %bitcast.84, ...), custom_call_target="tpu_custom_call" | custom-call | tf_op jit(solution)/shard_map/input_grad/pallas_call | solution.py:1063
  719.7 1.3 slice.138
  721.0 1.4 slice.137
  722.3 1.5 slice.135
  723.8 1.8 multiply_reduce_fusion
  725.6 1.4 fusion.20
  727.0 2.0 copy.62
  729.0 1.0 copy.63
  (53 shorter events, 0.7 us)
Async XLA Ops:
  3.1 102.6 %copy-start.14 = (f32[64]{0:T(128)S(1)}, f32[64]{0:T(128)}, u32[]{:S(2)}) copy-start(f32[64]{0:T(128)} %param.21) | copy-start | bytes 772
  7.0 98.5 %copy-start.8 = (pred[2,8]{1,0:T(4,128)(4,1)}, pred[2,8]{1,0:T(4,128)(4,1)S(1)}, u32[]{:S(2)}) copy-start(pred[2,8]{1,0:T(4,128)(4,1)S(1)} %slice_compare_fusion) | copy-start | bytes 52
  9.4 99.2 %copy-start.11 = (f32[64]{0:T(128)S(1)}, f32[64]{0:T(128)}, u32[]{:S(2)}) copy-start(f32[64]{0:T(128)} %param.22) | copy-start | bytes 772
  9.4 99.2 %copy-start.12 = (f32[64]{0:T(128)S(1)}, f32[64]{0:T(128)}, u32[]{:S(2)}) copy-start(f32[64]{0:T(128)} %param.20) | copy-start | bytes 772
  266.3 49.6 %collective-permute-start = (bf16[256,4096]{1,0:T(8,128)(2,1)}, bf16[256,4096]{1,0:T(8,128)(2,1)S(1)}, u32[]{:S(2)}, u32[]{:S(2)}) collective-permute-start(bf16[256,4096]{1,0:T(8,128)(2,1)} %get-tuple-element.47), channel_id=1, source_target_pairs={{0,1},{2,3},{4,5},{6,7},{8,9},{10,11},{12,13},{14,15},{16,17},{18,... | collective-permute-start | bytes 6291464 | tf_op jit(solution)/shard_map/ppermute | solution.py:543
  270.2 23.9 %copy-start = (bf16[2,2,2,2,2,64,4096]{6,5,4,3,2,1,0:T(8,128)(2,1)S(1)}, bf16[2,2,2,2,2,64,4096]{6,5,4,3,2,1,0:T(8,128)(2,1)}, u32[]{:S(2)}) copy-start(bf16[2,2,2,2,2,64,4096]{6,5,4,3,2,1,0:T(8,128)(2,1)} %get-tuple-element.48) | copy-start | bytes 50331652
  315.9 1.3 copy-start.1
  360.3 25.5 %collective-permute-start.1 = (bf16[128,4096]{1,0:T(8,128)(2,1)S(1)}, bf16[128,4096]{1,0:T(8,128)(2,1)S(1)}, u32[]{:S(2)}, u32[]{:S(2)}) collective-permute-start(bf16[128,4096]{1,0:T(8,128)(2,1)S(1)} %get-tuple-element.75), channel_id=1, source_target_pairs={{1,0},{3,2},{5,4},{7,6},{9,8},{11,10},{13,12},{15,14},{17,16},{19,... | collective-permute-start | bytes 3145736 | tf_op jit(solution)/shard_map/ppermute | solution.py:543
  361.6 25.4 %copy-start.3 = (bf16[2,512,2048]{2,1,0:T(8,128)(2,1)S(1)}, bf16[2,512,2048]{2,1,0:T(8,128)(2,1)}, u32[]{:S(2)}) copy-start(bf16[2,512,2048]{2,1,0:T(8,128)(2,1)} %param.23) | copy-start | bytes 12582916
  385.7 26.3 %collective-permute-start.2 = (bf16[128,4096]{1,0:T(8,128)(2,1)S(1)}, bf16[128,4096]{1,0:T(8,128)(2,1)S(1)}, u32[]{:S(2)}, u32[]{:S(2)}) collective-permute-start(bf16[128,4096]{1,0:T(8,128)(2,1)S(1)} %get-tuple-element.58), channel_id=1, source_target_pairs={{1,0},{3,2},{5,4},{7,6},{9,8},{11,10},{13,12},{15,14},{17,16},{19,... | collective-permute-start | bytes 3145736 | tf_op jit(solution)/shard_map/ppermute | solution.py:543
  413.5 181.7 %copy-start.6 = (bf16[128,2048]{1,0:T(8,128)(2,1)S(1)}, bf16[128,2048]{1,0:T(8,128)(2,1)}, u32[]{:S(2)}) copy-start(bf16[128,2048]{1,0:T(8,128)(2,1)} %refs_7_.1) | copy-start | bytes 1572868
  413.5 188.3 %copy-start.13 = (bf16[128]{0:T(256)(128)(2,1)S(1)}, bf16[128]{0:T(256)(128)(2,1)}, u32[]{:S(2)}) copy-start(bf16[128]{0:T(256)(128)(2,1)} %param.17) | copy-start | bytes 772
  413.5 191.9 %copy-start.9 = (pred[2,8]{1,0:T(4,128)(4,1)S(1)}, pred[2,8]{1,0:T(4,128)(4,1)}, u32[]{:S(2)}) copy-start(pred[2,8]{1,0:T(4,128)(4,1)} %copy-done.8) | copy-start | bytes 52
  598.3 7.1 collective-permute-start.3
  607.1 116.8 %copy-start.2 = (bf16[64,8512]{1,0:T(8,128)(2,1)S(1)}, bf16[64,8512]{1,0:T(8,128)(2,1)}, u32[]{:S(2)}) copy-start(bf16[64,8512]{1,0:T(8,128)(2,1)} %param.14) | copy-start | bytes 3268612
  607.1 116.8 %copy-start.7 = (f32[64,4096]{1,0:T(8,128)S(1)}, f32[64,4096]{1,0:T(8,128)}, u32[]{:S(2)}) copy-start(f32[64,4096]{1,0:T(8,128)} %get-tuple-element.67) | copy-start | bytes 3145732
  719.6 6.0 copy-start.10
  722.3 4.7 copy-start.4
  725.6 3.4 copy-start.5

commit v6 on v5

--- a/solution.py
+++ b/solution.py
@@ -19,9 +19,10 @@
 GROUP = 1024
 PIECE_ROWS = 32
 LAG = 2
-R_LAG = 2
 PUMPS = 4
-SLOTS = 4
+B_PLAN = (32, 2, 4, 2)
+I_PLAN = (32, 1, 3, 2)
+B_SLOTS = (18, 32)
 IN_TILE = 512
 Q = 128
 LB = 256
@@ -362,7 +363,8 @@
         dw_gate = made[0]
         dims = len(place_bits())
         every = (slice(None),) * (dims + 1)
-        streams = make_streams(layout, (dw_out, dw_gate), sums, refs[3:])
+        streams = make_streams(B_PLAN, layout, (dw_out, dw_gate), sums, refs[3:])
+        pieces = piece_count(layout, B_PLAN[0])
         tiles = DI // GROUP
         pl.when(number == 0)(greet)
 
@@ -379,8 +381,12 @@
             )
 
         def pump(place):
-            for stream in streams:
-                stream.pump(number * PUMPS + place)
+            slot, drain = number * PUMPS + place, B_PLAN[1] * dims
+
+            @pl.loop(spread_out(slot, pieces, B_SLOTS, drain), spread_out(slot + 1, pieces, B_SLOTS, drain))
+            def _(it):
+                for stream in streams:
+                    stream.pump(it)
 
         pl.when(number < tiles)(lambda: load().start())
 
@@ -744,7 +750,8 @@
 
 
 class Stream:
-    def __init__(self, order, count, start_piece, end_piece, bufs, dtype):
+    def __init__(self, plan, order, count, start_piece, end_piece, bufs, dtype):
+        _, self.lag, self.slots, self.accs = plan
         self.order, self.count = order, count
         self.start_piece, self.end_piece = start_piece, end_piece
         self.dtype = dtype
@@ -753,17 +760,18 @@
         self.own_sem, self.send, self.got, self.credit, self.out_sem = bufs[2 * self.dims + 1 :]
 
     @staticmethod
-    def buffers(dims, rows, cols, dtype):
+    def buffers(plan, dims, rows, cols, dtype):
+        _, _, slots, accs = plan
         shape = lambda n: (2,) * n + (rows, cols)
         return (
             [pltpu.VMEM((2,) + shape(dims - 1), dtype)]
-            + [pltpu.VMEM((SLOTS,) + shape(dims - 1 - k), dtype) for k in range(dims)]
-            + [pltpu.VMEM((2,) + shape(dims - 1 - k), dtype) for k in range(dims - 1)]
+            + [pltpu.VMEM((slots,) + shape(dims - 1 - k), dtype) for k in range(dims)]
+            + [pltpu.VMEM((accs,) + shape(dims - 1 - k), dtype) for k in range(dims - 1)]
             + [pltpu.VMEM((2, rows, cols), F32)]
             + [
                 pltpu.SemaphoreType.DMA((2,)),
                 pltpu.SemaphoreType.DMA((dims, 2)),
-                pltpu.SemaphoreType.DMA((dims, SLOTS)),
+                pltpu.SemaphoreType.DMA((dims, slots)),
                 pltpu.SemaphoreType.REGULAR((dims,)),
                 pltpu.SemaphoreType.DMA((2,)),
             ]
@@ -774,41 +782,41 @@
         return tuple(value if d == self.order[stage] else slice(None) for d in left)
 
     def copy(self, stage, src, piece, into=()):
-        dst = self.recv[stage].at[piece % SLOTS]
+        dst = self.recv[stage].at[piece % self.slots]
         return remote(
             src,
             dst.at[into] if into else dst,
             self.send.at[stage, piece % 2],
-            self.got.at[stage, piece % SLOTS],
+            self.got.at[stage, piece % self.slots],
             self.order[stage],
         )
 
     def sent_part(self, stage, piece):
-        return self.acc[stage - 1].at[(piece % 2,) + self.half(stage, 1 - bit_of(self.order[stage]))]
+        return self.acc[stage - 1].at[(piece % self.accs,) + self.half(stage, 1 - bit_of(self.order[stage]))]
 
     def credit_before(self, stage, piece):
-        @pl.when(piece >= SLOTS)
+        @pl.when(piece >= self.slots)
         def _():
             pl.semaphore_wait(self.credit.at[stage], 1)
 
     def pump(self, it):
         dims = self.dims
         for stage in reversed(range(dims)):
-            piece = it - R_LAG * (stage + 1)
+            piece = it - self.lag * (stage + 1)
 
             @pl.when((piece >= 0) & (piece < self.count))
             def _(stage=stage, piece=piece):
                 slot = piece % 2
                 if stage == 0:
-                    self.copy(0, self.recv[0].at[piece % SLOTS], piece).wait()
+                    self.copy(0, self.recv[0].at[piece % self.slots], piece).wait()
                     pltpu.make_async_copy(self.own.at[slot], self.own.at[slot], self.own_sem.at[slot]).wait()
                     kept = self.own[slot]
                 else:
                     self.copy(stage, self.sent_part(stage, piece), piece).wait()
-                    kept = self.acc[stage - 1][(slot,) + self.half(stage, bit_of(self.order[stage]))]
-                got = self.recv[stage][piece % SLOTS]
+                    kept = self.acc[stage - 1][(piece % self.accs,) + self.half(stage, bit_of(self.order[stage]))]
+                got = self.recv[stage][piece % self.slots]
                 if stage < dims - 1:
-                    self.acc[stage][slot] = kept + got
+                    self.acc[stage][piece % self.accs] = kept + got
                     self.credit_before(stage + 1, piece)
                     self.copy(stage + 1, self.sent_part(stage + 1, piece), piece).start()
                 else:
@@ -818,7 +826,7 @@
                     self.out[slot] = kept.astype(F32) + got.astype(F32)
                     self.end_piece(piece, self.out.at[slot], self.out_sem.at[slot])
 
-                @pl.when(piece < self.count - SLOTS)
+                @pl.when(piece < self.count - self.slots)
                 def _():
                     pl.semaphore_signal(
                         self.credit.at[stage], inc=1, device_id=partner(self.order[stage]),
@@ -840,23 +848,23 @@
             pltpu.make_async_copy(self.out.at[slot], self.out.at[slot], self.out_sem.at[slot]).wait()
 
 
-def piece_plan(arrays, lane):
-    dims = len(place_bits())
+def piece_plan(plan, arrays, lane):
+    dims, piece_rows = len(place_bits()), plan[0]
     width, offset = LANES[lane], sum(LANES[:lane])
     spans, first = [], 0
     for ref, out, rows, cols in arrays:
-        subs = rows // PIECE_ROWS
+        subs = rows // piece_rows
         whole = cols // GROUP * subs
         spans.append((ref, out, first, whole, lambda n, subs=subs: [
-            (0, width, n % subs * PIECE_ROWS, pl.multiple_of(n // subs * GROUP + offset, 128))
+            (0, width, n % subs * piece_rows, pl.multiple_of(n // subs * GROUP + offset, 128))
         ]))
         first += whole
         if cols % GROUP:
             base = cols // GROUP * GROUP
             if lane < 2:
-                parts = [(0, width, lane * PIECE_ROWS, base)]
+                parts = [(0, width, lane * piece_rows, base)]
             else:
-                parts = [(k * 128, 128, k * PIECE_ROWS, base + LANES[0]) for k in range(2)]
+                parts = [(k * 128, 128, k * piece_rows, base + LANES[0]) for k in range(2)]
             spans.append((ref, out, first, 1, lambda n, parts=parts: parts))
             first += 1
 
@@ -866,7 +874,7 @@
             def _(ref=ref, out=out, start=start, parts=parts):
                 for col, size, row, at in parts(piece - start):
                     held = (pl.ds(col, size),)
-                    act(ref, out, held, (pl.ds(pl.multiple_of(row, PIECE_ROWS), PIECE_ROWS), pl.ds(at, size)))
+                    act(ref, out, held, (pl.ds(pl.multiple_of(row, piece_rows), piece_rows), pl.ds(at, size)))
 
     def start(piece, own, own_sem, send, dim):
         def act(ref, out, held, at):
@@ -883,18 +891,23 @@
     return first, start, end
 
 
-def make_streams(layout, ins, outs, bufs):
+def make_streams(plan, layout, ins, outs, bufs):
     size = 2 * len(place_bits()) + 6
     arrays = [(ins[j], outs[j]) + shape for j, shape in enumerate(layout)]
     streams = []
     for lane, order in enumerate(halving_orders()):
-        count, start, end = piece_plan(arrays, lane)
-        streams.append(Stream(order, count, start, end, bufs[lane * size : (lane + 1) * size], BF))
+        count, start, end = piece_plan(plan, arrays, lane)
+        streams.append(Stream(plan, order, count, start, end, bufs[lane * size : (lane + 1) * size], BF))
     return streams
 
 
-def piece_count(layout):
-    return sum(rows // PIECE_ROWS * cols // GROUP for rows, cols in layout)
+def piece_count(layout, piece_rows=PIECE_ROWS):
+    return sum(rows // piece_rows * cols // GROUP for rows, cols in layout)
+
+
+def spread_out(slot, pieces, slots, drain):
+    first, last = slots
+    return jnp.where(slot <= first, slot * pieces // first, pieces + (slot - first) * drain // (last - first))
 
 
 def reduce_views(arrays):
@@ -908,8 +921,8 @@
     return views, layout, outs
 
 
-def reduce_buffers():
-    return sum((Stream.buffers(len(place_bits()), PIECE_ROWS, width, BF) for width in LANES), [])
+def reduce_buffers(plan):
+    return sum((Stream.buffers(plan, len(place_bits()), plan[0], width, BF) for width in LANES), [])
 
 
 class Gather:
@@ -972,7 +985,7 @@
     k = pl.program_id(0)
     dims = len(place_bits())
     every = (slice(None),) * (dims + 1)
-    streams = make_streams(layout, (dw,), (conv_sum,), bufs)
+    streams = make_streams(I_PLAN, layout, (dw,), (conv_sum,), bufs)
     n_conv, n_gate = CD // IN_TILE, DI // IN_TILE
 
     def start_small(piece, own, own_sem, send, dim):
@@ -983,7 +996,7 @@
     def end_small(piece, src, sem):
         pltpu.make_async_copy(src, small_sum, sem).start()
 
-    streams.append(Stream(halving_orders()[0], 1, start_small, end_small, bufs[len(LANES) * (2 * dims + 6) :], F32))
+    streams.append(Stream(I_PLAN, halving_orders()[0], 1, start_small, end_small, bufs[len(LANES) * (2 * dims + 6) :], F32))
 
     @pl.when(k == 0)
     def _():
@@ -1051,7 +1064,7 @@
     layout = [(in_rows, CD)]
     n_gate, n_conv = DI // IN_TILE, CD // IN_TILE
     steps = 2 * n_conv
-    pumps = piece_count(layout) + R_LAG * dims
+    pumps = piece_count(layout) + I_PLAN[1] * dims
     span = 3 * n_conv - 3
     pump_at = lambda slot: slot * pumps // span
     assert pumps <= span and n_conv == n_gate + 1
@@ -1086,8 +1099,8 @@
             pltpu.VMEM((2,) + lead + (in_rows, IN_TILE), BF),
             pltpu.SemaphoreType.DMA((2,)),
         ]
-        + reduce_buffers()
-        + Stream.buffers(dims, *small.shape[dims:], F32),
+        + reduce_buffers(I_PLAN)
+        + Stream.buffers(I_PLAN, dims, *small.shape[dims:], F32),
         compiler_params=pltpu.CompilerParams(
             dimension_semantics=("arbitrary",), collective_id=1, has_side_effects=True, vmem_limit_bytes=VMEM_LIMIT
         ),
@@ -1348,8 +1361,8 @@
             pltpu.VMEM((total, GROUP), BF),
             pltpu.VMEM(lead + (in_rows, GROUP), BF),
             pltpu.SemaphoreType.DMA((1 + GROUP // LB,)),
-        ] + reduce_buffers()
-        assert piece_count(layout) + R_LAG * len(lead) <= PUMPS * seqs * chunks
+        ] + reduce_buffers(B_PLAN)
+        assert B_SLOTS[1] == PUMPS * seqs * chunks
     dproj, front_grad, conv_sums, head_sums, *early = pl.pallas_call(
         partial(backward_kernel, layout),
         grid=grid,

time: 736 us -> 731 us (level)
  no operation moved by 1% of the time
where the time goes in v6:
time: 731 us; the launch traced here: 726 us
  Pallas kernels  581 us (79%)
  matrix products  93.7 us (13%)
  local copies, waits for them, and re-layouts  24.2 us (3%)
  other arithmetic  16.7 us (2%)
    pallas_call x1, Pallas kernels, shards(): pl.pallas_call(partial(backward_kernel, layout), grid=grid, in_specs=[pl....  179 us
    pallas_call x1, Pallas kernels, shards(): pl.pallas_call(partial(forward_kernel, shapes, chunks, before), grid=(bef...  156 us
    pallas_call x1, Pallas kernels, input_grad_and_reduce(): pl.pallas_call(partial(input_kernel, layout, pump_at), grid=(steps,), in_...  111 us
    pallas_call x1, Pallas kernels, gather_first(): pl.pallas_call(partial(first_kernel, groups), in_specs=[whole, any_space,...  93.7 us
    pallas_call x1, Pallas kernels, shards(): pl.pallas_call(gate_kernel, grid=grid, in_specs=[pl.BlockSpec((Q, DI), at...  41.3 us
    dot_general x1, matrix products, shards(): jnp.dot(mixed, w_out, preferred_element_type=F32)  24.1 us
    dot_general x1, matrix products, shards(): lax.dot_general(cotangent, w_out, (((1,), (1,)), ((), ())), preferred_ele...  23.9 us
    dot_general x1, matrix products, dot_tn(): lax.dot_general(a, b, (((0,), (0,)), ((), ())), preferred_element_type=F32)  23.8 us
  transfers between devices with their start and end apart: 4, of which 1 were waited for; matrix products, arithmetic and copies ran while one was open for 14% of the time, Pallas kernels for 0%

profile of v6, /device:TPU:0, one launch (start us, length us, event | category | flops | bytes accessed | tf_op | source)
XLA Modules:
  0.0 725.8 jit_solution(11470621751840419594)
XLA Ops:
  0.7 0.7 reshape.359
  1.4 0.6 reduce-window.6
  2.0 0.2 slice_reduce_fusion.3
  2.2 0.2 reduce-window.9
  2.4 0.2 slice_reduce_fusion.1
  2.7 0.2 slice_reduce_fusion.2
  3.0 0.1 fusion.14
  3.1 1.9 slice.124.refs_8_
  5.0 1.1 slice.121
  6.1 0.8 reshape.362
  6.8 0.1 copy.44
  6.9 0.1 slice_compare_fusion
  7.0 1.6 select_bitcast_fusion.tail_ref
  8.5 0.9 pad.37.own_a
  9.4 1.4 fusion.18.own_b
  10.8 93.7 %gather_first.1 = (bf16[1040,2048]{1,0:T(8,128)(2,1)}, bf16[2048,1024]{1,0:T(8,128)(2,1)}, bf16[2,2,2,2,2,64,4608]{6,5,4,3,2,1,0:T(8,128)(2,1)}, bf16[2,2,2,2,2,16,128]{6,5,4,3,2,1,0:T(8,128)(2,1)}) custom-call(bf16[1024,2048]{1,0:T(8,128)(2,1)} %bitcast.81, bf16[16,2048]{1,0:T(8,128)(2,1)} %select_bitcast_fusion.tail_ref, bf16[64,4608]{1,0:T(8,128)(2,1)} %pad.37.own_a, ...), custom_call_target="tpu_custom_call" | custom-call | tf_op jit(solution)/shard_map/gather_first/pallas_call | solution.py:721
  104.5 0.9 copy.56
  105.5 0.1 slice.148
  105.6 0.1 slice.147
  105.9 0.2 copy.38
  106.1 0.1 reshape.366
  106.2 0.1 reshape.364
  106.4 0.1 reshape.365
  106.6 0.8 pad.36.refs_0_.refs_2_
  107.4 1.2 compare_convert_fusion.refs_4_.spread_ref.refs_6_
  108.7 0.6 select_maximum_fusion.refs_3_.hp_ref.refs_5_
  109.3 0.7 maximum_convert_fusion.refs_2_.refs_4_
  110.0 0.6 broadcast_in_dim.40.refs_1_.refs_3_
  110.6 155.6 %scan_forward.1 = (f32[1024,4096]{1,0:T(8,128)}, bf16[1024,4352]{1,0:T(8,128)(2,1)}, bf16[1024,4352]{1,0:T(8,128)(2,1)}, bf16[1024,4096]{1,0:T(8,128)(2,1)}, f32...) custom-call(f32[1024,128]{1,0:T(8,128)} %pad.36.refs_0_.refs_2_, ...), custom_call_target="tpu_custom_call" | custom-call | tf_op jit(solution)/shard_map/scan_forward/pallas_call | solution.py:1275
  266.3 2.6 collective-permute-start
  268.9 0.7 slice_convert_fusion.1
  269.5 0.7 reshape.388.refs_7_
  270.2 23.9 %convolution_bitcast_fusion.mg_ref = f32[1024,4096]{1,0:T(8,128)} fusion(bf16[4096,2048]{1,0:T(8,128)(2,1)} %bitcast.122, bf16[1024,2048]{1,0:T(8,128)(2,1)} %bitcast.89), kind=kOutput, calls=%fused_computation.1 | convolution fusion | flops 17179869184 | bytes 37748736 | tf_op jit(solution)/shard_map/dot_general | solution.py:1292
  294.1 21.8 %fusion.gate_ref = f32[1024,4096]{1,0:T(8,128)} fusion(bf16[2048,4096]{1,0:T(8,128)(2,1)S(1)} %bitcast.85, bf16[1040,2048]{1,0:T(8,128)(2,1)} %get-tuple-element.42.refs_5_), kind=kOutput, calls=%fused_computation.3 | convolution fusion | flops 17179869184 | bytes 37748736 | tf_op jit(solution)/shard_map/dot_general | solution.py:1291
  315.9 1.3 copy-done.1
  317.2 41.3 %gate_both.1 = (bf16[1024,4096]{1,0:T(8,128)(2,1)}, bf16[1024,4096]{1,0:T(8,128)(2,1)}, bf16[1024,4096]{1,0:T(8,128)(2,1)}, f32[1024,64]{1,0:T(8,128)}, bf16[256,4096]{1,0:T(8,128)(2,1)}, /*index=5*/f32[8,4096]{1,0:T(8,128)}) custom-call(f32[1024,4096]{1,0:T(8,128)} %get-tuple-element.44.y_ref, bf16[1024,4352]{1,0:T(8,128)(2,1)} %get-tuple-element.45.act_ref.refs_14_, ...), custom_call_target="tpu_custom_call" | custom-call | tf_op jit(solution)/shard_map/gate_both/pallas_call | solution.py:1296
  358.6 1.7 fusion.19
  360.3 1.3 collective-permute-start.1
  361.6 24.1 %add_convert_fusion = bf16[1024,2048]{1,0:T(8,128)(2,1)} fusion(bf16[1024,2048]{1,0:T(8,128)(2,1)} %bitcast.82, bf16[1024,4096]{1,0:T(8,128)(2,1)} %get-tuple-element.50, bf16[4096,2048]{1,0:T(8,128)(2,1)} %bitcast.123), kind=kOutput, calls=%fused_computation.2 | convolution fusion | flops 17186160640 | bytes 33554432 | tf_op jit(solution)/shard_map/dot_general | solution.py:1346
  385.7 1.3 collective-permute-start.2
  387.0 23.8 %convolution_convert_fusion = bf16[4096,2048]{1,0:T(8,128)(2,1)} fusion(bf16[1024,4096]{1,0:T(8,128)(2,1)} %get-tuple-element.50, bf16[1024,2048]{1,0:T(8,128)(2,1)S(1)} %bitcast.91), kind=kOutput, calls=%fused_computation | convolution fusion | flops 17188257792 | bytes 29360128 | tf_op jit(solution)/shard_map/dot_general | solution.py:47
  410.9 0.9 slice_reduce_fusion
  411.9 0.1 reduce_sum.27
  412.0 1.5 pad_maximum_fusion.1.refs_10_
  413.5 178.7 %scan_backward.1 = (bf16[1024,4608]{1,0:T(8,128)(2,1)}, f32[16,4352]{1,0:T(8,128)}, f32[8,4352]{1,0:T(8,128)}, f32[8,64]{1,0:T(8,128)}, bf16[2,2,2,2,2,64,4096]{...) custom-call(f32[1040,4608]{1,0:T(8,128)} %get-tuple-element.53.refs_0_.refs_1_, ...), custom_call_target="tpu_custom_call" | custom-call | tf_op jit(solution)/shard_map/scan_backward/pallas_call | solution.py:1366
  592.2 1.4 multiply_reduce_fusion.1
  593.6 0.7 slice_bitcast_fusion.1
  594.3 1.0 convert_element_type.197
  595.3 1.3 collective-permute-start.3
  596.6 1.1 reshape.375
  597.7 0.1 copy.55
  597.8 0.1 reshape.376
  598.1 0.7 copy.50
  598.8 0.5 convert_divide_fusion
  599.3 3.0 collective-permute-done.3
  602.3 1.7 fusion.4
  604.0 111.3 %input_grad.1 = (bf16[1024,2048]{1,0:T(8,128)(2,1)}, bf16[2,2,2,2,2,64,4608]{6,5,4,3,2,1,0:T(8,128)(2,1)}, f32[64,4608]{1,0:T(8,128)}, f32[8,128]{1,0:T(8,128)}) custom-call(bf16[2048,1024]{1,0:T(8,128)(2,1)} %get-tuple-element.51.refs_16_.refs_0_, bf16[1024,4096]{1,0:T(8,128)(2,1)} %get-tuple-element.52.refs_17_.refs_1_, bf16[2048,4096]{1,0:T(8,128)(2,1)} %bitcast.84, ...), custom_call_target="tpu_custom_call" | custom-call | tf_op jit(solution)/shard_map/input_grad/pallas_call | solution.py:1076
  715.3 1.3 slice.138
  716.6 1.4 slice.137
  718.0 1.5 slice.135
  719.5 1.8 multiply_reduce_fusion
  721.3 1.4 fusion.20
  722.6 2.0 copy.62
  724.7 1.0 copy.63
  (53 shorter events, 0.7 us)
Async XLA Ops:
  3.1 102.6 %copy-start.14 = (f32[64]{0:T(128)S(1)}, f32[64]{0:T(128)}, u32[]{:S(2)}) copy-start(f32[64]{0:T(128)} %param.21) | copy-start | bytes 772
  7.0 98.5 %copy-start.8 = (pred[2,8]{1,0:T(4,128)(4,1)}, pred[2,8]{1,0:T(4,128)(4,1)S(1)}, u32[]{:S(2)}) copy-start(pred[2,8]{1,0:T(4,128)(4,1)S(1)} %slice_compare_fusion) | copy-start | bytes 52
  9.4 99.2 %copy-start.11 = (f32[64]{0:T(128)S(1)}, f32[64]{0:T(128)}, u32[]{:S(2)}) copy-start(f32[64]{0:T(128)} %param.22) | copy-start | bytes 772
  9.4 99.2 %copy-start.12 = (f32[64]{0:T(128)S(1)}, f32[64]{0:T(128)}, u32[]{:S(2)}) copy-start(f32[64]{0:T(128)} %param.20) | copy-start | bytes 772
  266.3 49.6 %collective-permute-start = (bf16[256,4096]{1,0:T(8,128)(2,1)}, bf16[256,4096]{1,0:T(8,128)(2,1)S(1)}, u32[]{:S(2)}, u32[]{:S(2)}) collective-permute-start(bf16[256,4096]{1,0:T(8,128)(2,1)} %get-tuple-element.47), channel_id=1, source_target_pairs={{0,1},{2,3},{4,5},{6,7},{8,9},{10,11},{12,13},{14,15},{16,17},{18,... | collective-permute-start | bytes 6291464 | tf_op jit(solution)/shard_map/ppermute | solution.py:549
  270.2 23.9 %copy-start = (bf16[2,2,2,2,2,64,4096]{6,5,4,3,2,1,0:T(8,128)(2,1)S(1)}, bf16[2,2,2,2,2,64,4096]{6,5,4,3,2,1,0:T(8,128)(2,1)}, u32[]{:S(2)}) copy-start(bf16[2,2,2,2,2,64,4096]{6,5,4,3,2,1,0:T(8,128)(2,1)} %get-tuple-element.48) | copy-start | bytes 50331652
  315.9 1.3 copy-start.1
  360.3 25.5 %collective-permute-start.1 = (bf16[128,4096]{1,0:T(8,128)(2,1)S(1)}, bf16[128,4096]{1,0:T(8,128)(2,1)S(1)}, u32[]{:S(2)}, u32[]{:S(2)}) collective-permute-start(bf16[128,4096]{1,0:T(8,128)(2,1)S(1)} %get-tuple-element.75), channel_id=1, source_target_pairs={{1,0},{3,2},{5,4},{7,6},{9,8},{11,10},{13,12},{15,14},{17,16},{19,... | collective-permute-start | bytes 3145736 | tf_op jit(solution)/shard_map/ppermute | solution.py:549
  361.6 25.4 %copy-start.3 = (bf16[2,512,2048]{2,1,0:T(8,128)(2,1)S(1)}, bf16[2,512,2048]{2,1,0:T(8,128)(2,1)}, u32[]{:S(2)}) copy-start(bf16[2,512,2048]{2,1,0:T(8,128)(2,1)} %param.23) | copy-start | bytes 12582916
  385.7 26.3 %collective-permute-start.2 = (bf16[128,4096]{1,0:T(8,128)(2,1)S(1)}, bf16[128,4096]{1,0:T(8,128)(2,1)S(1)}, u32[]{:S(2)}, u32[]{:S(2)}) collective-permute-start(bf16[128,4096]{1,0:T(8,128)(2,1)S(1)} %get-tuple-element.58), channel_id=1, source_target_pairs={{1,0},{3,2},{5,4},{7,6},{9,8},{11,10},{13,12},{15,14},{17,16},{19,... | collective-permute-start | bytes 3145736 | tf_op jit(solution)/shard_map/ppermute | solution.py:549
  413.5 178.7 %copy-start.6 = (bf16[128,2048]{1,0:T(8,128)(2,1)S(1)}, bf16[128,2048]{1,0:T(8,128)(2,1)}, u32[]{:S(2)}) copy-start(bf16[128,2048]{1,0:T(8,128)(2,1)} %refs_7_.1) | copy-start | bytes 1572868
  413.5 185.3 %copy-start.13 = (bf16[128]{0:T(256)(128)(2,1)S(1)}, bf16[128]{0:T(256)(128)(2,1)}, u32[]{:S(2)}) copy-start(bf16[128]{0:T(256)(128)(2,1)} %param.17) | copy-start | bytes 772
  413.5 188.8 %copy-start.9 = (pred[2,8]{1,0:T(4,128)(4,1)S(1)}, pred[2,8]{1,0:T(4,128)(4,1)}, u32[]{:S(2)}) copy-start(pred[2,8]{1,0:T(4,128)(4,1)} %copy-done.8) | copy-start | bytes 52
  595.3 6.9 collective-permute-start.3
  603.9 115.5 %copy-start.2 = (bf16[64,8512]{1,0:T(8,128)(2,1)S(1)}, bf16[64,8512]{1,0:T(8,128)(2,1)}, u32[]{:S(2)}) copy-start(bf16[64,8512]{1,0:T(8,128)(2,1)} %param.14) | copy-start | bytes 3268612
  604.0 115.5 %copy-start.7 = (f32[64,4096]{1,0:T(8,128)S(1)}, f32[64,4096]{1,0:T(8,128)}, u32[]{:S(2)}) copy-start(f32[64,4096]{1,0:T(8,128)} %get-tuple-element.67) | copy-start | bytes 3145732
  715.3 6.0 copy-start.10
  718.0 4.7 copy-start.4
  721.2 3.4 copy-start.5
